TPU v7x, 512 devices: a whole 4x4x16 slice. The times are simulated.
512 devices in a mesh: batch: 16 (over z), hist: 32 (over y, x, core).
Axes of the slice: x: 4, y: 4, z: 16, core: 2. Of those that a mesh axis runs over, the one named last changes fastest.
Arguments:
- feats: bfloat16 [512, 128, 768], P(('batch', 'hist')), may hold values from -6 to 6
- history: bfloat16 [8192, 1536], P('hist'), may hold values from -6 to 6
- weight: bfloat16 [768, 768], replicated, may hold values from -0.21875 to 0.21875
- edge_coef: bfloat16 [512, 128, 256], P(('batch', 'hist')), may hold values from -0.375 to 0.375
- tile_map: int32 [512, 2], P(('batch', 'hist')), may hold values from 0 to 1, each once within a row
- nbr_owner: int32 [512, 256, 1], P(('batch', 'hist')), may hold values from 0 to 31; in each aligned block of 256 rows (0 to 255, 256 to 511, ..., all dimensions but the last counted through in order) at most 16 rows name the same one
- nbr_row: int32 [512, 256], P(('batch', 'hist')), may hold values from 0 to 383
- grad_out: bfloat16 [512, 128, 768], P(('batch', 'hist')), may hold values from -6 to 6
Outputs:
- out: bfloat16 [512, 128, 768], P(('batch', 'hist'))
- grad_feats: bfloat16 [512, 128, 768], P(('batch', 'hist'))
- grad_weight: float32 [768, 768], P('hist')
Inputs may be any that keep to these rules, and one draw needn't show every extreme that they name: `nbr_owner`: in each group's 256 slots no hist index is named by more than 16 slots; some index is named exactly 16 times. `tile_map`: each group's row is a permutation of 0 to 1.
All inputs are finite; a program needn't handle non-finite values.
Results may differ from a plain program's by a relative error of at most 0.0055.
Values may be sent and summed in bfloat16 or wider, within the bound.
No kernel may reach another device: no remote copies, remote signals or barrier semaphores. Data moves between devices by JAX's collectives and lax.ppermute only.
A program may use at most 64 MiB of HBM per device.

v0:
```python
import jax
import jax.numpy as jnp
from jax import lax
from jax.sharding import PartitionSpec as P


def body(feats, history, weight, edge_coef, tile_map, nbr_owner, nbr_row, grad_out):
    feat_width = weight.shape[0]
    node_rows = feats.shape[1]
    table_rows = history.shape[0]
    peer_count = lax.axis_size("hist")
    owners = nbr_owner[0, :, 0]
    slot_rows = nbr_row[0]
    slot_count = slot_rows.shape[0]
    block_count = tile_map.shape[1]
    tile_rows = slot_count // block_count
    dst_blocks = node_rows // tile_rows
    capacity = 2 * slot_count // peer_count
    onehot = (owners[:, None] == jnp.arange(peer_count, dtype=jnp.int32)[None, :]).astype(jnp.int32)
    position = jnp.sum((jnp.cumsum(onehot, axis=0) - 1) * onehot, axis=1)
    request = jnp.zeros((peer_count, capacity), jnp.int32).at[owners, position].set(slot_rows)
    local_feats = feats[0]
    zero_rows = jnp.zeros((node_rows, feat_width), jnp.bfloat16)
    table = jnp.concatenate([jnp.concatenate([local_feats, zero_rows], axis=1), history], axis=0)
    received = lax.all_to_all(request, "hist", split_axis=0, concat_axis=0, tiled=True)
    taken = jnp.take(table, received, axis=0)
    answered = lax.all_to_all(taken, "hist", split_axis=0, concat_axis=0, tiled=True)
    pulled = answered[owners, position]
    pulled_emb = pulled[:, :feat_width]
    inside = slot_rows < node_rows
    tile_order = tile_map[0]
    edge_tiles = edge_coef[0].reshape(dst_blocks, tile_rows, -1)

    def arrange(values):
        blocks = values.reshape(block_count, tile_rows, feat_width)[tile_order]
        return blocks.reshape(dst_blocks, -1, feat_width)

    aggregate = jnp.einsum(
        "cik,ckd->cid", edge_tiles, arrange(pulled_emb), preferred_element_type=jnp.float32
    ).reshape(node_rows, feat_width)
    mixed_rows = (local_feats.astype(jnp.float32) + aggregate).astype(jnp.bfloat16)
    pre_act = jnp.dot(mixed_rows, weight, preferred_element_type=jnp.float32)
    sigmoid_pre = jax.nn.sigmoid(pre_act)
    out_rows = (pre_act * sigmoid_pre).astype(jnp.bfloat16)
    grad_pre = (
        grad_out[0].astype(jnp.float32) * sigmoid_pre * (1.0 + pre_act * (1.0 - sigmoid_pre))
    ).astype(jnp.bfloat16)
    pulled_aux = pulled[:, feat_width:]
    grad_mixed = jnp.dot(grad_pre, weight.T, preferred_element_type=jnp.float32).astype(
        jnp.bfloat16
    )
    slot_tiles = jnp.einsum(
        "cik,cid->ckd",
        edge_tiles,
        grad_mixed.reshape(dst_blocks, tile_rows, feat_width),
        preferred_element_type=jnp.float32,
    )
    slot_tiles = slot_tiles.reshape(block_count, tile_rows, feat_width)
    slot_grad = (
        jnp.zeros((block_count, tile_rows, feat_width), jnp.float32).at[tile_order].set(slot_tiles)
    )
    slot_grad = slot_grad.reshape(slot_count, feat_width).astype(jnp.bfloat16)
    slot_grad = jnp.where(inside[:, None], slot_grad, jnp.zeros_like(slot_grad))
    outgoing = (
        jnp.zeros((peer_count, capacity, feat_width), jnp.bfloat16)
        .at[owners, position]
        .set(slot_grad)
    )
    incoming = lax.all_to_all(outgoing, "hist", split_axis=0, concat_axis=0, tiled=True)
    returned = (
        jnp.zeros((node_rows + table_rows, feat_width), jnp.float32)
        .at[received]
        .add(incoming.astype(jnp.float32))[:node_rows]
    )
    compensation = jnp.einsum(
        "cik,ckd->cid", edge_tiles, arrange(pulled_aux), preferred_element_type=jnp.float32
    ).reshape(node_rows, feat_width)
    grad_rows = (grad_mixed.astype(jnp.float32) + returned + compensation).astype(jnp.bfloat16)
    share_rows = feat_width // peer_count
    local_term = lax.dot_general(
        mixed_rows, grad_pre, (((0,), (0,)), ((), ())), preferred_element_type=jnp.float32
    )
    full_sum = lax.psum(local_term, ("batch", "hist"))
    weight_share = lax.dynamic_slice_in_dim(
        full_sum, lax.axis_index("hist") * share_rows, share_rows, 0
    )
    return (out_rows[None], grad_rows[None], weight_share)


def solution(mesh):
    return jax.shard_map(
        body,
        mesh=mesh,
        in_specs=(
            P(("batch", "hist"), None, None),
            P("hist", None),
            P(),
            P(("batch", "hist"), None, None),
            P(("batch", "hist"), None),
            P(("batch", "hist"), None, None),
            P(("batch", "hist"), None),
            P(("batch", "hist"), None, None),
        ),
        out_specs=(
            P(("batch", "hist"), None, None),
            P(("batch", "hist"), None, None),
            P("hist", None),
        ),
        check_vma=False,
    )
```

profile of v0, /device:TPU:6, one launch (start us, length us, event | category | flops | bytes accessed | tf_op | source)
XLA Modules:
  0.0 578.8 jit_solution(12510178827901942333)
XLA Ops:
  7.2 0.8 fusion.18
  8.8 0.8 fusion.17
  9.6 0.7 or_select_fusion
  10.3 21.7 %scatter_fusion = s32[32,16]{0,1:T(8,128)S(1)} fusion(s32[32,16]{0,1:T(8,128)S(1)} %broadcast.116, s32[256]{0:T(256)S(1)} %bitcast.96, s32[256]{0:T(256)} %bitcast.112), kind=kCustom, calls=%fused_computation.4 | custom fusion | bytes 5120 | tf_op jit(solution)/shard_map/scatter | solution.py:21
  32.0 0.7 copy.29
  32.7 9.4 %all-to-all-start = ((s32[32,1,16]{2,1,0:T(1,128)}), s32[32,1,16]{2,1,0:T(1,128)S(1)}, u32[]{:S(2)}, u32[]{:S(2)}) async-start(s32[32,1,16]{2,1,0:T(1,128)} %copy.29), calls=%async_computation | async-start | bytes 32768 | tf_op jit(solution)/shard_map/all_to_all | solution.py:25
  42.2 5.4 all-to-all-done
  47.9 3.0 gather_fusion
  50.8 2.8 broadcast_select_fusion
  53.6 6.5 %all-to-all-start.1 = ((bf16[32,16,1536]{2,1,0:T(8,128)(2,1)}), bf16[32,16,1536]{2,1,0:T(8,128)(2,1)}, u32[]{:S(2)}, u32[]{:S(2)}) async-start(bf16[32,16,1536]{2,1,0:T(8,128)(2,1)} %broadcast_select_fusion), calls=%async_computation.1 | async-start | bytes 3145728 | tf_op jit(solution)/shard_map/all_to_all | solution.py:27
  60.5 19.6 %all-to-all-done.1 = bf16[32,16,1536]{2,1,0:T(8,128)(2,1)} async-done(((bf16[32,16,1536]{2,1,0:T(8,128)(2,1)}), bf16[32,16,1536]{2,1,0:T(8,128)(2,1)}, u32[]{:S(2)}, u32[]{:S(2)}) %all-to-all-start.1) | async-done | bytes 1572896 | tf_op jit(solution)/shard_map/all_to_all | solution.py:27
  80.2 3.8 gather_fusion.1
  83.9 0.8 fusion.25
  86.6 1.9 fusion.21
  89.2 0.8 scatter_fusion.1
  90.1 0.9 broadcast_in_dim.53
  91.0 34.2 %scatter_fusion.2 = bf16[32,16,768]{2,1,0:T(8,128)(2,1)} fusion(bf16[32,16,768]{2,1,0:T(8,128)(2,1)} %broadcast_in_dim.53, s32[256]{0:T(256)S(1)} %bitcast.97, bf16[256,768]{1,0:T(8,128)(2,1)S(1)} %bitcast_select_fusion), kind=kCustom, calls=%fused_computation.6 | custom fusion | bytes 1181696 | tf_op jit(solution)/shard_map/scatter | solution.py:67
  125.2 8.1 %all-to-all-start.2 = ((bf16[32,16,768]{2,1,0:T(8,128)(2,1)}), bf16[32,16,768]{2,1,0:T(8,128)(2,1)S(1)}, u32[]{:S(2)}, u32[]{:S(2)}) async-start(bf16[32,16,768]{2,1,0:T(8,128)(2,1)} %scatter_fusion.2), calls=%async_computation.2 | async-start | bytes 1572864 | tf_op jit(solution)/shard_map/all_to_all | solution.py:69
  134.0 0.8 fusion.13
  134.8 10.9 %all-to-all-done.2 = bf16[32,16,768]{2,1,0:T(8,128)(2,1)S(1)} async-done(((bf16[32,16,768]{2,1,0:T(8,128)(2,1)}), bf16[32,16,768]{2,1,0:T(8,128)(2,1)S(1)}, u32[]{:S(2)}, u32[]{:S(2)}) %all-to-all-start.2) | async-done | bytes 786464 | tf_op jit(solution)/shard_map/all_to_all | solution.py:69
  145.6 4.2 scatter_custom_fusion.3
  149.9 1.9 fusion.8
  151.8 418.7 %all-reduce.3.cloned.1.call-done = f32[768,768]{1,0:T(8,128)} async-done(((f32[768,768]{1,0:T(8,128)}), f32[768,768]{1,0:T(8,128)}) %all-reduce.3.cloned.1.call-update) | async-done | bytes 2359312 | tf_op jit(solution)/shard_map/psum | solution.py:83
  570.4 1.5 constant_dynamic-slice_fusion
  (46 shorter events, 4.6 us)
Async XLA Ops:
  7.2 78.5 %copy-start = (bf16[768,768]{1,0:T(8,128)(2,1)S(1)}, bf16[768,768]{1,0:T(8,128)(2,1)}, u32[]{:S(2)}) copy-start(bf16[768,768]{1,0:T(8,128)(2,1)} %param.10) | copy-start | bytes 3538948
  7.2 34.9 %copy-start.3 = (bf16[1,128,768]{2,1,0:T(8,128)(2,1)S(1)}, bf16[1,128,768]{2,1,0:T(8,128)(2,1)}, u32[]{:S(2)}) copy-start(bf16[1,128,768]{2,1,0:T(8,128)(2,1)} %param.8) | copy-start | bytes 589828
  7.2 34.9 %copy-start.4 = (bf16[256,1536]{1,0:T(8,128)(2,1)S(1)}, bf16[256,1536]{1,0:T(8,128)(2,1)}, u32[]{:S(2)}) copy-start(bf16[256,1536]{1,0:T(8,128)(2,1)} %param.9) | copy-start | bytes 2359300
  32.7 14.9 %all-to-all-start = ((s32[32,1,16]{2,1,0:T(1,128)}), s32[32,1,16]{2,1,0:T(1,128)S(1)}, u32[]{:S(2)}, u32[]{:S(2)}) async-start(s32[32,1,16]{2,1,0:T(1,128)} %copy.29), calls=%async_computation | async-start | bytes 32768 | tf_op jit(solution)/shard_map/all_to_all | solution.py:25
  53.6 6.8 %copy-start.5 = (bf16[1,128,256]{2,1,0:T(8,128)(2,1)S(1)}, bf16[1,128,256]{2,1,0:T(8,128)(2,1)}, u32[]{:S(2)}) copy-start(bf16[1,128,256]{2,1,0:T(8,128)(2,1)} %param.11) | copy-start | bytes 196612
  53.6 6.9 %copy-start.8 = (s32[1,2]{1,0:T(1,128)S(1)}, s32[1,2]{1,0:T(1,128)}, u32[]{:S(2)}) copy-start(s32[1,2]{1,0:T(1,128)} %param.12) | copy-start | bytes 28
  53.6 6.9 %copy-start.7 = (s32[1,256]{1,0:T(1,128)S(1)}, s32[1,256]{1,0:T(1,128)}, u32[]{:S(2)}) copy-start(s32[1,256]{1,0:T(1,128)} %param.14) | copy-start | bytes 3076
  53.6 26.6 %all-to-all-start.1 = ((bf16[32,16,1536]{2,1,0:T(8,128)(2,1)}), bf16[32,16,1536]{2,1,0:T(8,128)(2,1)}, u32[]{:S(2)}, u32[]{:S(2)}) async-start(bf16[32,16,1536]{2,1,0:T(8,128)(2,1)} %broadcast_select_fusion), calls=%async_computation.1 | async-start | bytes 3145728 | tf_op jit(solution)/shard_map/all_to_all | solution.py:27
  60.1 510.3 %all-reduce.3.cloned.1.call-start = ((), (), s32[]{:S(2)}) async-start(), calls=%async_computation.3 | async-start | bytes 4718592 | tf_op jit(solution)/shard_map/psum | solution.py:83
  84.7 1.3 copy-start.6
  86.6 1.9 copy-start.2
  125.2 8.1 %copy-start.1 = (bf16[256,768]{1,0:T(8,128)(2,1)S(1)}, bf16[256,768]{1,0:T(8,128)(2,1)}, u32[]{:S(2)}) copy-start(bf16[256,768]{1,0:T(8,128)(2,1)} %get-tuple-element.5) | copy-start | bytes 1179652
  125.2 20.4 %all-to-all-start.2 = ((bf16[32,16,768]{2,1,0:T(8,128)(2,1)}), bf16[32,16,768]{2,1,0:T(8,128)(2,1)S(1)}, u32[]{:S(2)}, u32[]{:S(2)}) async-start(bf16[32,16,768]{2,1,0:T(8,128)(2,1)} %scatter_fusion.2), calls=%async_computation.2 | async-start | bytes 1572864 | tf_op jit(solution)/shard_map/all_to_all | solution.py:69
Sparse Core Ops, SparseCore 0:
  88.6 481.7 all-reduce.2
where the time goes:
time: 581 us; the launch traced here: 579 us
  waiting for transfers between devices  455 us (78%)
  local copies, waits for them, and re-layouts  69.6 us (12%)
  starting transfers between devices  24.1 us (4%)
  between operations  14.3 us (2%)
  other arithmetic  10.9 us (2%)
    psum x1, waiting for transfers between devices, body(): full_sum = lax.psum(local_term, ('batch', 'hist'))  419 us
    scatter x1, local copies, waits for them, and re-layouts, body(): outgoing = jnp.zeros((peer_count, capacity, feat_width), jnp.bfloat16).at...  34.2 us
    scatter x1, local copies, waits for them, and re-layouts, body(): jnp.zeros((peer_count, capacity), jnp.int32).at[owners, position]  21.7 us
    all_to_all x1, waiting for transfers between devices, body(): lax.all_to_all(taken, 'hist', split_axis=0, concat_axis=0, tiled=True)  19.6 us
  transfers between devices with their start and end apart: 4, of which 4 were waited for; matrix products, arithmetic and copies ran while one was open for 8% of the time, Pallas kernels for 0%

commit v1 on v0

v1 whole, which is shorter than its diff:
```python
import functools

import jax
import jax.numpy as jnp
from jax import lax
from jax.experimental import pallas as pl
from jax.experimental.pallas import tpu as pltpu
from jax.sharding import PartitionSpec as P

F32 = jnp.float32
BF16 = jnp.bfloat16
LANES = 128
CAP = 16
ROWS_T = (((1,), (1,)), ((), ()))
COLS_T = (((0,), (0,)), ((), ()))


def dot(a, b, dims=(((1,), (0,)), ((), ()))):
    return lax.dot_general(a, b, dims, preferred_element_type=F32)


def in_edge_order(first_tile, values):
    half = values.shape[1] // 2
    swapped = jnp.concatenate([values[:, half:], values[:, :half]], axis=1)
    return jnp.where(first_tile == 0, values, swapped)


def slot_places(owners, peers):
    slots = owners.shape[1]
    named = lax.broadcasted_iota(jnp.int32, (peers, slots), 0) == owners
    named = jnp.where(named, 1.0, 0.0)
    earlier = (
        lax.broadcasted_iota(jnp.int32, (slots, slots), 0)
        < lax.broadcasted_iota(jnp.int32, (slots, slots), 1)
    )
    rank = dot(named.astype(BF16), jnp.where(earlier, 1.0, 0.0).astype(BF16))
    return named, jnp.sum(named * rank, axis=0, keepdims=True).astype(jnp.int32)


def request_kernel(tile_ref, owner_ref, row_ref, ids_ref):
    peers = ids_ref.shape[0]
    first = tile_ref[0, 0]
    owners = in_edge_order(first, owner_ref[...])
    rows = in_edge_order(first, row_ref[...])
    named, place = slot_places(owners, peers)
    spot = lax.broadcasted_iota(jnp.int32, (LANES, rows.shape[1]), 0) == place
    spot = jnp.where(spot, 1.0, 0.0).astype(BF16)
    low = (rows % LANES).astype(F32)
    high = (rows // LANES).astype(F32)
    ids = dot((named * low).astype(BF16), spot, ROWS_T) + LANES * dot(
        (named * high).astype(BF16), spot, ROWS_T
    )
    ids_ref[...] = ids.astype(jnp.int32).reshape(ids_ref.shape)


def coef_kernel(peers, node_rows, tile_ref, owner_ref, row_ref, edge_ref, all_ref, inside_ref):
    first = tile_ref[0, 0]
    owners = in_edge_order(first, owner_ref[...])
    rows = in_edge_order(first, row_ref[...])
    _, place = slot_places(owners, peers)
    target = owners * CAP + place
    total = all_ref.shape[1]
    at = lax.broadcasted_iota(jnp.int32, (total, target.shape[1]), 0) == target
    moved = jnp.where(at, 1.0, 0.0)
    edge = edge_ref[...]
    all_ref[...] = dot(edge, moved.astype(BF16), ROWS_T).astype(BF16)
    kept = jnp.where(rows < node_rows, moved, 0.0).astype(BF16)
    inside_ref[...] = dot(edge, kept, ROWS_T).astype(BF16)


def gather_kernel(ids_ref, feats_ref, history_ref, taken_ref, pick_ref):
    node_rows, width = feats_ref.shape
    table_rows = history_ref.shape[0]
    peers = ids_ref.shape[0]
    ids = ids_ref[...].reshape(peers, LANES).astype(F32)
    ids = jnp.concatenate([ids, jnp.zeros((LANES - peers, LANES), F32)], axis=0)
    by_place = ids.T.astype(jnp.int32)
    columns = lax.broadcasted_iota(jnp.int32, (CAP, node_rows + table_rows), 1)
    part = peers // 4
    for start in range(0, peers, part):
        picks = [
            jnp.where(columns == by_place[:CAP, g : g + 1], 1.0, 0.0).astype(BF16)
            for g in range(start, start + part)
        ]
        pick = jnp.concatenate(picks, axis=0)
        near, far = pick[:, :node_rows], pick[:, node_rows:]
        pick_ref[start * CAP : (start + part) * CAP, :] = near
        emb = dot(near, feats_ref[...]) + dot(far, history_ref[:, :width])
        aux = dot(far, history_ref[:, width:])
        taken_ref[start : start + part, :, :width] = emb.astype(BF16).reshape(part, CAP, width)
        taken_ref[start : start + part, :, width:] = aux.astype(BF16).reshape(part, CAP, width)


def layer_kernel(
    pulled_ref, all_ref, inside_ref, feats_ref, weight_ref, grad_ref, out_ref, part_ref, send_ref
):
    peers = pulled_ref.shape[0]
    node_rows, width = feats_ref.shape
    pulled = pulled_ref[...].reshape(peers * CAP, 2 * width)
    both = dot(all_ref[...], pulled)
    mixed = (feats_ref[...].astype(F32) + both[:, :width]).astype(BF16)
    pre = dot(mixed, weight_ref[...])
    gate = jax.nn.sigmoid(pre)
    out_ref[...] = (pre * gate).astype(BF16)
    grad_pre = (grad_ref[...].astype(F32) * gate * (1.0 + pre * (1.0 - gate))).astype(BF16)
    grad_mixed = dot(grad_pre, weight_ref[...], ROWS_T).astype(BF16)
    part_ref[...] = grad_mixed.astype(F32) + both[:, width:]
    slot_grad = dot(inside_ref[...], grad_mixed, COLS_T).astype(BF16)
    send_ref[:, :, :width] = slot_grad.reshape(peers, CAP, width)
    share = width // peers
    rest = share - CAP
    half = width // 2
    for chunk in range(2):
        span = width // 2
        term = dot(mixed[:, chunk * span : (chunk + 1) * span], grad_pre, COLS_T)
        for i in range(peers // 2):
            peer = chunk * (peers // 2) + i
            rows = term[i * share : (i + 1) * share, :]
            tail = rows[CAP:, :]
            tail = jnp.concatenate([tail[:, :half], tail[:, half:]], axis=0)
            send_ref[peer, :, width : 2 * width] = rows[:CAP, :].astype(BF16)
            send_ref[peer, :, 2 * width :] = tail.astype(BF16)


def weight_kernel(back_ref, near_ref):
    width = near_ref.shape[2]
    terms = jnp.sum(back_ref[:, :, width:].astype(F32), axis=0)
    head = terms[:, :width]
    tail = terms[:, width:]
    half = tail.shape[0] // 2
    tail = jnp.concatenate([tail[:half, :], tail[half:, :]], axis=1)
    share = jnp.concatenate([head, tail], axis=0).astype(BF16)
    for i in range(near_ref.shape[0]):
        near_ref[i] = share


def final_kernel(back_ref, pick_ref, part_ref, grad_ref):
    peers = back_ref.shape[0]
    width = part_ref.shape[1]
    slots = back_ref[:, :, :width].reshape(peers * CAP, width)
    returned = dot(pick_ref[...], slots, COLS_T)
    grad_ref[...] = (part_ref[...] + returned).astype(BF16)


def call(kernel, out_shape, *args, smem=0, cost=None):
    in_specs = [
        pl.BlockSpec(memory_space=pltpu.SMEM if i < smem else pltpu.VMEM) for i in range(len(args))
    ]
    single = not isinstance(out_shape, (list, tuple))
    out_specs = pl.BlockSpec(memory_space=pltpu.VMEM)
    return pl.pallas_call(
        kernel,
        out_shape=out_shape,
        in_specs=in_specs,
        out_specs=out_specs if single else [out_specs] * len(out_shape),
        compiler_params=pltpu.CompilerParams(vmem_limit_bytes=40 << 20),
        cost_estimate=cost,
    )(*args)


def swap(values, axis, groups=None):
    return lax.all_to_all(
        values, axis, split_axis=0, concat_axis=0, tiled=True, axis_index_groups=groups
    )


def body(feats, history, weight, edge_coef, tile_map, nbr_owner, nbr_row, grad_out):
    peers = lax.axis_size("hist")
    planes = lax.axis_size("batch")
    node_rows, width = feats.shape[1:]
    slots = nbr_row.shape[1]
    capacity = 2 * slots // peers
    assert capacity == CAP
    shape = jax.ShapeDtypeStruct
    owners = nbr_owner.reshape(1, slots)
    ids = call(
        request_kernel, shape((peers, 1, LANES), jnp.int32), tile_map, owners, nbr_row, smem=1
    )
    received = swap(ids, "hist")
    coef, coef_inside = call(
        functools.partial(coef_kernel, peers, node_rows),
        [shape((node_rows, peers * CAP), BF16)] * 2,
        tile_map,
        owners,
        nbr_row,
        edge_coef[0],
        smem=1,
    )
    taken, pick = call(
        gather_kernel,
        [shape((peers, CAP, 2 * width), BF16), shape((peers * CAP, node_rows), BF16)],
        received,
        feats[0],
        history,
    )
    pulled = swap(taken, "hist")
    share = width // peers
    sent_width = width + share * width // CAP
    out_rows, part, sent = call(
        layer_kernel,
        [
            shape((node_rows, width), BF16),
            shape((node_rows, width), F32),
            shape((peers, CAP, sent_width), BF16),
        ],
        pulled,
        coef,
        coef_inside,
        feats[0],
        weight,
        grad_out[0],
    )
    back = swap(sent, "hist")
    side = 4
    near = [[a * side + i for i in range(side)] for a in range(planes // side)]
    far = [[a + side * i for i in range(planes // side)] for a in range(side)]
    term = call(weight_kernel, shape((side, share, width), BF16), back)
    term = swap(term, "batch", near)
    grad_rows = call(final_kernel, shape((node_rows, width), BF16), back, pick, part)
    term = jnp.sum(term.astype(F32), axis=0).astype(BF16)
    term = jnp.broadcast_to(term[None], (planes // side, share, width))
    term = swap(term, "batch", far)
    weight_share = jnp.sum(term.astype(F32), axis=0)
    return (out_rows[None], grad_rows[None], weight_share)


def solution(mesh):
    return jax.shard_map(
        body,
        mesh=mesh,
        in_specs=(
            P(("batch", "hist"), None, None),
            P("hist", None),
            P(),
            P(("batch", "hist"), None, None),
            P(("batch", "hist"), None),
            P(("batch", "hist"), None, None),
            P(("batch", "hist"), None),
            P(("batch", "hist"), None, None),
        ),
        out_specs=(
            P(("batch", "hist"), None, None),
            P(("batch", "hist"), None, None),
            P("hist", None),
        ),
        check_vma=False,
    )
```

time: 581 us -> 126 us (0.22)
  waiting for transfers between devices: 455 us -> 32.5 us
  local copies, waits for them, and re-layouts: 69.6 us -> 8.52 us
  blocking collectives: 0 us -> 57.9 us
  between operations: 14.3 us -> 0.76 us
  other arithmetic: 10.9 us -> 0.68 us
  Pallas kernels: 0 us -> 6.83 us
  starting transfers between devices: 24.1 us -> 18.2 us
    psum x1 -> x0, waiting for transfers between devices: 419 us -> none  [body(): full_sum = lax.psum(local_term, ('batch', 'hist'))]
    all_to_all x0 -> x3, blocking collectives: none -> 57.9 us  [swap(): lax.all_to_all(values, axis, split_axis=0, concat_axis=0, tiled=True, axi...]
    scatter x3 -> x0, local copies, waits for them, and re-layouts: 56.7 us -> none  [the longest x1 34.2 us: body(): outgoing = jnp.zeros((peer_count, capacity, feat_width), jnp.bfloat16).at...]
    gather x4 -> x0, local copies, waits for them, and re-layouts: 7.87 us -> none  [the longest x1 3.76 us: body(): pulled = answered[owners, position]]
    unnamed x19 -> x36, local copies, waits for them, and re-layouts: 0.21 us -> 7.86 us
    pallas_call x0 -> x6, Pallas kernels: none -> 6.83 us  [call(): pl.pallas_call(kernel, out_shape=out_shape, in_specs=in_specs, out_specs=...]
    all_to_all x3 -> x2, starting transfers between devices: 24 us -> 18.2 us  [swap(): lax.all_to_all(values, axis, split_axis=0, concat_axis=0, tiled=True, axi...]
    all_to_all x3 -> x2, waiting for transfers between devices: 35.9 us -> 32.5 us  [swap(): lax.all_to_all(values, axis, split_axis=0, concat_axis=0, tiled=True, axi...]
  transfers between devices with their start and end apart: 4 -> 2, of which waited for: 4 -> 2; matrix products, arithmetic and copies ran while one was open for 8% -> 0% of each run, Pallas kernels for 0% -> 2%
where the time goes in v1:
time: 126 us; the launch traced here: 125 us
  blocking collectives  57.9 us (46%)
  waiting for transfers between devices  32.5 us (26%)
  starting transfers between devices  18.2 us (14%)
  local copies, waits for them, and re-layouts  8.52 us (7%)
  Pallas kernels  6.83 us (5%)
    all_to_all x3, blocking collectives, swap(): lax.all_to_all(values, axis, split_axis=0, concat_axis=0, tiled=True, axi...  57.9 us
    all_to_all x2, waiting for transfers between devices, swap(): lax.all_to_all(values, axis, split_axis=0, concat_axis=0, tiled=True, axi...  32.5 us
    all_to_all x2, starting transfers between devices, swap(): lax.all_to_all(values, axis, split_axis=0, concat_axis=0, tiled=True, axi...  18.2 us
    unnamed x36, local copies, waits for them, and re-layouts  7.86 us
    pallas_call x6, Pallas kernels, call(): pl.pallas_call(kernel, out_shape=out_shape, in_specs=in_specs, out_specs=...  6.83 us
  transfers between devices with their start and end apart: 2, of which 2 were waited for; matrix products, arithmetic and copies ran while one was open for 0% of the time, Pallas kernels for 2%

profile of v1, /device:TPU:6, one launch (start us, length us, event | category | flops | bytes accessed | tf_op | source)
XLA Modules:
  0.0 125.4 jit_solution(2196749951645327323)
XLA Ops:
  0.6 0.7 copy-done.12
  1.3 0.7 copy-done.14
  2.0 0.7 copy-done.16
  2.6 0.9 shard_map.103
  3.5 14.1 %all_to_all.25.ids_ref = s32[32,1,128]{2,1,0:T(1,128)S(1)} all-to-all(s32[32,1,128]{2,1,0:T(1,128)S(1)} %shard_map.103), channel_id=1, replica_groups=mesh['batch'=16,'hist'=32] {'hist'}, dimensions={0} | all-to-all | bytes 32768 | tf_op jit(solution)/shard_map/all_to_all | solution.py:162
  17.7 1.1 copy-done.1
  18.8 0.9 copy-done.2
  19.7 2.1 %shard_map.104 = (bf16[32,16,1536]{2,1,0:T(8,128)(2,1)}, bf16[512,128]{1,0:T(8,128)(2,1)S(1)}) custom-call(s32[32,1,128]{2,1,0:T(1,128)S(1)} %all_to_all.25.ids_ref, bf16[128,768]{1,0:T(8,128)(2,1)S(1)} %bitcast.6, bf16[256,1536]{1,0:T(8,128)(2,1)S(1)} %copy-done.1), custom_call_target="tpu_custom_call" | custom-call | tf_op jit(solution)/shard_map/pallas_call | solution.py:151
  21.8 0.6 copy-done.5
  22.5 5.9 %all-to-all-start.1 = ((bf16[32,16,1536]{2,1,0:T(8,128)(2,1)}), bf16[32,16,1536]{2,1,0:T(8,128)(2,1)S(1)}, u32[]{:S(2)}, u32[]{:S(2)}) async-start(bf16[32,16,1536]{2,1,0:T(8,128)(2,1)} %get-tuple-element.10), calls=%async_computation.1 | async-start | bytes 3145728 | tf_op jit(solution)/shard_map/all_to_all | solution.py:162
  28.4 1.0 shard_map.105
  29.5 0.6 copy-done.7
  30.1 0.7 copy-done.9
  30.8 17.6 %all-to-all-done.1.pulled_ref = bf16[32,16,1536]{2,1,0:T(8,128)(2,1)S(1)} async-done(((bf16[32,16,1536]{2,1,0:T(8,128)(2,1)}), bf16[32,16,1536]{2,1,0:T(8,128)(2,1)S(1)}, u32[]{:S(2)}, u32[]{:S(2)}) %all-to-all-start.1) | async-done | bytes 1572896 | tf_op jit(solution)/shard_map/all_to_all | solution.py:162
  48.4 0.9 copy-done.8
  49.3 0.9 copy-done.10
  50.2 1.7 %shard_map.106 = (bf16[128,768]{1,0:T(8,128)(2,1)}, f32[128,768]{1,0:T(8,128)S(1)}, bf16[32,16,1920]{2,1,0:T(8,128)(2,1)S(1)}) custom-call(bf16[32,16,1536]{2,1,0:T(8,128)(2,1)S(1)} %all-to-all-done.1.pulled_ref, bf16[128,512]{1,0:T(8,128)(2,1)S(1)} %copy-done.8, bf16[128,512]{1,0:T(8,128)(2,1)S(1)} %copy-done.10, bf16[128,768]{1,0:T(8,128)(2,1)S(1)} %bitcast.7, ...), custom_call_target="tpu_custom_call" | custom-call | tf_op jit(solution)/shard_map/pallas_call | solution.py:151
  51.8 31.6 %all_to_all.26.back_ref = bf16[32,16,1920]{2,1,0:T(8,128)(2,1)S(1)} all-to-all(bf16[32,16,1920]{2,1,0:T(8,128)(2,1)S(1)} %get-tuple-element.14), channel_id=1, replica_groups=mesh['batch'=16,'hist'=32] {'hist'}, dimensions={0} | all-to-all | bytes 3932160 | tf_op jit(solution)/shard_map/all_to_all | solution.py:162
  83.6 12.2 %all_to_all.27 = bf16[4,24,768]{2,1,0:T(8,128)(2,1)S(1)} all-to-all(bf16[4,24,768]{2,1,0:T(8,128)(2,1)S(1)} %shard_map.108), channel_id=1, replica_groups={{0,32,64,96},{128,160,192,224},{256,288,320,352},{384,416,448,480},{1,3..., dimensions={0} | all-to-all | bytes 294912 | tf_op jit(solution)/shard_map/all_to_all | solution.py:162
  95.8 0.7 broadcast_in_dim.14
  96.5 12.4 %all-to-all-start.4 = ((bf16[4,24,768]{2,1,0:T(8,128)(2,1)}), bf16[4,24,768]{2,1,0:T(8,128)(2,1)S(1)}, u32[]{:S(2)}, u32[]{:S(2)}) async-start(bf16[4,24,768]{2,1,0:T(8,128)(2,1)} %broadcast_in_dim.14), calls=%async_computation.4 | async-start | bytes 294912 | tf_op jit(solution)/shard_map/all_to_all | solution.py:162
  108.9 1.0 shard_map.107
  109.8 14.9 %all-to-all-done.4 = bf16[4,24,768]{2,1,0:T(8,128)(2,1)S(1)} async-done(((bf16[4,24,768]{2,1,0:T(8,128)(2,1)}), bf16[4,24,768]{2,1,0:T(8,128)(2,1)S(1)}, u32[]{:S(2)}, u32[]{:S(2)}) %all-to-all-start.4) | async-done | bytes 147488 | tf_op jit(solution)/shard_map/all_to_all | solution.py:162
  124.8 0.7 convert_reduce_fusion
  (28 shorter events, 0.2 us)
Async XLA Ops:
  0.6 0.7 copy-start.12
  1.3 0.7 copy-start.14
  2.0 0.7 copy-start.16
  17.7 1.1 copy-start.1
  18.8 0.9 copy-start.2
  21.8 0.6 copy-start.5
  22.4 5.9 %copy-start.11 = (bf16[1,128,256]{2,1,0:T(8,128)(2,1)S(1)}, bf16[1,128,256]{2,1,0:T(8,128)(2,1)}, u32[]{:S(2)}) copy-start(bf16[1,128,256]{2,1,0:T(8,128)(2,1)} %param.11) | copy-start | bytes 196612
  22.5 5.9 %copy-start.13 = (s32[1,256,1]{1,2,0:T(1,128)S(1)}, s32[1,256,1]{1,2,0:T(1,128)}, u32[]{:S(2)}) copy-start(s32[1,256,1]{1,2,0:T(1,128)} %param.13) | copy-start | bytes 3076
  22.5 5.9 %copy-start.15 = (s32[1,256]{1,0:T(1,128)S(1)}, s32[1,256]{1,0:T(1,128)}, u32[]{:S(2)}) copy-start(s32[1,256]{1,0:T(1,128)} %row_ref.3) | copy-start | bytes 3076
  22.5 5.9 %copy-start.17 = (s32[1,2]{1,0:T(1,128)S(1)}, s32[1,2]{1,0:T(1,128)}, u32[]{:S(2)}) copy-start(s32[1,2]{1,0:T(1,128)} %tile_ref.3) | copy-start | bytes 28
  22.5 25.9 %copy-start = (bf16[768,768]{1,0:T(8,128)(2,1)S(1)}, bf16[768,768]{1,0:T(8,128)(2,1)}, u32[]{:S(2)}) copy-start(bf16[768,768]{1,0:T(8,128)(2,1)} %weight_ref.1) | copy-start | bytes 3538948
  22.5 25.9 %copy-start.3 = (bf16[1,128,768]{2,1,0:T(8,128)(2,1)S(1)}, bf16[1,128,768]{2,1,0:T(8,128)(2,1)}, u32[]{:S(2)}) copy-start(bf16[1,128,768]{2,1,0:T(8,128)(2,1)} %param.8) | copy-start | bytes 589828
  22.5 25.9 %copy-start.4 = (bf16[1,128,768]{2,1,0:T(8,128)(2,1)S(1)}, bf16[1,128,768]{2,1,0:T(8,128)(2,1)}, u32[]{:S(2)}) copy-start(bf16[1,128,768]{2,1,0:T(8,128)(2,1)} %param.15) | copy-start | bytes 589828
  22.5 25.9 %all-to-all-start.1 = ((bf16[32,16,1536]{2,1,0:T(8,128)(2,1)}), bf16[32,16,1536]{2,1,0:T(8,128)(2,1)S(1)}, u32[]{:S(2)}, u32[]{:S(2)}) async-start(bf16[32,16,1536]{2,1,0:T(8,128)(2,1)} %get-tuple-element.10), calls=%async_computation.1 | async-start | bytes 3145728 | tf_op jit(solution)/shard_map/all_to_all | solution.py:162
  29.5 0.7 copy-start.7
  30.1 0.7 copy-start.9
  48.4 0.9 copy-start.8
  49.3 0.9 copy-start.10
  83.4 25.4 %copy-start.6 = (bf16[512,128]{1,0:T(8,128)(2,1)S(1)}, bf16[512,128]{1,0:T(8,128)(2,1)}, u32[]{:S(2)}) copy-start(bf16[512,128]{1,0:T(8,128)(2,1)} %copy-done.5) | copy-start | bytes 393220
  96.5 28.3 %all-to-all-start.4 = ((bf16[4,24,768]{2,1,0:T(8,128)(2,1)}), bf16[4,24,768]{2,1,0:T(8,128)(2,1)S(1)}, u32[]{:S(2)}, u32[]{:S(2)}) async-start(bf16[4,24,768]{2,1,0:T(8,128)(2,1)} %broadcast_in_dim.14), calls=%async_computation.4 | async-start | bytes 294912 | tf_op jit(solution)/shard_map/all_to_all | solution.py:162

commit v2 on v1

v2 whole, which is shorter than its diff:
```python
import functools

import jax
import jax.numpy as jnp
from jax import lax
from jax.experimental import pallas as pl
from jax.experimental.pallas import tpu as pltpu
from jax.sharding import PartitionSpec as P

F32 = jnp.float32
BF16 = jnp.bfloat16
LANES = 128
CAP = 16
ROWS_T = (((1,), (1,)), ((), ()))
COLS_T = (((0,), (0,)), ((), ()))


def dot(a, b, dims=(((1,), (0,)), ((), ()))):
    return lax.dot_general(a, b, dims, preferred_element_type=F32)


def in_edge_order(first_tile, values):
    half = values.shape[1] // 2
    swapped = jnp.concatenate([values[:, half:], values[:, :half]], axis=1)
    return jnp.where(first_tile == 0, values, swapped)


def slot_places(owners, peers):
    slots = owners.shape[1]
    named = lax.broadcasted_iota(jnp.int32, (peers, slots), 0) == owners
    named = jnp.where(named, 1.0, 0.0)
    earlier = (
        lax.broadcasted_iota(jnp.int32, (slots, slots), 0)
        < lax.broadcasted_iota(jnp.int32, (slots, slots), 1)
    )
    rank = dot(named.astype(BF16), jnp.where(earlier, 1.0, 0.0).astype(BF16))
    return named, jnp.sum(named * rank, axis=0, keepdims=True).astype(jnp.int32)


def request_kernel(tile_in, owner_in, row_in, ids_ref, tile_ref, owner_ref, row_ref, sems):
    copies = [
        pltpu.make_async_copy(tile_in, tile_ref, sems.at[0]),
        pltpu.make_async_copy(owner_in, owner_ref, sems.at[1]),
        pltpu.make_async_copy(row_in, row_ref, sems.at[2]),
    ]
    for copy in copies:
        copy.start()
    for copy in copies:
        copy.wait()
    peers = ids_ref.shape[0]
    first = tile_ref[0, 0]
    owners = in_edge_order(first, owner_ref[...])
    rows = in_edge_order(first, row_ref[...])
    named, place = slot_places(owners, peers)
    spot = lax.broadcasted_iota(jnp.int32, (LANES, rows.shape[1]), 0) == place
    spot = jnp.where(spot, 1.0, 0.0).astype(BF16)
    low = (rows % LANES).astype(F32)
    high = (rows // LANES).astype(F32)
    ids = dot((named * low).astype(BF16), spot, ROWS_T) + LANES * dot(
        (named * high).astype(BF16), spot, ROWS_T
    )
    ids_ref[...] = ids.astype(jnp.int32).reshape(ids_ref.shape)


def gather_kernel(ids_ref, feats_in, history_in, taken_ref, pick_out, feats, history, pick, sems):
    node_rows, width = feats.shape
    table_rows = history.shape[0]
    peers = ids_ref.shape[0]
    load_feats = pltpu.make_async_copy(feats_in, feats, sems.at[0])
    load_history = pltpu.make_async_copy(history_in.at[:, :width], history, sems.at[1])
    load_feats.start()
    load_history.start()
    ids = ids_ref[...].reshape(peers, LANES).astype(F32)
    ids = jnp.concatenate([ids, jnp.zeros((LANES - peers, LANES), F32)], axis=0)
    by_place = ids.T.astype(jnp.int32)
    columns = lax.broadcasted_iota(jnp.int32, (CAP, node_rows + table_rows), 1)
    for g in range(peers):
        chosen = columns == by_place[:CAP, g : g + 1]
        pick[g * CAP : (g + 1) * CAP, :] = jnp.where(chosen, 1.0, 0.0).astype(BF16)
    store = pltpu.make_async_copy(pick, pick_out, sems.at[2])
    store.start()
    load_feats.wait()
    load_history.wait()
    part = peers // 4
    for start in range(0, peers, part):
        near = pick[start * CAP : (start + part) * CAP, :node_rows]
        far = pick[start * CAP : (start + part) * CAP, node_rows:]
        emb = dot(near, feats[...]) + dot(far, history[...])
        taken_ref[start : start + part] = emb.astype(BF16).reshape(part, CAP, width)
    store.wait()


def forward_kernel(
    peers,
    tile_ref,
    owner_ref,
    row_ref,
    edge_ref,
    pulled_ref,
    feats_ref,
    weight_ref,
    grad_ref,
    out_ref,
    pre_ref,
    own_ref,
    away_ref,
    all_ref,
    inside_ref,
):
    node_rows, width = feats_ref.shape
    half = width // 2
    first = tile_ref[0, 0]
    owners = in_edge_order(first, owner_ref[...])
    rows = in_edge_order(first, row_ref[...])
    _, place = slot_places(owners, peers)
    target = owners * CAP + place
    at = lax.broadcasted_iota(jnp.int32, (peers * CAP, target.shape[1]), 0) == target
    moved = jnp.where(at, 1.0, 0.0)
    coef = dot(edge_ref[...], moved.astype(BF16), ROWS_T).astype(BF16)
    pulled = pulled_ref[...].reshape(peers * CAP, width)
    mixed = (feats_ref[...].astype(F32) + dot(coef, pulled)).astype(BF16)
    pre = dot(mixed, weight_ref[...])
    gate = jax.nn.sigmoid(pre)
    grad_pre = (grad_ref[...].astype(F32) * gate * (1.0 + pre * (1.0 - gate))).astype(BF16)
    second_core = lax.axis_index("hist") % 2 == 1
    left, right = grad_pre[:, :half], grad_pre[:, half:]
    own_ref[:, :width] = mixed
    own_ref[:, width:] = jnp.where(second_core, right, left)
    away_ref[:, :width] = mixed
    away_ref[:, width:] = jnp.where(second_core, left, right)
    pre_ref[...] = grad_pre
    out_ref[...] = (pre * gate).astype(BF16)
    all_ref[...] = coef
    kept = jnp.where(rows < node_rows, moved, 0.0).astype(BF16)
    inside_ref[...] = dot(edge_ref[...], kept, ROWS_T).astype(BF16)


def term_kernel(peers, width, own_ref, away_ref, term_ref):
    mixed = jnp.concatenate([own_ref[:, :width], away_ref[:, :width]], axis=0)
    grad_pre = jnp.concatenate([own_ref[:, width:], away_ref[:, width:]], axis=0)
    share = width // peers
    step = 8
    term = dot(mixed, grad_pre, COLS_T)
    for peer in range(peers):
        blocks = [
            term[peer * share + i : peer * share + i + step, :] for i in range(0, share, step)
        ]
        term_ref[peer] = jnp.concatenate(blocks, axis=1).astype(BF16)


def backward_kernel(
    pre_ref, weight_ref, inside_ref, pick_in, history_in, send_ref, mixed_ref, pick, aux, sems
):
    node_rows, width = mixed_ref.shape
    peers = send_ref.shape[0]
    load_pick = pltpu.make_async_copy(pick_in, pick, sems.at[0])
    load_aux = pltpu.make_async_copy(history_in.at[:, width:], aux, sems.at[1])
    load_pick.start()
    load_aux.start()
    grad_mixed = dot(pre_ref[...], weight_ref[...], ROWS_T).astype(BF16)
    mixed_ref[...] = grad_mixed
    slot_grad = dot(inside_ref[...], grad_mixed, COLS_T).astype(BF16)
    send_ref[:, :, :width] = slot_grad.reshape(peers, CAP, width)
    load_pick.wait()
    load_aux.wait()
    taken = dot(pick[:, node_rows:], aux[...]).astype(BF16)
    send_ref[:, :, width:] = taken.reshape(peers, CAP, width)


def weight_kernel(terms_ref, sum_ref):
    peers, step = terms_ref.shape[:2]
    for core in range(2):
        total = terms_ref[core].astype(F32)
        for peer in range(core + 2, peers, 2):
            total = total + terms_ref[peer].astype(F32)
        sum_ref[core * step : (core + 1) * step, :] = total.astype(BF16)


def add_kernel(a_ref, b_ref, c_ref, d_ref, sum_ref):
    total = a_ref[...].astype(F32) + b_ref[...].astype(F32)
    total = total + (c_ref[...].astype(F32) + d_ref[...].astype(F32))
    sum_ref[...] = total.astype(BF16)


def share_kernel(a_ref, b_ref, c_ref, d_ref, share_ref):
    total = a_ref[...].astype(F32) + b_ref[...].astype(F32)
    total = total + (c_ref[...].astype(F32) + d_ref[...].astype(F32))
    share, width = share_ref.shape
    half = width // 2
    step = total.shape[0] // 2
    for i in range(share // step):
        for core in range(2):
            share_ref[i * step : (i + 1) * step, core * half : (core + 1) * half] = total[
                core * step : (core + 1) * step, i * half : (i + 1) * half
            ]


def final_kernel(back_ref, pick_ref, all_ref, mixed_ref, grad_ref):
    peers = back_ref.shape[0]
    node_rows, width = mixed_ref.shape
    slots = back_ref[:, :, :width].reshape(peers * CAP, width)
    aux = back_ref[:, :, width:].reshape(peers * CAP, width)
    returned = dot(pick_ref[:, :node_rows], slots, COLS_T)
    compensation = dot(all_ref[...], aux)
    total = mixed_ref[...].astype(F32) + returned + compensation
    grad_ref[...] = total.astype(BF16)


def call(kernel, out_shape, *args, smem=(), hbm=(), hbm_out=(), scratch=()):
    spaces = [
        pltpu.SMEM if i in smem else pltpu.HBM if i in hbm else pltpu.VMEM
        for i in range(len(args))
    ]
    single = not isinstance(out_shape, (list, tuple))
    out_shape = [out_shape] if single else out_shape
    out_spaces = [pltpu.HBM if i in hbm_out else pltpu.VMEM for i in range(len(out_shape))]
    result = pl.pallas_call(
        kernel,
        out_shape=out_shape,
        in_specs=[pl.BlockSpec(memory_space=space) for space in spaces],
        out_specs=[pl.BlockSpec(memory_space=space) for space in out_spaces],
        scratch_shapes=list(scratch),
        compiler_params=pltpu.CompilerParams(vmem_limit_bytes=32 << 20),
    )(*args)
    return result[0] if single else result


def swap(values):
    return lax.all_to_all(values, "hist", split_axis=0, concat_axis=0, tiled=True)


def shift(values, axis, by):
    count = lax.axis_size(axis)
    return lax.ppermute(values, axis, [(i, (i + by) % count) for i in range(count)])


def body(feats, history, weight, edge_coef, tile_map, nbr_owner, nbr_row, grad_out):
    peers = lax.axis_size("hist")
    planes = lax.axis_size("batch")
    node_rows, width = feats.shape[1:]
    table_rows = history.shape[0]
    slots = nbr_row.shape[1]
    assert 2 * slots // peers == CAP and planes == 16
    share = width // peers
    shape = jax.ShapeDtypeStruct
    owners = nbr_owner.reshape(1, slots)
    ids = call(
        request_kernel,
        shape((peers, 1, LANES), jnp.int32),
        tile_map,
        owners,
        nbr_row,
        hbm=(0, 1, 2),
        scratch=(
            pltpu.SMEM(tile_map.shape, jnp.int32),
            pltpu.VMEM(owners.shape, jnp.int32),
            pltpu.VMEM(nbr_row.shape, jnp.int32),
            pltpu.SemaphoreType.DMA((3,)),
        ),
    )
    received = swap(ids)
    table = node_rows + table_rows
    taken, pick = call(
        gather_kernel,
        [shape((peers, CAP, width), BF16), shape((peers * CAP, table), BF16)],
        received,
        feats[0],
        history,
        hbm=(1, 2),
        hbm_out=(1,),
        scratch=(
            pltpu.VMEM((node_rows, width), BF16),
            pltpu.VMEM((table_rows, width), BF16),
            pltpu.VMEM((peers * CAP, table), BF16),
            pltpu.SemaphoreType.DMA((3,)),
        ),
    )
    pulled = swap(taken)
    out_rows, grad_pre, own, away, coef, coef_inside = call(
        functools.partial(forward_kernel, peers),
        [
            shape((node_rows, width), BF16),
            shape((node_rows, width), BF16),
            shape((node_rows, width + width // 2), BF16),
            shape((node_rows, width + width // 2), BF16),
            shape((node_rows, peers * CAP), BF16),
            shape((node_rows, peers * CAP), BF16),
        ],
        tile_map,
        owners,
        nbr_row,
        edge_coef[0],
        pulled,
        feats[0],
        weight,
        grad_out[0],
        smem=(0,),
    )
    away = lax.ppermute(away, "hist", [(i, i ^ 1) for i in range(peers)])
    terms = call(
        functools.partial(term_kernel, peers, width),
        shape((peers, 8, share * width // 16), BF16),
        own,
        away,
    )
    grad_pre, terms = lax.optimization_barrier((grad_pre, terms))
    terms = swap(terms)
    sent, grad_mixed = call(
        backward_kernel,
        [shape((peers, CAP, 2 * width), BF16), shape((node_rows, width), BF16)],
        grad_pre,
        weight,
        coef_inside,
        pick,
        history,
        hbm=(3, 4),
        scratch=(
            pltpu.VMEM((peers * CAP, table), BF16),
            pltpu.VMEM((table_rows, width), BF16),
            pltpu.SemaphoreType.DMA((2,)),
        ),
    )
    sent, terms = lax.optimization_barrier((sent, terms))
    back = swap(sent)
    term = call(weight_kernel, shape((16, share * width // 16), BF16), terms)
    near = [shift(term, "batch", by) for by in (1, -1, 2)]
    term = call(add_kernel, shape(term.shape, BF16), term, *near)
    far = [shift(term, "batch", by) for by in (4, -4, 8)]
    weight_share = call(share_kernel, shape((share, width), F32), term, *far)
    grad_rows = call(
        final_kernel, shape((node_rows, width), BF16), back, pick, coef, grad_mixed
    )
    return (out_rows[None], grad_rows[None], weight_share)


def solution(mesh):
    return jax.shard_map(
        body,
        mesh=mesh,
        in_specs=(
            P(("batch", "hist"), None, None),
            P("hist", None),
            P(),
            P(("batch", "hist"), None, None),
            P(("batch", "hist"), None),
            P(("batch", "hist"), None, None),
            P(("batch", "hist"), None),
            P(("batch", "hist"), None, None),
        ),
        out_specs=(
            P(("batch", "hist"), None, None),
            P(("batch", "hist"), None, None),
            P("hist", None),
        ),
        check_vma=False,
    )
```

time: 126 us -> 116 us (0.921)
  starting transfers between devices: 18.2 us -> 48 us
  blocking collectives: 57.9 us -> 31.2 us
  waiting for transfers between devices: 32.5 us -> 19.5 us
  local copies, waits for them, and re-layouts: 8.52 us -> 6.28 us
  Pallas kernels: 6.83 us -> 8.98 us
    ppermute x0 -> x7, starting transfers between devices: none -> 36.1 us  [the longest x6 32.8 us: shift(): lax.ppermute(values, axis, [(i, (i + by) % count) for i in range(count)])]
    all_to_all x3 -> x2, blocking collectives: 57.9 us -> 31.2 us  [swap(): lax.all_to_all(values, 'hist', split_axis=0, concat_axis=0, tiled=True)]
    all_to_all x2, waiting for transfers between devices: 32.5 us -> 6.45 us  [swap(): lax.all_to_all(values, 'hist', split_axis=0, concat_axis=0, tiled=True)]
    ppermute x0 -> x7, waiting for transfers between devices: none -> 13.1 us  [the longest x6 11.9 us: shift(): lax.ppermute(values, axis, [(i, (i + by) % count) for i in range(count)])]
    all_to_all x2, starting transfers between devices: 18.2 us -> 11.9 us  [swap(): lax.all_to_all(values, 'hist', split_axis=0, concat_axis=0, tiled=True)]
    pallas_call x6 -> x9, Pallas kernels: 6.83 us -> 8.98 us  [call(): pl.pallas_call(kernel, out_shape=out_shape, in_specs=[pl.BlockSpec(memory...]
    unnamed x36 -> x32, local copies, waits for them, and re-layouts: 7.86 us -> 6.28 us
  transfers between devices with their start and end apart: 2 -> 9, of which waited for: 2 -> 4; matrix products, arithmetic and copies ran while one was open for 0% -> 0% of each run, Pallas kernels for 2% -> 2%
where the time goes in v2:
time: 116 us; the launch traced here: 115 us
  starting transfers between devices  48 us (41%)
  blocking collectives  31.2 us (27%)
  waiting for transfers between devices  19.5 us (17%)
  Pallas kernels  8.98 us (8%)
  local copies, waits for them, and re-layouts  6.28 us (5%)
    ppermute x6, starting transfers between devices, shift(): lax.ppermute(values, axis, [(i, (i + by) % count) for i in range(count)])  32.8 us
    all_to_all x2, blocking collectives, swap(): lax.all_to_all(values, 'hist', split_axis=0, concat_axis=0, tiled=True)  31.2 us
    all_to_all x2, starting transfers between devices, swap(): lax.all_to_all(values, 'hist', split_axis=0, concat_axis=0, tiled=True)  11.9 us
    ppermute x6, waiting for transfers between devices, shift(): lax.ppermute(values, axis, [(i, (i + by) % count) for i in range(count)])  11.9 us
    pallas_call x9, Pallas kernels, call(): pl.pallas_call(kernel, out_shape=out_shape, in_specs=[pl.BlockSpec(memory...  8.98 us
    all_to_all x2, waiting for transfers between devices, swap(): lax.all_to_all(values, 'hist', split_axis=0, concat_axis=0, tiled=True)  6.45 us
    unnamed x32, local copies, waits for them, and re-layouts  6.28 us
    ppermute x1, starting transfers between devices, body(): away = lax.ppermute(away, 'hist', [(i, i ^ 1) for i in range(peers)])  3.25 us
  transfers between devices with their start and end apart: 9, of which 4 were waited for; matrix products, arithmetic and copies ran while one was open for 0% of the time, Pallas kernels for 2%

profile of v2, /device:TPU:6, one launch (start us, length us, event | category | flops | bytes accessed | tf_op | source)
XLA Modules:
  0.0 114.9 jit_solution(6120059950487871384)
XLA Ops:
  2.8 0.9 shard_map.103
  3.7 14.1 %all_to_all.20.ids_ref = s32[32,1,128]{2,1,0:T(1,128)S(1)} all-to-all(s32[32,1,128]{2,1,0:T(1,128)S(1)} %shard_map.103), channel_id=1, replica_groups=mesh['batch'=16,'hist'=32] {'hist'}, dimensions={0} | all-to-all | bytes 32768 | tf_op jit(solution)/shard_map/all_to_all | solution.py:229
  17.8 1.1 copy-done.1
  18.9 0.9 copy-done.4
  19.9 1.3 %shard_map.104 = (bf16[32,16,768]{2,1,0:T(8,128)(2,1)S(1)}, bf16[512,384]{1,0:T(8,128)(2,1)S(1)}) custom-call(s32[32,1,128]{2,1,0:T(1,128)S(1)} %all_to_all.20.ids_ref, bf16[128,768]{1,0:T(8,128)(2,1)S(1)} %bitcast.6, bf16[256,1536]{1,0:T(8,128)(2,1)S(1)} %copy-done.1), custom_call_target="tpu_custom_call" | custom-call | tf_op jit(solution)/shard_map/pallas_call | solution.py:217
  21.2 17.1 %all_to_all.21.pulled_ref = bf16[32,16,768]{2,1,0:T(8,128)(2,1)S(1)} all-to-all(bf16[32,16,768]{2,1,0:T(8,128)(2,1)S(1)} %get-tuple-element.17), channel_id=1, replica_groups=mesh['batch'=16,'hist'=32] {'hist'}, dimensions={0} | all-to-all | bytes 1572864 | tf_op jit(solution)/shard_map/all_to_all | solution.py:229
  38.4 2.1 %shard_map.105 = (bf16[128,768]{1,0:T(8,128)(2,1)}, bf16[128,768]{1,0:T(8,128)(2,1)S(1)}, bf16[128,1152]{1,0:T(8,128)(2,1)S(1)}, bf16[128,1152]{1,0:T(8,128)(2,1...) custom-call(s32[1,2]{1,0:T(1,128)S(1)} %copy-done.15, s32[1,256]{1,0:T(1,128)S(1)} %bitcast.11, ...), custom_call_target="tpu_custom_call" | custom-call | tf_op jit(solution)/shard_map/pallas_call | solution.py:217
  40.6 3.2 %collective-permute-start = (bf16[128,1152]{1,0:T(8,128)(2,1)S(1)}, bf16[128,1152]{1,0:T(8,128)(2,1)S(1)}, u32[]{:S(2)}, u32[]{:S(2)}) collective-permute-start(bf16[128,1152]{1,0:T(8,128)(2,1)S(1)} %get-tuple-element.21), channel_id=1, source_target_pairs={{0,1},{1,0},{2,3},{3,2},{4,5},{5,4},{6,7},{7,6},{8,9},{9,8},{10,11... | collective-permute-start | bytes 884744 | tf_op jit(solution)/shard_map/ppermute | solution.py:299
  43.8 1.2 %collective-permute-done.away_ref = bf16[128,1152]{1,0:T(8,128)(2,1)S(1)} collective-permute-done((bf16[128,1152]{1,0:T(8,128)(2,1)S(1)}, bf16[128,1152]{1,0:T(8,128)(2,1)S(1)}, u32[]{:S(2)}, u32[]{:S(2)}) %collective-permute-start) | collective-permute-done | bytes 294944 | tf_op jit(solution)/shard_map/ppermute | solution.py:299
  45.0 1.2 %shard_map.106 = bf16[32,8,1152]{2,1,0:T(8,128)(2,1)} custom-call(bf16[128,1152]{1,0:T(8,128)(2,1)S(1)} %get-tuple-element.20.own_ref, bf16[128,1152]{1,0:T(8,128)(2,1)S(1)} %collective-permute-done.away_ref), custom_call_target="tpu_custom_call" | custom-call | tf_op jit(solution)/shard_map/pallas_call | solution.py:217
  46.2 5.5 %all-to-all-start.2 = ((bf16[32,8,1152]{2,1,0:T(8,128)(2,1)}), bf16[32,8,1152]{2,1,0:T(8,128)(2,1)S(1)}, u32[]{:S(2)}, u32[]{:S(2)}) async-start(bf16[32,8,1152]{2,1,0:T(8,128)(2,1)} %shard_map.106), calls=%async_computation.2 | async-start | bytes 1179648 | tf_op jit(solution)/shard_map/all_to_all | solution.py:229
  52.7 1.5 %shard_map.107 = (bf16[32,16,1536]{2,1,0:T(8,128)(2,1)S(1)}, bf16[128,768]{1,0:T(8,128)(2,1)S(1)}) custom-call(bf16[128,768]{1,0:T(8,128)(2,1)S(1)} %get-tuple-element.22.pre_ref, bf16[768,768]{1,0:T(8,128)(2,1)S(1)} %copy-done, bf16[128,512]{1,0:T(8,128)(2,1)S(1)} %copy-done.8, bf16[512,384]{1,0:T(8,128)(2,1)S(1)} %get-tuple-element.24.pick_in.pick_ref, ...), custom_call_target="tpu_custom_call" | custom-call | tf_op jit(solution)/shard_map/pallas_call | solution.py:217
  54.2 1.2 %copy-done.3 = bf16[32,16,1536]{2,1,0:T(8,128)(2,1)} copy-done((bf16[32,16,1536]{2,1,0:T(8,128)(2,1)}, bf16[32,16,1536]{2,1,0:T(8,128)(2,1)S(1)}, u32[]{:S(2)}) %copy-start.3) | copy-done | bytes 1572888
  55.4 6.5 %all-to-all-done.2.terms_ref = bf16[32,8,1152]{2,1,0:T(8,128)(2,1)S(1)} async-done(((bf16[32,8,1152]{2,1,0:T(8,128)(2,1)}), bf16[32,8,1152]{2,1,0:T(8,128)(2,1)S(1)}, u32[]{:S(2)}, u32[]{:S(2)}) %all-to-all-start.2) | async-done | bytes 589856 | tf_op jit(solution)/shard_map/all_to_all | solution.py:229
  61.9 6.4 %all-to-all-start.3 = ((bf16[32,16,1536]{2,1,0:T(8,128)(2,1)}), bf16[32,16,1536]{2,1,0:T(8,128)(2,1)S(1)}, u32[]{:S(2)}, u32[]{:S(2)}) async-start(bf16[32,16,1536]{2,1,0:T(8,128)(2,1)} %copy-done.3), calls=%async_computation.3 | async-start | bytes 3145728 | tf_op jit(solution)/shard_map/all_to_all | solution.py:229
  68.4 2.6 %collective-permute-start.1 = (bf16[16,1152]{1,0:T(8,128)(2,1)S(1)}, bf16[16,1152]{1,0:T(8,128)(2,1)S(1)}, u32[]{:S(2)}, u32[]{:S(2)}) collective-permute-start(bf16[16,1152]{1,0:T(8,128)(2,1)S(1)} %shard_map.109.a_ref), channel_id=1, source_target_pairs={{0,32},{32,64},{64,96},{96,128},{128,160},{160,192},{192,224},{224... | collective-permute-start | bytes 110600 | tf_op jit(solution)/shard_map/ppermute | solution.py:234
  71.0 9.5 %collective-permute-start.2 = (bf16[16,1152]{1,0:T(8,128)(2,1)S(1)}, bf16[16,1152]{1,0:T(8,128)(2,1)S(1)}, u32[]{:S(2)}, u32[]{:S(2)}) collective-permute-start(bf16[16,1152]{1,0:T(8,128)(2,1)S(1)} %shard_map.109.a_ref), channel_id=1, source_target_pairs={{0,480},{32,0},{64,32},{96,64},{128,96},{160,128},{192,160},{224,1... | collective-permute-start | bytes 110600 | tf_op jit(solution)/shard_map/ppermute | solution.py:234
  80.5 1.9 %collective-permute-start.3 = (bf16[16,1152]{1,0:T(8,128)(2,1)S(1)}, bf16[16,1152]{1,0:T(8,128)(2,1)S(1)}, u32[]{:S(2)}, u32[]{:S(2)}) collective-permute-start(bf16[16,1152]{1,0:T(8,128)(2,1)S(1)} %shard_map.109.a_ref), channel_id=1, source_target_pairs={{0,64},{32,96},{64,128},{96,160},{128,192},{160,224},{192,256},{22... | collective-permute-start | bytes 110600 | tf_op jit(solution)/shard_map/ppermute | solution.py:234
  82.4 6.4 %collective-permute-done.3.d_ref = bf16[16,1152]{1,0:T(8,128)(2,1)S(1)} collective-permute-done((bf16[16,1152]{1,0:T(8,128)(2,1)S(1)}, bf16[16,1152]{1,0:T(8,128)(2,1)S(1)}, u32[]{:S(2)}, u32[]{:S(2)}) %collective-permute-start.3) | collective-permute-done | bytes 36896 | tf_op jit(solution)/shard_map/ppermute | solution.py:234
  88.9 2.4 %collective-permute-start.4 = (bf16[16,1152]{1,0:T(8,128)(2,1)S(1)}, bf16[16,1152]{1,0:T(8,128)(2,1)S(1)}, u32[]{:S(2)}, u32[]{:S(2)}) collective-permute-start(bf16[16,1152]{1,0:T(8,128)(2,1)S(1)} %shard_map.110.a_ref), channel_id=1, source_target_pairs={{0,128},{32,160},{64,192},{96,224},{128,256},{160,288},{192,320},{... | collective-permute-start | bytes 110600 | tf_op jit(solution)/shard_map/ppermute | solution.py:234
  91.3 7.3 %collective-permute-start.5 = (bf16[16,1152]{1,0:T(8,128)(2,1)S(1)}, bf16[16,1152]{1,0:T(8,128)(2,1)S(1)}, u32[]{:S(2)}, u32[]{:S(2)}) collective-permute-start(bf16[16,1152]{1,0:T(8,128)(2,1)S(1)} %shard_map.110.a_ref), channel_id=1, source_target_pairs={{0,384},{32,416},{64,448},{96,480},{128,0},{160,32},{192,64},{224,... | collective-permute-start | bytes 110600 | tf_op jit(solution)/shard_map/ppermute | solution.py:234
  98.6 9.1 %collective-permute-start.6 = (bf16[16,1152]{1,0:T(8,128)(2,1)S(1)}, bf16[16,1152]{1,0:T(8,128)(2,1)S(1)}, u32[]{:S(2)}, u32[]{:S(2)}) collective-permute-start(bf16[16,1152]{1,0:T(8,128)(2,1)S(1)} %shard_map.110.a_ref), channel_id=1, source_target_pairs={{0,256},{32,288},{64,320},{96,352},{128,384},{160,416},{192,448},{... | collective-permute-start | bytes 110600 | tf_op jit(solution)/shard_map/ppermute | solution.py:234
  107.7 5.5 %collective-permute-done.6.d_ref = bf16[16,1152]{1,0:T(8,128)(2,1)S(1)} collective-permute-done((bf16[16,1152]{1,0:T(8,128)(2,1)S(1)}, bf16[16,1152]{1,0:T(8,128)(2,1)S(1)}, u32[]{:S(2)}, u32[]{:S(2)}) %collective-permute-start.6) | collective-permute-done | bytes 36896 | tf_op jit(solution)/shard_map/ppermute | solution.py:234
  113.8 1.1 shard_map.108
  (37 shorter events, 3.8 us)
Async XLA Ops:
  0.6 37.7 %copy-start = (bf16[768,768]{1,0:T(8,128)(2,1)S(1)}, bf16[768,768]{1,0:T(8,128)(2,1)}, u32[]{:S(2)}) copy-start(bf16[768,768]{1,0:T(8,128)(2,1)} %weight_ref.3) | copy-start | bytes 3538948
  0.6 0.8 copy-start.10
  1.4 0.7 copy-start.12
  17.8 1.1 copy-start.1
  18.9 0.9 copy-start.4
  19.9 18.5 %copy-start.5 = (bf16[1,128,768]{2,1,0:T(8,128)(2,1)S(1)}, bf16[1,128,768]{2,1,0:T(8,128)(2,1)}, u32[]{:S(2)}) copy-start(bf16[1,128,768]{2,1,0:T(8,128)(2,1)} %param.8) | copy-start | bytes 589828
  19.9 18.5 %copy-start.6 = (bf16[1,128,768]{2,1,0:T(8,128)(2,1)S(1)}, bf16[1,128,768]{2,1,0:T(8,128)(2,1)}, u32[]{:S(2)}) copy-start(bf16[1,128,768]{2,1,0:T(8,128)(2,1)} %param.15) | copy-start | bytes 589828
  19.9 18.5 %copy-start.9 = (bf16[1,128,256]{2,1,0:T(8,128)(2,1)S(1)}, bf16[1,128,256]{2,1,0:T(8,128)(2,1)}, u32[]{:S(2)}) copy-start(bf16[1,128,256]{2,1,0:T(8,128)(2,1)} %param.11) | copy-start | bytes 196612
  19.9 18.5 %copy-start.11 = (s32[1,256,1]{1,2,0:T(1,128)S(1)}, s32[1,256,1]{1,2,0:T(1,128)}, u32[]{:S(2)}) copy-start(s32[1,256,1]{1,2,0:T(1,128)} %param.13) | copy-start | bytes 3076
  19.9 18.5 %copy-start.13 = (s32[1,256]{1,0:T(1,128)S(1)}, s32[1,256]{1,0:T(1,128)}, u32[]{:S(2)}) copy-start(s32[1,256]{1,0:T(1,128)} %row_ref.1) | copy-start | bytes 3076
  19.9 18.5 %copy-start.15 = (s32[1,2]{1,0:T(1,128)S(1)}, s32[1,2]{1,0:T(1,128)}, u32[]{:S(2)}) copy-start(s32[1,2]{1,0:T(1,128)} %tile_ref.1) | copy-start | bytes 28
  40.6 11.2 %copy-start.7 = (bf16[128,512]{1,0:T(8,128)(2,1)}, bf16[128,512]{1,0:T(8,128)(2,1)S(1)}, u32[]{:S(2)}) copy-start(bf16[128,512]{1,0:T(8,128)(2,1)S(1)} %get-tuple-element.23.inside_ref) | copy-start | bytes 393220
  40.6 11.2 %copy-start.2 = (bf16[256,1536]{1,0:T(8,128)(2,1)S(1)}, bf16[256,1536]{1,0:T(8,128)(2,1)}, u32[]{:S(2)}) copy-start(bf16[256,1536]{1,0:T(8,128)(2,1)} %history_in.3) | copy-start | bytes 2359300
  40.6 4.4 %collective-permute-start = (bf16[128,1152]{1,0:T(8,128)(2,1)S(1)}, bf16[128,1152]{1,0:T(8,128)(2,1)S(1)}, u32[]{:S(2)}, u32[]{:S(2)}) collective-permute-start(bf16[128,1152]{1,0:T(8,128)(2,1)S(1)} %get-tuple-element.21), channel_id=1, source_target_pairs={{0,1},{1,0},{2,3},{3,2},{4,5},{5,4},{6,7},{7,6},{8,9},{9,8},{10,11... | collective-permute-start | bytes 884744 | tf_op jit(solution)/shard_map/ppermute | solution.py:299
  46.2 15.6 %all-to-all-start.2 = ((bf16[32,8,1152]{2,1,0:T(8,128)(2,1)}), bf16[32,8,1152]{2,1,0:T(8,128)(2,1)S(1)}, u32[]{:S(2)}, u32[]{:S(2)}) async-start(bf16[32,8,1152]{2,1,0:T(8,128)(2,1)} %shard_map.106), calls=%async_computation.2 | async-start | bytes 1179648 | tf_op jit(solution)/shard_map/all_to_all | solution.py:229
  51.8 0.9 copy-start.8
  54.2 1.2 %copy-start.3 = (bf16[32,16,1536]{2,1,0:T(8,128)(2,1)}, bf16[32,16,1536]{2,1,0:T(8,128)(2,1)S(1)}, u32[]{:S(2)}) copy-start(bf16[32,16,1536]{2,1,0:T(8,128)(2,1)S(1)} %get-tuple-element.27) | copy-start | bytes 4718596
  61.9 52.0 %all-to-all-start.3 = ((bf16[32,16,1536]{2,1,0:T(8,128)(2,1)}), bf16[32,16,1536]{2,1,0:T(8,128)(2,1)S(1)}, u32[]{:S(2)}, u32[]{:S(2)}) async-start(bf16[32,16,1536]{2,1,0:T(8,128)(2,1)} %copy-done.3), calls=%async_computation.3 | async-start | bytes 3145728 | tf_op jit(solution)/shard_map/all_to_all | solution.py:229
  68.4 14.0 %collective-permute-start.1 = (bf16[16,1152]{1,0:T(8,128)(2,1)S(1)}, bf16[16,1152]{1,0:T(8,128)(2,1)S(1)}, u32[]{:S(2)}, u32[]{:S(2)}) collective-permute-start(bf16[16,1152]{1,0:T(8,128)(2,1)S(1)} %shard_map.109.a_ref), channel_id=1, source_target_pairs={{0,32},{32,64},{64,96},{96,128},{128,160},{160,192},{192,224},{224... | collective-permute-start | bytes 110600 | tf_op jit(solution)/shard_map/ppermute | solution.py:234
  71.0 11.4 %collective-permute-start.2 = (bf16[16,1152]{1,0:T(8,128)(2,1)S(1)}, bf16[16,1152]{1,0:T(8,128)(2,1)S(1)}, u32[]{:S(2)}, u32[]{:S(2)}) collective-permute-start(bf16[16,1152]{1,0:T(8,128)(2,1)S(1)} %shard_map.109.a_ref), channel_id=1, source_target_pairs={{0,480},{32,0},{64,32},{96,64},{128,96},{160,128},{192,160},{224,1... | collective-permute-start | bytes 110600 | tf_op jit(solution)/shard_map/ppermute | solution.py:234
  80.5 8.4 %collective-permute-start.3 = (bf16[16,1152]{1,0:T(8,128)(2,1)S(1)}, bf16[16,1152]{1,0:T(8,128)(2,1)S(1)}, u32[]{:S(2)}, u32[]{:S(2)}) collective-permute-start(bf16[16,1152]{1,0:T(8,128)(2,1)S(1)} %shard_map.109.a_ref), channel_id=1, source_target_pairs={{0,64},{32,96},{64,128},{96,160},{128,192},{160,224},{192,256},{22... | collective-permute-start | bytes 110600 | tf_op jit(solution)/shard_map/ppermute | solution.py:234
  88.9 18.8 %collective-permute-start.4 = (bf16[16,1152]{1,0:T(8,128)(2,1)S(1)}, bf16[16,1152]{1,0:T(8,128)(2,1)S(1)}, u32[]{:S(2)}, u32[]{:S(2)}) collective-permute-start(bf16[16,1152]{1,0:T(8,128)(2,1)S(1)} %shard_map.110.a_ref), channel_id=1, source_target_pairs={{0,128},{32,160},{64,192},{96,224},{128,256},{160,288},{192,320},{... | collective-permute-start | bytes 110600 | tf_op jit(solution)/shard_map/ppermute | solution.py:234
  91.3 16.4 %collective-permute-start.5 = (bf16[16,1152]{1,0:T(8,128)(2,1)S(1)}, bf16[16,1152]{1,0:T(8,128)(2,1)S(1)}, u32[]{:S(2)}, u32[]{:S(2)}) collective-permute-start(bf16[16,1152]{1,0:T(8,128)(2,1)S(1)} %shard_map.110.a_ref), channel_id=1, source_target_pairs={{0,384},{32,416},{64,448},{96,480},{128,0},{160,32},{192,64},{224,... | collective-permute-start | bytes 110600 | tf_op jit(solution)/shard_map/ppermute | solution.py:234
  98.6 14.6 %collective-permute-start.6 = (bf16[16,1152]{1,0:T(8,128)(2,1)S(1)}, bf16[16,1152]{1,0:T(8,128)(2,1)S(1)}, u32[]{:S(2)}, u32[]{:S(2)}) collective-permute-start(bf16[16,1152]{1,0:T(8,128)(2,1)S(1)} %shard_map.110.a_ref), channel_id=1, source_target_pairs={{0,256},{32,288},{64,320},{96,352},{128,384},{160,416},{192,448},{... | collective-permute-start | bytes 110600 | tf_op jit(solution)/shard_map/ppermute | solution.py:234
  (1 other events, 0.7 us)

commit v3 on v2

--- a/solution.py
+++ b/solution.py
@@ -173,13 +173,13 @@
         total = terms_ref[core].astype(F32)
         for peer in range(core + 2, peers, 2):
             total = total + terms_ref[peer].astype(F32)
-        sum_ref[core * step : (core + 1) * step, :] = total.astype(BF16)
-
-
-def add_kernel(a_ref, b_ref, c_ref, d_ref, sum_ref):
-    total = a_ref[...].astype(F32) + b_ref[...].astype(F32)
-    total = total + (c_ref[...].astype(F32) + d_ref[...].astype(F32))
-    sum_ref[...] = total.astype(BF16)
+        total = total.astype(BF16)
+        for plane in range(sum_ref.shape[0]):
+            sum_ref[plane, core * step : (core + 1) * step, :] = total
+
+
+def add_kernel(near_ref, sum_ref):
+    sum_ref[...] = jnp.sum(near_ref[...].astype(F32), axis=0).astype(BF16)
 
 
 def share_kernel(a_ref, b_ref, c_ref, d_ref, share_ref):
@@ -206,7 +206,7 @@
     grad_ref[...] = total.astype(BF16)
 
 
-def call(kernel, out_shape, *args, smem=(), hbm=(), hbm_out=(), scratch=()):
+def call(kernel, out_shape, *args, smem=(), hbm=(), hbm_out=(), scratch=(), vmem=32):
     spaces = [
         pltpu.SMEM if i in smem else pltpu.HBM if i in hbm else pltpu.VMEM
         for i in range(len(args))
@@ -220,13 +220,15 @@
         in_specs=[pl.BlockSpec(memory_space=space) for space in spaces],
         out_specs=[pl.BlockSpec(memory_space=space) for space in out_spaces],
         scratch_shapes=list(scratch),
-        compiler_params=pltpu.CompilerParams(vmem_limit_bytes=32 << 20),
+        compiler_params=pltpu.CompilerParams(vmem_limit_bytes=vmem << 20),
     )(*args)
     return result[0] if single else result
 
 
-def swap(values):
-    return lax.all_to_all(values, "hist", split_axis=0, concat_axis=0, tiled=True)
+def swap(values, axis="hist", groups=None):
+    return lax.all_to_all(
+        values, axis, split_axis=0, concat_axis=0, tiled=True, axis_index_groups=groups
+    )
 
 
 def shift(values, axis, by):
@@ -251,6 +253,7 @@
         owners,
         nbr_row,
         hbm=(0, 1, 2),
+        vmem=60,
         scratch=(
             pltpu.SMEM(tile_map.shape, jnp.int32),
             pltpu.VMEM(owners.shape, jnp.int32),
@@ -268,6 +271,7 @@
         history,
         hbm=(1, 2),
         hbm_out=(1,),
+        vmem=60,
         scratch=(
             pltpu.VMEM((node_rows, width), BF16),
             pltpu.VMEM((table_rows, width), BF16),
@@ -320,11 +324,13 @@
             pltpu.SemaphoreType.DMA((2,)),
         ),
     )
-    sent, terms = lax.optimization_barrier((sent, terms))
+    side = 4
+    near = [[a * side + i for i in range(side)] for a in range(planes // side)]
+    term = call(weight_kernel, shape((side, 16, share * width // 16), BF16), terms)
+    term = swap(term, "batch", near)
+    sent, term = lax.optimization_barrier((sent, term))
     back = swap(sent)
-    term = call(weight_kernel, shape((16, share * width // 16), BF16), terms)
-    near = [shift(term, "batch", by) for by in (1, -1, 2)]
-    term = call(add_kernel, shape(term.shape, BF16), term, *near)
+    term = call(add_kernel, shape(term.shape[1:], BF16), term)
     far = [shift(term, "batch", by) for by in (4, -4, 8)]
     weight_share = call(share_kernel, shape((share, width), F32), term, *far)
     grad_rows = call(

time: 116 us -> 107 us (0.922)
  blocking collectives: 31.2 us -> 48.2 us
  starting transfers between devices: 48 us -> 35.4 us
  waiting for transfers between devices: 19.5 us -> 9.2 us
  local copies, waits for them, and re-layouts: 6.28 us -> 0.04 us
  Pallas kernels: 8.98 us -> 12.9 us
    all_to_all x2 -> x3, blocking collectives: 31.2 us -> 48.2 us  [swap(): lax.all_to_all(values, axis, split_axis=0, concat_axis=0, tiled=True, axi...]
    ppermute x6 -> x3, starting transfers between devices: 32.8 us -> 23 us  [shift(): lax.ppermute(values, axis, [(i, (i + by) % count) for i in range(count)])]
    ppermute x6 -> x3, waiting for transfers between devices: 11.9 us -> 3.72 us  [shift(): lax.ppermute(values, axis, [(i, (i + by) % count) for i in range(count)])]
    unnamed x32 -> x18, local copies, waits for them, and re-layouts: 6.28 us -> 0.04 us
    pallas_call x9, Pallas kernels: 8.98 us -> 12.9 us  [call(): pl.pallas_call(kernel, out_shape=out_shape, in_specs=[pl.BlockSpec(memory...]
    all_to_all x2, starting transfers between devices: 11.9 us -> 9.27 us  [swap(): lax.all_to_all(values, axis, split_axis=0, concat_axis=0, tiled=True, axi...]
    all_to_all x2, waiting for transfers between devices: 6.45 us -> 4.29 us  [swap(): lax.all_to_all(values, axis, split_axis=0, concat_axis=0, tiled=True, axi...]
  transfers between devices with their start and end apart: 9 -> 6, of which waited for: 4 -> 3; matrix products, arithmetic and copies ran while one was open for 0% -> 0% of each run, Pallas kernels for 2% -> 3%
where the time goes in v3:
time: 107 us
  blocking collectives  48.2 us (45%)
  starting transfers between devices  35.4 us (33%)
  Pallas kernels  12.9 us (12%)
  waiting for transfers between devices  9.2 us (9%)
    all_to_all x3, blocking collectives, swap(): lax.all_to_all(values, axis, split_axis=0, concat_axis=0, tiled=True, axi...  48.2 us
    ppermute x3, starting transfers between devices, shift(): lax.ppermute(values, axis, [(i, (i + by) % count) for i in range(count)])  23 us
    pallas_call x9, Pallas kernels, call(): pl.pallas_call(kernel, out_shape=out_shape, in_specs=[pl.BlockSpec(memory...  12.9 us
    all_to_all x2, starting transfers between devices, swap(): lax.all_to_all(values, axis, split_axis=0, concat_axis=0, tiled=True, axi...  9.27 us
    all_to_all x2, waiting for transfers between devices, swap(): lax.all_to_all(values, axis, split_axis=0, concat_axis=0, tiled=True, axi...  4.29 us
    ppermute x3, waiting for transfers between devices, shift(): lax.ppermute(values, axis, [(i, (i + by) % count) for i in range(count)])  3.72 us
    ppermute x1, starting transfers between devices, body(): away = lax.ppermute(away, 'hist', [(i, i ^ 1) for i in range(peers)])  3.11 us
  transfers between devices with their start and end apart: 6, of which 3 were waited for; matrix products, arithmetic and copies ran while one was open for 0% of the time, Pallas kernels for 3%

profile of v3, /device:TPU:6, one launch (start us, length us, event | category | flops | bytes accessed | tf_op | source)
XLA Modules:
  0.0 106.5 jit_solution(15246650507731745933)
XLA Ops:
  0.7 0.0 copy-start.3
  0.7 1.8 %shard_map.103 = s32[32,1,128]{2,1,0:T(1,128)} custom-call(s32[1,2]{1,0:T(1,128)} %tile_ref.1, s32[1,256]{1,0:T(1,128)} %bitcast.10, s32[1,256]{1,0:T(1,128)} %row_ref.1), custom_call_target="tpu_custom_call" | custom-call | tf_op jit(solution)/shard_map/pallas_call | solution.py:217
  2.5 15.4 %all_to_all.25.ids_ref = s32[32,1,128]{2,1,0:T(1,128)} all-to-all(s32[32,1,128]{2,1,0:T(1,128)} %shard_map.103), channel_id=1, replica_groups=mesh['batch'=16,'hist'=32] {'hist'}, dimensions={0} | all-to-all | bytes 32768 | tf_op jit(solution)/shard_map/all_to_all | solution.py:229
  17.9 3.3 %shard_map.104 = (bf16[32,16,768]{2,1,0:T(8,128)(2,1)}, bf16[512,384]{1,0:T(8,128)(2,1)}) custom-call(s32[32,1,128]{2,1,0:T(1,128)} %all_to_all.25.ids_ref, bf16[128,768]{1,0:T(8,128)(2,1)} %bitcast.6, bf16[256,1536]{1,0:T(8,128)(2,1)} %history_in.3), custom_call_target="tpu_custom_call" | custom-call | tf_op jit(solution)/shard_map/pallas_call | solution.py:217
  21.3 17.7 %all_to_all.26.pulled_ref = bf16[32,16,768]{2,1,0:T(8,128)(2,1)S(1)} all-to-all(bf16[32,16,768]{2,1,0:T(8,128)(2,1)} %get-tuple-element.17), channel_id=1, replica_groups=mesh['batch'=16,'hist'=32] {'hist'}, dimensions={0} | all-to-all | bytes 1572864 | tf_op jit(solution)/shard_map/all_to_all | solution.py:229
  39.0 2.1 %shard_map.105 = (bf16[128,768]{1,0:T(8,128)(2,1)}, bf16[128,768]{1,0:T(8,128)(2,1)S(1)}, bf16[128,1152]{1,0:T(8,128)(2,1)S(1)}, bf16[128,1152]{1,0:T(8,128)(2,1...) custom-call(s32[1,2]{1,0:T(1,128)S(1)} %copy-done.8, s32[1,256]{1,0:T(1,128)S(1)} %bitcast.11, ...), custom_call_target="tpu_custom_call" | custom-call | tf_op jit(solution)/shard_map/pallas_call | solution.py:217
  41.2 3.1 %collective-permute-start = (bf16[128,1152]{1,0:T(8,128)(2,1)S(1)}, bf16[128,1152]{1,0:T(8,128)(2,1)S(1)}, u32[]{:S(2)}, u32[]{:S(2)}) collective-permute-start(bf16[128,1152]{1,0:T(8,128)(2,1)S(1)} %get-tuple-element.21), channel_id=1, source_target_pairs={{0,1},{1,0},{2,3},{3,2},{4,5},{5,4},{6,7},{7,6},{8,9},{9,8},{10,11... | collective-permute-start | bytes 884744 | tf_op jit(solution)/shard_map/ppermute | solution.py:303
  44.3 1.2 %collective-permute-done.away_ref = bf16[128,1152]{1,0:T(8,128)(2,1)S(1)} collective-permute-done((bf16[128,1152]{1,0:T(8,128)(2,1)S(1)}, bf16[128,1152]{1,0:T(8,128)(2,1)S(1)}, u32[]{:S(2)}, u32[]{:S(2)}) %collective-permute-start) | collective-permute-done | bytes 294944 | tf_op jit(solution)/shard_map/ppermute | solution.py:303
  45.5 0.4 shard_map.106
  45.9 15.1 %all_to_all.27.terms_ref = bf16[32,8,1152]{2,1,0:T(8,128)(2,1)S(1)} all-to-all(bf16[32,8,1152]{2,1,0:T(8,128)(2,1)S(1)} %shard_map.106), channel_id=1, replica_groups=mesh['batch'=16,'hist'=32] {'hist'}, dimensions={0} | all-to-all | bytes 1179648 | tf_op jit(solution)/shard_map/all_to_all | solution.py:229
  60.9 0.7 shard_map.108
  61.7 3.5 %all-to-all-start.3 = ((bf16[4,16,1152]{2,1,0:T(8,128)(2,1)}), bf16[4,16,1152]{2,1,0:T(8,128)(2,1)S(1)}, u32[]{:S(2)}, u32[]{:S(2)}) async-start(bf16[4,16,1152]{2,1,0:T(8,128)(2,1)} %shard_map.108), calls=%async_computation.3 | async-start | bytes 294912 | tf_op jit(solution)/shard_map/all_to_all | solution.py:229
  65.2 2.7 %shard_map.107 = (bf16[32,16,1536]{2,1,0:T(8,128)(2,1)}, bf16[128,768]{1,0:T(8,128)(2,1)S(1)}) custom-call(bf16[128,768]{1,0:T(8,128)(2,1)S(1)} %get-tuple-element.22.pre_ref, bf16[768,768]{1,0:T(8,128)(2,1)S(1)} %copy-done, bf16[128,512]{1,0:T(8,128)(2,1)S(1)} %get-tuple-element.23.inside_ref, bf16[512,384]{1,0:T(8,128)(2,1)S(1)} %copy-done.2, ...), custom_call_target="tpu_custom_call" | custom-call | tf_op jit(solution)/shard_map/pallas_call | solution.py:217
  67.9 4.3 %all-to-all-done.3.near_ref = bf16[4,16,1152]{2,1,0:T(8,128)(2,1)S(1)} async-done(((bf16[4,16,1152]{2,1,0:T(8,128)(2,1)}), bf16[4,16,1152]{2,1,0:T(8,128)(2,1)S(1)}, u32[]{:S(2)}, u32[]{:S(2)}) %all-to-all-start.3) | async-done | bytes 147488 | tf_op jit(solution)/shard_map/all_to_all | solution.py:229
  72.2 5.8 %all-to-all-start.4 = ((bf16[32,16,1536]{2,1,0:T(8,128)(2,1)}), bf16[32,16,1536]{2,1,0:T(8,128)(2,1)S(1)}, u32[]{:S(2)}, u32[]{:S(2)}) async-start(bf16[32,16,1536]{2,1,0:T(8,128)(2,1)} %get-tuple-element.27), calls=%async_computation.4 | async-start | bytes 3145728 | tf_op jit(solution)/shard_map/all_to_all | solution.py:229
  78.0 9.0 %collective-permute-start.1 = (bf16[16,1152]{1,0:T(8,128)(2,1)S(1)}, bf16[16,1152]{1,0:T(8,128)(2,1)S(1)}, u32[]{:S(2)}, u32[]{:S(2)}) collective-permute-start(bf16[16,1152]{1,0:T(8,128)(2,1)S(1)} %shard_map.110.a_ref), channel_id=1, source_target_pairs={{0,128},{32,160},{64,192},{96,224},{128,256},{160,288},{192,320},{... | collective-permute-start | bytes 110600 | tf_op jit(solution)/shard_map/ppermute | solution.py:236
  87.0 3.3 %collective-permute-start.2 = (bf16[16,1152]{1,0:T(8,128)(2,1)S(1)}, bf16[16,1152]{1,0:T(8,128)(2,1)S(1)}, u32[]{:S(2)}, u32[]{:S(2)}) collective-permute-start(bf16[16,1152]{1,0:T(8,128)(2,1)S(1)} %shard_map.110.a_ref), channel_id=1, source_target_pairs={{0,384},{32,416},{64,448},{96,480},{128,0},{160,32},{192,64},{224,... | collective-permute-start | bytes 110600 | tf_op jit(solution)/shard_map/ppermute | solution.py:236
  90.2 10.8 %collective-permute-start.3 = (bf16[16,1152]{1,0:T(8,128)(2,1)S(1)}, bf16[16,1152]{1,0:T(8,128)(2,1)S(1)}, u32[]{:S(2)}, u32[]{:S(2)}) collective-permute-start(bf16[16,1152]{1,0:T(8,128)(2,1)S(1)} %shard_map.110.a_ref), channel_id=1, source_target_pairs={{0,256},{32,288},{64,320},{96,352},{128,384},{160,416},{192,448},{... | collective-permute-start | bytes 110600 | tf_op jit(solution)/shard_map/ppermute | solution.py:236
  101.1 0.0 collective-permute-done.1.b_ref
  101.1 0.0 collective-permute-done.2.c_ref
  101.1 3.7 %collective-permute-done.3.d_ref = bf16[16,1152]{1,0:T(8,128)(2,1)S(1)} collective-permute-done((bf16[16,1152]{1,0:T(8,128)(2,1)S(1)}, bf16[16,1152]{1,0:T(8,128)(2,1)S(1)}, u32[]{:S(2)}, u32[]{:S(2)}) %collective-permute-start.3) | collective-permute-done | bytes 36896 | tf_op jit(solution)/shard_map/ppermute | solution.py:236
  104.8 0.7 shard_map.111
  105.5 0.0 all-to-all-done.4.back_ref
  105.5 1.1 %shard_map.109 = bf16[128,768]{1,0:T(8,128)(2,1)} custom-call(bf16[32,16,1536]{2,1,0:T(8,128)(2,1)S(1)} %all-to-all-done.4.back_ref, bf16[512,384]{1,0:T(8,128)(2,1)S(1)} %copy-done.2, bf16[128,512]{1,0:T(8,128)(2,1)S(1)} %get-tuple-element.28.all_ref, bf16[128,768]{1,0:T(8,128)(2,1)S(1)} %get-tuple-element.29.mixed_ref), custom_call_target="tpu_custom_call" | custom-call | tf_op jit(solution)/shard_map/pallas_call | solution.py:217
  (18 shorter events, 0.1 us)
Async XLA Ops:
  0.6 38.4 %copy-start.6 = (s32[1,256,1]{1,2,0:T(1,128)S(1)}, s32[1,256,1]{1,2,0:T(1,128)}, u32[]{:S(2)}) copy-start(s32[1,256,1]{1,2,0:T(1,128)} %param.13) | copy-start | bytes 3076
  0.6 38.4 %copy-start.8 = (s32[1,2]{1,0:T(1,128)S(1)}, s32[1,2]{1,0:T(1,128)}, u32[]{:S(2)}) copy-start(s32[1,2]{1,0:T(1,128)} %tile_ref.1) | copy-start | bytes 28
  0.7 38.4 %copy-start.7 = (s32[1,256]{1,0:T(1,128)S(1)}, s32[1,256]{1,0:T(1,128)}, u32[]{:S(2)}) copy-start(s32[1,256]{1,0:T(1,128)} %row_ref.1) | copy-start | bytes 3076
  0.7 38.3 %copy-start.3 = (bf16[1,128,768]{2,1,0:T(8,128)(2,1)S(1)}, bf16[1,128,768]{2,1,0:T(8,128)(2,1)}, u32[]{:S(2)}) copy-start(bf16[1,128,768]{2,1,0:T(8,128)(2,1)} %param.8) | copy-start | bytes 589828
  0.7 38.3 %copy-start.5 = (bf16[1,128,256]{2,1,0:T(8,128)(2,1)S(1)}, bf16[1,128,256]{2,1,0:T(8,128)(2,1)}, u32[]{:S(2)}) copy-start(bf16[1,128,256]{2,1,0:T(8,128)(2,1)} %param.11) | copy-start | bytes 196612
  0.7 38.3 %copy-start.4 = (bf16[1,128,768]{2,1,0:T(8,128)(2,1)S(1)}, bf16[1,128,768]{2,1,0:T(8,128)(2,1)}, u32[]{:S(2)}) copy-start(bf16[1,128,768]{2,1,0:T(8,128)(2,1)} %param.15) | copy-start | bytes 589828
  0.7 38.3 %copy-start = (bf16[768,768]{1,0:T(8,128)(2,1)S(1)}, bf16[768,768]{1,0:T(8,128)(2,1)}, u32[]{:S(2)}) copy-start(bf16[768,768]{1,0:T(8,128)(2,1)} %weight_ref.3) | copy-start | bytes 3538948
  41.2 4.3 %collective-permute-start = (bf16[128,1152]{1,0:T(8,128)(2,1)S(1)}, bf16[128,1152]{1,0:T(8,128)(2,1)S(1)}, u32[]{:S(2)}, u32[]{:S(2)}) collective-permute-start(bf16[128,1152]{1,0:T(8,128)(2,1)S(1)} %get-tuple-element.21), channel_id=1, source_target_pairs={{0,1},{1,0},{2,3},{3,2},{4,5},{5,4},{6,7},{7,6},{8,9},{9,8},{10,11... | collective-permute-start | bytes 884744 | tf_op jit(solution)/shard_map/ppermute | solution.py:303
  45.5 19.7 %copy-start.1 = (bf16[256,1536]{1,0:T(8,128)(2,1)S(1)}, bf16[256,1536]{1,0:T(8,128)(2,1)}, u32[]{:S(2)}) copy-start(bf16[256,1536]{1,0:T(8,128)(2,1)} %history_in.3) | copy-start | bytes 2359300
  45.5 19.7 %copy-start.2 = (bf16[512,384]{1,0:T(8,128)(2,1)S(1)}, bf16[512,384]{1,0:T(8,128)(2,1)}, u32[]{:S(2)}) copy-start(bf16[512,384]{1,0:T(8,128)(2,1)} %get-tuple-element.24.pick_in.pick_ref) | copy-start | bytes 1179652
  61.7 10.5 %all-to-all-start.3 = ((bf16[4,16,1152]{2,1,0:T(8,128)(2,1)}), bf16[4,16,1152]{2,1,0:T(8,128)(2,1)S(1)}, u32[]{:S(2)}, u32[]{:S(2)}) async-start(bf16[4,16,1152]{2,1,0:T(8,128)(2,1)} %shard_map.108), calls=%async_computation.3 | async-start | bytes 294912 | tf_op jit(solution)/shard_map/all_to_all | solution.py:229
  72.2 33.3 %all-to-all-start.4 = ((bf16[32,16,1536]{2,1,0:T(8,128)(2,1)}), bf16[32,16,1536]{2,1,0:T(8,128)(2,1)S(1)}, u32[]{:S(2)}, u32[]{:S(2)}) async-start(bf16[32,16,1536]{2,1,0:T(8,128)(2,1)} %get-tuple-element.27), calls=%async_computation.4 | async-start | bytes 3145728 | tf_op jit(solution)/shard_map/all_to_all | solution.py:229
  78.0 23.1 %collective-permute-start.1 = (bf16[16,1152]{1,0:T(8,128)(2,1)S(1)}, bf16[16,1152]{1,0:T(8,128)(2,1)S(1)}, u32[]{:S(2)}, u32[]{:S(2)}) collective-permute-start(bf16[16,1152]{1,0:T(8,128)(2,1)S(1)} %shard_map.110.a_ref), channel_id=1, source_target_pairs={{0,128},{32,160},{64,192},{96,224},{128,256},{160,288},{192,320},{... | collective-permute-start | bytes 110600 | tf_op jit(solution)/shard_map/ppermute | solution.py:236
  87.0 14.1 %collective-permute-start.2 = (bf16[16,1152]{1,0:T(8,128)(2,1)S(1)}, bf16[16,1152]{1,0:T(8,128)(2,1)S(1)}, u32[]{:S(2)}, u32[]{:S(2)}) collective-permute-start(bf16[16,1152]{1,0:T(8,128)(2,1)S(1)} %shard_map.110.a_ref), channel_id=1, source_target_pairs={{0,384},{32,416},{64,448},{96,480},{128,0},{160,32},{192,64},{224,... | collective-permute-start | bytes 110600 | tf_op jit(solution)/shard_map/ppermute | solution.py:236
  90.2 14.6 %collective-permute-start.3 = (bf16[16,1152]{1,0:T(8,128)(2,1)S(1)}, bf16[16,1152]{1,0:T(8,128)(2,1)S(1)}, u32[]{:S(2)}, u32[]{:S(2)}) collective-permute-start(bf16[16,1152]{1,0:T(8,128)(2,1)S(1)} %shard_map.110.a_ref), channel_id=1, source_target_pairs={{0,256},{32,288},{64,320},{96,352},{128,384},{160,416},{192,448},{... | collective-permute-start | bytes 110600 | tf_op jit(solution)/shard_map/ppermute | solution.py:236

commit v4 on v3

--- a/solution.py
+++ b/solution.py
@@ -62,41 +62,51 @@
     ids_ref[...] = ids.astype(jnp.int32).reshape(ids_ref.shape)
 
 
-def gather_kernel(ids_ref, feats_in, history_in, taken_ref, pick_out, feats, history, pick, sems):
-    node_rows, width = feats.shape
-    table_rows = history.shape[0]
+def gather_kernel(ids_ref, table_ref, taken_ref, pick):
+    table_rows, width = table_ref.shape
     peers = ids_ref.shape[0]
-    load_feats = pltpu.make_async_copy(feats_in, feats, sems.at[0])
-    load_history = pltpu.make_async_copy(history_in.at[:, :width], history, sems.at[1])
-    load_feats.start()
-    load_history.start()
     ids = ids_ref[...].reshape(peers, LANES).astype(F32)
     ids = jnp.concatenate([ids, jnp.zeros((LANES - peers, LANES), F32)], axis=0)
     by_place = ids.T.astype(jnp.int32)
-    columns = lax.broadcasted_iota(jnp.int32, (CAP, node_rows + table_rows), 1)
+    columns = lax.broadcasted_iota(jnp.int32, (CAP, table_rows), 1)
     for g in range(peers):
         chosen = columns == by_place[:CAP, g : g + 1]
         pick[g * CAP : (g + 1) * CAP, :] = jnp.where(chosen, 1.0, 0.0).astype(BF16)
-    store = pltpu.make_async_copy(pick, pick_out, sems.at[2])
-    store.start()
-    load_feats.wait()
-    load_history.wait()
     part = peers // 4
     for start in range(0, peers, part):
-        near = pick[start * CAP : (start + part) * CAP, :node_rows]
-        far = pick[start * CAP : (start + part) * CAP, node_rows:]
-        emb = dot(near, feats[...]) + dot(far, history[...])
+        emb = dot(pick[start * CAP : (start + part) * CAP, :], table_ref[...])
         taken_ref[start : start + part] = emb.astype(BF16).reshape(part, CAP, width)
-    store.wait()
+
+
+def coef_kernel(
+    peers, node_rows, tile_in, owner_in, row_in, edge_in, all_ref, inside_ref, tile_ref, owner_ref,
+    row_ref, edge_ref, sems
+):
+    copies = [
+        pltpu.make_async_copy(tile_in, tile_ref, sems.at[0]),
+        pltpu.make_async_copy(owner_in, owner_ref, sems.at[1]),
+        pltpu.make_async_copy(row_in, row_ref, sems.at[2]),
+        pltpu.make_async_copy(edge_in, edge_ref, sems.at[3]),
+    ]
+    for copy in copies:
+        copy.start()
+    for copy in copies:
+        copy.wait()
+    first = tile_ref[0, 0]
+    owners = in_edge_order(first, owner_ref[...])
+    rows = in_edge_order(first, row_ref[...])
+    _, place = slot_places(owners, peers)
+    target = owners * CAP + place
+    at = lax.broadcasted_iota(jnp.int32, (peers * CAP, target.shape[1]), 0) == target
+    moved = jnp.where(at, 1.0, 0.0)
+    all_ref[...] = dot(edge_ref[...], moved.astype(BF16), ROWS_T).astype(BF16)
+    kept = jnp.where(rows < node_rows, moved, 0.0).astype(BF16)
+    inside_ref[...] = dot(edge_ref[...], kept, ROWS_T).astype(BF16)
 
 
 def forward_kernel(
-    peers,
-    tile_ref,
-    owner_ref,
-    row_ref,
-    edge_ref,
     pulled_ref,
+    all_ref,
     feats_ref,
     weight_ref,
     grad_ref,
@@ -104,21 +114,11 @@
     pre_ref,
     own_ref,
     away_ref,
-    all_ref,
-    inside_ref,
 ):
-    node_rows, width = feats_ref.shape
+    width = feats_ref.shape[1]
     half = width // 2
-    first = tile_ref[0, 0]
-    owners = in_edge_order(first, owner_ref[...])
-    rows = in_edge_order(first, row_ref[...])
-    _, place = slot_places(owners, peers)
-    target = owners * CAP + place
-    at = lax.broadcasted_iota(jnp.int32, (peers * CAP, target.shape[1]), 0) == target
-    moved = jnp.where(at, 1.0, 0.0)
-    coef = dot(edge_ref[...], moved.astype(BF16), ROWS_T).astype(BF16)
-    pulled = pulled_ref[...].reshape(peers * CAP, width)
-    mixed = (feats_ref[...].astype(F32) + dot(coef, pulled)).astype(BF16)
+    pulled = pulled_ref[...].reshape(-1, width)
+    mixed = (feats_ref[...].astype(F32) + dot(all_ref[...], pulled)).astype(BF16)
     pre = dot(mixed, weight_ref[...])
     gate = jax.nn.sigmoid(pre)
     grad_pre = (grad_ref[...].astype(F32) * gate * (1.0 + pre * (1.0 - gate))).astype(BF16)
@@ -130,9 +130,6 @@
     away_ref[:, width:] = jnp.where(second_core, left, right)
     pre_ref[...] = grad_pre
     out_ref[...] = (pre * gate).astype(BF16)
-    all_ref[...] = coef
-    kept = jnp.where(rows < node_rows, moved, 0.0).astype(BF16)
-    inside_ref[...] = dot(edge_ref[...], kept, ROWS_T).astype(BF16)
 
 
 def term_kernel(peers, width, own_ref, away_ref, term_ref):
@@ -206,7 +203,7 @@
     grad_ref[...] = total.astype(BF16)
 
 
-def call(kernel, out_shape, *args, smem=(), hbm=(), hbm_out=(), scratch=(), vmem=32):
+def call(kernel, out_shape, *args, smem=(), hbm=(), hbm_out=(), scratch=(), vmem=32, cost=None):
     spaces = [
         pltpu.SMEM if i in smem else pltpu.HBM if i in hbm else pltpu.VMEM
         for i in range(len(args))
@@ -221,6 +218,7 @@
         out_specs=[pl.BlockSpec(memory_space=space) for space in out_spaces],
         scratch_shapes=list(scratch),
         compiler_params=pltpu.CompilerParams(vmem_limit_bytes=vmem << 20),
+        cost_estimate=cost,
     )(*args)
     return result[0] if single else result
 
@@ -262,43 +260,45 @@
         ),
     )
     received = swap(ids)
+    coef, coef_inside = call(
+        functools.partial(coef_kernel, peers, node_rows),
+        [shape((node_rows, peers * CAP), BF16)] * 2,
+        tile_map,
+        owners,
+        nbr_row,
+        edge_coef[0],
+        hbm=(0, 1, 2, 3),
+        vmem=60,
+        scratch=(
+            pltpu.SMEM(tile_map.shape, jnp.int32),
+            pltpu.VMEM(owners.shape, jnp.int32),
+            pltpu.VMEM(nbr_row.shape, jnp.int32),
+            pltpu.VMEM(edge_coef.shape[1:], BF16),
+            pltpu.SemaphoreType.DMA((4,)),
+        ),
+    )
     table = node_rows + table_rows
+    received, coef, coef_inside = lax.optimization_barrier((received, coef, coef_inside))
     taken, pick = call(
         gather_kernel,
         [shape((peers, CAP, width), BF16), shape((peers * CAP, table), BF16)],
         received,
-        feats[0],
-        history,
-        hbm=(1, 2),
-        hbm_out=(1,),
-        vmem=60,
-        scratch=(
-            pltpu.VMEM((node_rows, width), BF16),
-            pltpu.VMEM((table_rows, width), BF16),
-            pltpu.VMEM((peers * CAP, table), BF16),
-            pltpu.SemaphoreType.DMA((3,)),
-        ),
+        jnp.concatenate([feats[0], history[:, :width]], axis=0),
     )
     pulled = swap(taken)
-    out_rows, grad_pre, own, away, coef, coef_inside = call(
-        functools.partial(forward_kernel, peers),
+    out_rows, grad_pre, own, away = call(
+        forward_kernel,
         [
             shape((node_rows, width), BF16),
             shape((node_rows, width), BF16),
             shape((node_rows, width + width // 2), BF16),
             shape((node_rows, width + width // 2), BF16),
-            shape((node_rows, peers * CAP), BF16),
-            shape((node_rows, peers * CAP), BF16),
         ],
-        tile_map,
-        owners,
-        nbr_row,
-        edge_coef[0],
         pulled,
+        coef,
         feats[0],
         weight,
         grad_out[0],
-        smem=(0,),
     )
     away = lax.ppermute(away, "hist", [(i, i ^ 1) for i in range(peers)])
     terms = call(
@@ -331,7 +331,7 @@
     sent, term = lax.optimization_barrier((sent, term))
     back = swap(sent)
     term = call(add_kernel, shape(term.shape[1:], BF16), term)
-    far = [shift(term, "batch", by) for by in (4, -4, 8)]
+    far = [shift(term, "batch", by) for by in (8, 4, -4)]
     weight_share = call(share_kernel, shape((share, width), F32), term, *far)
     grad_rows = call(
         final_kernel, shape((node_rows, width), BF16), back, pick, coef, grad_mixed

time: 107 us -> 106 us (level)
  blocking collectives: 48.2 us -> 33.2 us
  starting transfers between devices: 35.4 us -> 45.4 us
  waiting for transfers between devices: 9.2 us -> 12 us
  Pallas kernels: 12.9 us -> 11.4 us
    all_to_all x3 -> x2, blocking collectives: 48.2 us -> 33.2 us  [swap(): lax.all_to_all(values, axis, split_axis=0, concat_axis=0, tiled=True, axi...]
    all_to_all x2 -> x3, starting transfers between devices: 9.27 us -> 19.2 us  [swap(): lax.all_to_all(values, axis, split_axis=0, concat_axis=0, tiled=True, axi...]
    ppermute x3, waiting for transfers between devices: 3.72 us -> 5.3 us  [shift(): lax.ppermute(values, axis, [(i, (i + by) % count) for i in range(count)])]
    pallas_call x9 -> x10, Pallas kernels: 12.9 us -> 11.4 us  [call(): pl.pallas_call(kernel, out_shape=out_shape, in_specs=[pl.BlockSpec(memory...]
    all_to_all x2 -> x3, waiting for transfers between devices: 4.29 us -> 5.5 us  [swap(): lax.all_to_all(values, axis, split_axis=0, concat_axis=0, tiled=True, axi...]
  transfers between devices with their start and end apart: 6 -> 7, of which waited for: 3 -> 5; matrix products, arithmetic and copies ran while one was open for 0% -> 2% of each run, Pallas kernels for 3% -> 5%
where the time goes in v4:
time: 106 us; the launch traced here: 105 us
  starting transfers between devices  45.4 us (43%)
  blocking collectives  33.2 us (31%)
  waiting for transfers between devices  12 us (11%)
  Pallas kernels  11.4 us (11%)
  local copies, waits for them, and re-layouts  1.06 us (1%)
    all_to_all x2, blocking collectives, swap(): lax.all_to_all(values, axis, split_axis=0, concat_axis=0, tiled=True, axi...  33.2 us
    ppermute x3, starting transfers between devices, shift(): lax.ppermute(values, axis, [(i, (i + by) % count) for i in range(count)])  23.2 us
    all_to_all x3, starting transfers between devices, swap(): lax.all_to_all(values, axis, split_axis=0, concat_axis=0, tiled=True, axi...  19.2 us
    pallas_call x10, Pallas kernels, call(): pl.pallas_call(kernel, out_shape=out_shape, in_specs=[pl.BlockSpec(memory...  11.4 us
    all_to_all x3, waiting for transfers between devices, swap(): lax.all_to_all(values, axis, split_axis=0, concat_axis=0, tiled=True, axi...  5.5 us
    ppermute x3, waiting for transfers between devices, shift(): lax.ppermute(values, axis, [(i, (i + by) % count) for i in range(count)])  5.3 us
    ppermute x1, starting transfers between devices, body(): away = lax.ppermute(away, 'hist', [(i, i ^ 1) for i in range(peers)])  3.1 us
  transfers between devices with their start and end apart: 7, of which 5 were waited for; matrix products, arithmetic and copies ran while one was open for 2% of the time, Pallas kernels for 5%

profile of v4, /device:TPU:6, one launch (start us, length us, event | category | flops | bytes accessed | tf_op | source)
XLA Modules:
  0.0 104.9 jit_solution(17915178435576850211)
XLA Ops:
  0.6 1.7 %shard_map.103 = s32[32,1,128]{2,1,0:T(1,128)} custom-call(s32[1,2]{1,0:T(1,128)} %tile_in.3, s32[1,256]{1,0:T(1,128)} %bitcast.11, s32[1,256]{1,0:T(1,128)} %row_in.3), custom_call_target="tpu_custom_call" | custom-call | tf_op jit(solution)/shard_map/pallas_call | solution.py:214
  2.3 9.4 %all-to-all-start = ((s32[32,1,128]{2,1,0:T(1,128)}), s32[32,1,128]{2,1,0:T(1,128)S(1)}, u32[]{:S(2)}, u32[]{:S(2)}) async-start(s32[32,1,128]{2,1,0:T(1,128)} %shard_map.103), calls=%async_computation | async-start | bytes 32768 | tf_op jit(solution)/shard_map/all_to_all | solution.py:227
  11.7 1.0 slice.3
  12.7 1.0 pad_maximum_fusion.table_ref
  13.7 2.2 %shard_map.104 = (bf16[128,512]{1,0:T(8,128)(2,1)}, bf16[128,512]{1,0:T(8,128)(2,1)}) custom-call(s32[1,2]{1,0:T(1,128)} %tile_in.3, s32[1,256]{1,0:T(1,128)} %bitcast.12, s32[1,256]{1,0:T(1,128)} %row_in.3, bf16[128,256]{1,0:T(8,128)(2,1)} %bitcast.10), custom_call_target="tpu_custom_call" | custom-call | tf_op jit(solution)/shard_map/pallas_call | solution.py:214
  15.9 1.3 %all-to-all-done.ids_ref = s32[32,1,128]{2,1,0:T(1,128)S(1)} async-done(((s32[32,1,128]{2,1,0:T(1,128)}), s32[32,1,128]{2,1,0:T(1,128)S(1)}, u32[]{:S(2)}, u32[]{:S(2)}) %all-to-all-start) | async-done | bytes 16416 | tf_op jit(solution)/shard_map/all_to_all | solution.py:227
  17.2 0.7 shard_map.105
  17.9 18.0 %all_to_all.25.pulled_ref = bf16[32,16,768]{2,1,0:T(8,128)(2,1)S(1)} all-to-all(bf16[32,16,768]{2,1,0:T(8,128)(2,1)S(1)} %get-tuple-element.23), channel_id=1, replica_groups=mesh['batch'=16,'hist'=32] {'hist'}, dimensions={0} | all-to-all | bytes 1572864 | tf_op jit(solution)/shard_map/all_to_all | solution.py:227
  35.9 1.3 %shard_map.106 = (bf16[128,768]{1,0:T(8,128)(2,1)}, bf16[128,768]{1,0:T(8,128)(2,1)S(1)}, bf16[128,1152]{1,0:T(8,128)(2,1)S(1)}, bf16[128,1152]{1,0:T(8,128)(2,1)S(1)}) custom-call(bf16[32,16,768]{2,1,0:T(8,128)(2,1)S(1)} %all_to_all.25.pulled_ref, bf16[128,512]{1,0:T(8,128)(2,1)S(1)} %copy-done.3, bf16[128,768]{1,0:T(8,128)(2,1)S(1)} %bitcast.7, ...), custom_call_target="tpu_custom_call" | custom-call | tf_op jit(solution)/shard_map/pallas_call | solution.py:214
  37.2 3.1 %collective-permute-start = (bf16[128,1152]{1,0:T(8,128)(2,1)S(1)}, bf16[128,1152]{1,0:T(8,128)(2,1)S(1)}, u32[]{:S(2)}, u32[]{:S(2)}) collective-permute-start(bf16[128,1152]{1,0:T(8,128)(2,1)S(1)} %get-tuple-element.28), channel_id=1, source_target_pairs={{0,1},{1,0},{2,3},{3,2},{4,5},{5,4},{6,7},{7,6},{8,9},{9,8},{10,11... | collective-permute-start | bytes 884744 | tf_op jit(solution)/shard_map/ppermute | solution.py:303
  40.3 1.2 %collective-permute-done.away_ref = bf16[128,1152]{1,0:T(8,128)(2,1)S(1)} collective-permute-done((bf16[128,1152]{1,0:T(8,128)(2,1)S(1)}, bf16[128,1152]{1,0:T(8,128)(2,1)S(1)}, u32[]{:S(2)}, u32[]{:S(2)}) %collective-permute-start) | collective-permute-done | bytes 294944 | tf_op jit(solution)/shard_map/ppermute | solution.py:303
  41.9 15.2 %all_to_all.26.terms_ref = bf16[32,8,1152]{2,1,0:T(8,128)(2,1)S(1)} all-to-all(bf16[32,8,1152]{2,1,0:T(8,128)(2,1)S(1)} %shard_map.107), channel_id=1, replica_groups=mesh['batch'=16,'hist'=32] {'hist'}, dimensions={0} | all-to-all | bytes 1179648 | tf_op jit(solution)/shard_map/all_to_all | solution.py:227
  57.1 0.7 shard_map.109
  57.9 4.0 %all-to-all-start.3 = ((bf16[4,16,1152]{2,1,0:T(8,128)(2,1)}), bf16[4,16,1152]{2,1,0:T(8,128)(2,1)S(1)}, u32[]{:S(2)}, u32[]{:S(2)}) async-start(bf16[4,16,1152]{2,1,0:T(8,128)(2,1)} %shard_map.109), calls=%async_computation.3 | async-start | bytes 294912 | tf_op jit(solution)/shard_map/all_to_all | solution.py:227
  61.9 2.7 %shard_map.108 = (bf16[32,16,1536]{2,1,0:T(8,128)(2,1)}, bf16[128,768]{1,0:T(8,128)(2,1)S(1)}) custom-call(bf16[128,768]{1,0:T(8,128)(2,1)S(1)} %get-tuple-element.29.pre_ref, bf16[768,768]{1,0:T(8,128)(2,1)S(1)} %copy-done, bf16[128,512]{1,0:T(8,128)(2,1)S(1)} %copy-done.5, bf16[512,384]{1,0:T(8,128)(2,1)S(1)} %get-tuple-element.31.pick_in.pick_ref, ...), custom_call_target="tpu_custom_call" | custom-call | tf_op jit(solution)/shard_map/pallas_call | solution.py:214
  64.6 4.2 %all-to-all-done.3.near_ref = bf16[4,16,1152]{2,1,0:T(8,128)(2,1)S(1)} async-done(((bf16[4,16,1152]{2,1,0:T(8,128)(2,1)}), bf16[4,16,1152]{2,1,0:T(8,128)(2,1)S(1)}, u32[]{:S(2)}, u32[]{:S(2)}) %all-to-all-start.3) | async-done | bytes 147488 | tf_op jit(solution)/shard_map/all_to_all | solution.py:227
  68.8 5.8 %all-to-all-start.4 = ((bf16[32,16,1536]{2,1,0:T(8,128)(2,1)}), bf16[32,16,1536]{2,1,0:T(8,128)(2,1)S(1)}, u32[]{:S(2)}, u32[]{:S(2)}) async-start(bf16[32,16,1536]{2,1,0:T(8,128)(2,1)} %get-tuple-element.34), calls=%async_computation.4 | async-start | bytes 3145728 | tf_op jit(solution)/shard_map/all_to_all | solution.py:227
  74.6 13.4 %collective-permute-start.1 = (bf16[16,1152]{1,0:T(8,128)(2,1)S(1)}, bf16[16,1152]{1,0:T(8,128)(2,1)S(1)}, u32[]{:S(2)}, u32[]{:S(2)}) collective-permute-start(bf16[16,1152]{1,0:T(8,128)(2,1)S(1)} %shard_map.111.a_ref), channel_id=1, source_target_pairs={{0,256},{32,288},{64,320},{96,352},{128,384},{160,416},{192,448},{... | collective-permute-start | bytes 110600 | tf_op jit(solution)/shard_map/ppermute | solution.py:234
  88.1 4.3 %collective-permute-start.2 = (bf16[16,1152]{1,0:T(8,128)(2,1)S(1)}, bf16[16,1152]{1,0:T(8,128)(2,1)S(1)}, u32[]{:S(2)}, u32[]{:S(2)}) collective-permute-start(bf16[16,1152]{1,0:T(8,128)(2,1)S(1)} %shard_map.111.a_ref), channel_id=1, source_target_pairs={{0,128},{32,160},{64,192},{96,224},{128,256},{160,288},{192,320},{... | collective-permute-start | bytes 110600 | tf_op jit(solution)/shard_map/ppermute | solution.py:234
  92.4 5.5 %collective-permute-start.3 = (bf16[16,1152]{1,0:T(8,128)(2,1)S(1)}, bf16[16,1152]{1,0:T(8,128)(2,1)S(1)}, u32[]{:S(2)}, u32[]{:S(2)}) collective-permute-start(bf16[16,1152]{1,0:T(8,128)(2,1)S(1)} %shard_map.111.a_ref), channel_id=1, source_target_pairs={{0,384},{32,416},{64,448},{96,480},{128,0},{160,32},{192,64},{224,... | collective-permute-start | bytes 110600 | tf_op jit(solution)/shard_map/ppermute | solution.py:234
  97.8 0.6 collective-permute-done.2.c_ref
  98.4 4.7 %collective-permute-done.3.d_ref = bf16[16,1152]{1,0:T(8,128)(2,1)S(1)} collective-permute-done((bf16[16,1152]{1,0:T(8,128)(2,1)S(1)}, bf16[16,1152]{1,0:T(8,128)(2,1)S(1)}, u32[]{:S(2)}, u32[]{:S(2)}) %collective-permute-start.3) | collective-permute-done | bytes 36896 | tf_op jit(solution)/shard_map/ppermute | solution.py:234
  103.1 0.7 shard_map.112
  103.8 1.1 %shard_map.110 = bf16[128,768]{1,0:T(8,128)(2,1)} custom-call(bf16[32,16,1536]{2,1,0:T(8,128)(2,1)S(1)} %all-to-all-done.4.back_ref, bf16[512,384]{1,0:T(8,128)(2,1)S(1)} %get-tuple-element.31.pick_in.pick_ref, bf16[128,512]{1,0:T(8,128)(2,1)S(1)} %copy-done.3, bf16[128,768]{1,0:T(8,128)(2,1)S(1)} %get-tuple-element.35.mixed_ref), custom_call_target="tpu_custom_call" | custom-call | tf_op jit(solution)/shard_map/pallas_call | solution.py:214
  (16 shorter events, 0.5 us)
Async XLA Ops:
  2.3 14.9 %all-to-all-start = ((s32[32,1,128]{2,1,0:T(1,128)}), s32[32,1,128]{2,1,0:T(1,128)S(1)}, u32[]{:S(2)}, u32[]{:S(2)}) async-start(s32[32,1,128]{2,1,0:T(1,128)} %shard_map.103), calls=%async_computation | async-start | bytes 32768 | tf_op jit(solution)/shard_map/all_to_all | solution.py:227
  13.7 22.2 %copy-start = (bf16[768,768]{1,0:T(8,128)(2,1)S(1)}, bf16[768,768]{1,0:T(8,128)(2,1)}, u32[]{:S(2)}) copy-start(bf16[768,768]{1,0:T(8,128)(2,1)} %weight_ref.3) | copy-start | bytes 3538948
  13.7 22.2 %copy-start.2 = (bf16[1,128,768]{2,1,0:T(8,128)(2,1)S(1)}, bf16[1,128,768]{2,1,0:T(8,128)(2,1)}, u32[]{:S(2)}) copy-start(bf16[1,128,768]{2,1,0:T(8,128)(2,1)} %param.8) | copy-start | bytes 589828
  13.7 22.2 %copy-start.4 = (bf16[1,128,768]{2,1,0:T(8,128)(2,1)S(1)}, bf16[1,128,768]{2,1,0:T(8,128)(2,1)}, u32[]{:S(2)}) copy-start(bf16[1,128,768]{2,1,0:T(8,128)(2,1)} %param.15) | copy-start | bytes 589828
  15.9 20.0 %copy-start.3 = (bf16[128,512]{1,0:T(8,128)(2,1)S(1)}, bf16[128,512]{1,0:T(8,128)(2,1)}, u32[]{:S(2)}) copy-start(bf16[128,512]{1,0:T(8,128)(2,1)} %get-tuple-element.24.all_ref) | copy-start | bytes 393220
  37.2 4.3 %collective-permute-start = (bf16[128,1152]{1,0:T(8,128)(2,1)S(1)}, bf16[128,1152]{1,0:T(8,128)(2,1)S(1)}, u32[]{:S(2)}, u32[]{:S(2)}) collective-permute-start(bf16[128,1152]{1,0:T(8,128)(2,1)S(1)} %get-tuple-element.28), channel_id=1, source_target_pairs={{0,1},{1,0},{2,3},{3,2},{4,5},{5,4},{6,7},{7,6},{8,9},{9,8},{10,11... | collective-permute-start | bytes 884744 | tf_op jit(solution)/shard_map/ppermute | solution.py:303
  41.9 20.0 %copy-start.1 = (bf16[256,1536]{1,0:T(8,128)(2,1)S(1)}, bf16[256,1536]{1,0:T(8,128)(2,1)}, u32[]{:S(2)}) copy-start(bf16[256,1536]{1,0:T(8,128)(2,1)} %history_in.1) | copy-start | bytes 2359300
  41.9 20.0 %copy-start.5 = (bf16[128,512]{1,0:T(8,128)(2,1)S(1)}, bf16[128,512]{1,0:T(8,128)(2,1)}, u32[]{:S(2)}) copy-start(bf16[128,512]{1,0:T(8,128)(2,1)} %get-tuple-element.30.inside_ref) | copy-start | bytes 393220
  57.9 10.9 %all-to-all-start.3 = ((bf16[4,16,1152]{2,1,0:T(8,128)(2,1)}), bf16[4,16,1152]{2,1,0:T(8,128)(2,1)S(1)}, u32[]{:S(2)}, u32[]{:S(2)}) async-start(bf16[4,16,1152]{2,1,0:T(8,128)(2,1)} %shard_map.109), calls=%async_computation.3 | async-start | bytes 294912 | tf_op jit(solution)/shard_map/all_to_all | solution.py:227
  68.8 34.9 %all-to-all-start.4 = ((bf16[32,16,1536]{2,1,0:T(8,128)(2,1)}), bf16[32,16,1536]{2,1,0:T(8,128)(2,1)S(1)}, u32[]{:S(2)}, u32[]{:S(2)}) async-start(bf16[32,16,1536]{2,1,0:T(8,128)(2,1)} %get-tuple-element.34), calls=%async_computation.4 | async-start | bytes 3145728 | tf_op jit(solution)/shard_map/all_to_all | solution.py:227
  74.6 23.2 %collective-permute-start.1 = (bf16[16,1152]{1,0:T(8,128)(2,1)S(1)}, bf16[16,1152]{1,0:T(8,128)(2,1)S(1)}, u32[]{:S(2)}, u32[]{:S(2)}) collective-permute-start(bf16[16,1152]{1,0:T(8,128)(2,1)S(1)} %shard_map.111.a_ref), channel_id=1, source_target_pairs={{0,256},{32,288},{64,320},{96,352},{128,384},{160,416},{192,448},{... | collective-permute-start | bytes 110600 | tf_op jit(solution)/shard_map/ppermute | solution.py:234
  88.1 10.4 %collective-permute-start.2 = (bf16[16,1152]{1,0:T(8,128)(2,1)S(1)}, bf16[16,1152]{1,0:T(8,128)(2,1)S(1)}, u32[]{:S(2)}, u32[]{:S(2)}) collective-permute-start(bf16[16,1152]{1,0:T(8,128)(2,1)S(1)} %shard_map.111.a_ref), channel_id=1, source_target_pairs={{0,128},{32,160},{64,192},{96,224},{128,256},{160,288},{192,320},{... | collective-permute-start | bytes 110600 | tf_op jit(solution)/shard_map/ppermute | solution.py:234
  92.4 10.8 %collective-permute-start.3 = (bf16[16,1152]{1,0:T(8,128)(2,1)S(1)}, bf16[16,1152]{1,0:T(8,128)(2,1)S(1)}, u32[]{:S(2)}, u32[]{:S(2)}) collective-permute-start(bf16[16,1152]{1,0:T(8,128)(2,1)S(1)} %shard_map.111.a_ref), channel_id=1, source_target_pairs={{0,384},{32,416},{64,448},{96,480},{128,0},{160,32},{192,64},{224,... | collective-permute-start | bytes 110600 | tf_op jit(solution)/shard_map/ppermute | solution.py:234

commit v5 on v4

--- a/solution.py
+++ b/solution.py
@@ -179,9 +179,10 @@
     sum_ref[...] = jnp.sum(near_ref[...].astype(F32), axis=0).astype(BF16)
 
 
-def share_kernel(a_ref, b_ref, c_ref, d_ref, share_ref):
-    total = a_ref[...].astype(F32) + b_ref[...].astype(F32)
-    total = total + (c_ref[...].astype(F32) + d_ref[...].astype(F32))
+def final_kernel(
+    back_ref, pick_ref, all_ref, mixed_ref, far_ref, grad_ref, share_ref
+):
+    total = jnp.sum(far_ref[...].astype(F32), axis=0)
     share, width = share_ref.shape
     half = width // 2
     step = total.shape[0] // 2
@@ -190,17 +191,14 @@
             share_ref[i * step : (i + 1) * step, core * half : (core + 1) * half] = total[
                 core * step : (core + 1) * step, i * half : (i + 1) * half
             ]
-
-
-def final_kernel(back_ref, pick_ref, all_ref, mixed_ref, grad_ref):
     peers = back_ref.shape[0]
-    node_rows, width = mixed_ref.shape
+    node_rows = mixed_ref.shape[0]
     slots = back_ref[:, :, :width].reshape(peers * CAP, width)
     aux = back_ref[:, :, width:].reshape(peers * CAP, width)
     returned = dot(pick_ref[:, :node_rows], slots, COLS_T)
     compensation = dot(all_ref[...], aux)
-    total = mixed_ref[...].astype(F32) + returned + compensation
-    grad_ref[...] = total.astype(BF16)
+    grad = mixed_ref[...].astype(F32) + returned + compensation
+    grad_ref[...] = grad.astype(BF16)
 
 
 def call(kernel, out_shape, *args, smem=(), hbm=(), hbm_out=(), scratch=(), vmem=32, cost=None):
@@ -227,11 +225,6 @@
     return lax.all_to_all(
         values, axis, split_axis=0, concat_axis=0, tiled=True, axis_index_groups=groups
     )
-
-
-def shift(values, axis, by):
-    count = lax.axis_size(axis)
-    return lax.ppermute(values, axis, [(i, (i + by) % count) for i in range(count)])
 
 
 def body(feats, history, weight, edge_coef, tile_map, nbr_owner, nbr_row, grad_out):
@@ -331,10 +324,16 @@
     sent, term = lax.optimization_barrier((sent, term))
     back = swap(sent)
     term = call(add_kernel, shape(term.shape[1:], BF16), term)
-    far = [shift(term, "batch", by) for by in (8, 4, -4)]
-    weight_share = call(share_kernel, shape((share, width), F32), term, *far)
-    grad_rows = call(
-        final_kernel, shape((node_rows, width), BF16), back, pick, coef, grad_mixed
+    far = [[a + side * i for i in range(planes // side)] for a in range(side)]
+    term = lax.all_gather(term, "batch", axis=0, axis_index_groups=far)
+    grad_rows, weight_share = call(
+        final_kernel,
+        [shape((node_rows, width), BF16), shape((share, width), F32)],
+        back,
+        pick,
+        coef,
+        grad_mixed,
+        term,
     )
     return (out_rows[None], grad_rows[None], weight_share)
 

time: 106 us -> 101 us (0.953)
  blocking collectives: 33.2 us -> 57.7 us
  starting transfers between devices: 45.4 us -> 22.3 us
  waiting for transfers between devices: 12 us -> 6.7 us
    all_gather x0 -> x1, blocking collectives: none -> 24.4 us  [body(): term = lax.all_gather(term, 'batch', axis=0, axis_index_groups=far)]
    ppermute x3 -> x0, starting transfers between devices: 23.2 us -> none  [shift(): lax.ppermute(values, axis, [(i, (i + by) % count) for i in range(count)])]
    ppermute x3 -> x0, waiting for transfers between devices: 5.3 us -> none  [shift(): lax.ppermute(values, axis, [(i, (i + by) % count) for i in range(count)])]
    pallas_call x10 -> x9, Pallas kernels: 11.4 us -> 10.8 us  [call(): pl.pallas_call(kernel, out_shape=out_shape, in_specs=[pl.BlockSpec(memory...]
  transfers between devices with their start and end apart: 7 -> 4, of which waited for: 5 -> 3; matrix products, arithmetic and copies ran while one was open for 2% -> 2% of each run, Pallas kernels for 5% -> 5%
where the time goes in v5:
time: 101 us; the launch traced here: 100 us
  blocking collectives  57.7 us (57%)
  starting transfers between devices  22.3 us (22%)
  Pallas kernels  10.8 us (11%)
  waiting for transfers between devices  6.7 us (7%)
  local copies, waits for them, and re-layouts  1.06 us (1%)
    all_to_all x2, blocking collectives, swap(): lax.all_to_all(values, axis, split_axis=0, concat_axis=0, tiled=True, axi...  33.2 us
    all_gather x1, blocking collectives, body(): term = lax.all_gather(term, 'batch', axis=0, axis_index_groups=far)  24.4 us
    all_to_all x3, starting transfers between devices, swap(): lax.all_to_all(values, axis, split_axis=0, concat_axis=0, tiled=True, axi...  19.2 us
    pallas_call x9, Pallas kernels, call(): pl.pallas_call(kernel, out_shape=out_shape, in_specs=[pl.BlockSpec(memory...  10.8 us
    all_to_all x3, waiting for transfers between devices, swap(): lax.all_to_all(values, axis, split_axis=0, concat_axis=0, tiled=True, axi...  5.51 us
    ppermute x1, starting transfers between devices, body(): away = lax.ppermute(away, 'hist', [(i, i ^ 1) for i in range(peers)])  3.1 us
  transfers between devices with their start and end apart: 4, of which 3 were waited for; matrix products, arithmetic and copies ran while one was open for 2% of the time, Pallas kernels for 5%

profile of v5, /device:TPU:6, one launch (start us, length us, event | category | flops | bytes accessed | tf_op | source)
XLA Modules:
  0.0 100.2 jit_solution(11588687347871238820)
XLA Ops:
  0.6 1.7 %shard_map.103 = s32[32,1,128]{2,1,0:T(1,128)} custom-call(s32[1,2]{1,0:T(1,128)} %tile_in.3, s32[1,256]{1,0:T(1,128)} %bitcast.12, s32[1,256]{1,0:T(1,128)} %row_in.3), custom_call_target="tpu_custom_call" | custom-call | tf_op jit(solution)/shard_map/pallas_call | solution.py:212
  2.3 9.4 %all-to-all-start = ((s32[32,1,128]{2,1,0:T(1,128)}), s32[32,1,128]{2,1,0:T(1,128)S(1)}, u32[]{:S(2)}, u32[]{:S(2)}) async-start(s32[32,1,128]{2,1,0:T(1,128)} %shard_map.103), calls=%async_computation | async-start | bytes 32768 | tf_op jit(solution)/shard_map/all_to_all | solution.py:225
  11.7 1.0 %slice.3 = bf16[256,768]{1,0:T(8,128)(2,1)S(1)} slice(bf16[256,1536]{1,0:T(8,128)(2,1)} %history_in.1), slice={[0:256], [0:768]} | slice | bytes 786432 | tf_op jit(solution)/shard_map/slice | solution.py:279
  12.7 1.0 pad_maximum_fusion.table_ref
  13.7 0.0 copy-start
  13.7 0.0 copy-start.2
  13.7 2.2 %shard_map.104 = (bf16[128,512]{1,0:T(8,128)(2,1)}, bf16[128,512]{1,0:T(8,128)(2,1)}) custom-call(s32[1,2]{1,0:T(1,128)} %tile_in.3, s32[1,256]{1,0:T(1,128)} %bitcast.13, s32[1,256]{1,0:T(1,128)} %row_in.3, bf16[128,256]{1,0:T(8,128)(2,1)} %bitcast.11), custom_call_target="tpu_custom_call" | custom-call | tf_op jit(solution)/shard_map/pallas_call | solution.py:212
  15.9 0.0 copy-start.3
  15.9 1.3 %all-to-all-done.ids_ref = s32[32,1,128]{2,1,0:T(1,128)S(1)} async-done(((s32[32,1,128]{2,1,0:T(1,128)}), s32[32,1,128]{2,1,0:T(1,128)S(1)}, u32[]{:S(2)}, u32[]{:S(2)}) %all-to-all-start) | async-done | bytes 16416 | tf_op jit(solution)/shard_map/all_to_all | solution.py:225
  17.2 0.7 shard_map.105
  17.9 18.0 %all_to_all.25.pulled_ref = bf16[32,16,768]{2,1,0:T(8,128)(2,1)S(1)} all-to-all(bf16[32,16,768]{2,1,0:T(8,128)(2,1)S(1)} %get-tuple-element.25), channel_id=1, replica_groups=mesh['batch'=16,'hist'=32] {'hist'}, dimensions={0} | all-to-all | bytes 1572864 | tf_op jit(solution)/shard_map/all_to_all | solution.py:225
  35.9 1.3 %shard_map.106 = (bf16[128,768]{1,0:T(8,128)(2,1)}, bf16[128,768]{1,0:T(8,128)(2,1)S(1)}, bf16[128,1152]{1,0:T(8,128)(2,1)S(1)}, bf16[128,1152]{1,0:T(8,128)(2,1)S(1)}) custom-call(bf16[32,16,768]{2,1,0:T(8,128)(2,1)S(1)} %all_to_all.25.pulled_ref, bf16[128,512]{1,0:T(8,128)(2,1)S(1)} %copy-done.3, bf16[128,768]{1,0:T(8,128)(2,1)S(1)} %bitcast.8, ...), custom_call_target="tpu_custom_call" | custom-call | tf_op jit(solution)/shard_map/pallas_call | solution.py:212
  37.2 3.1 %collective-permute-start = (bf16[128,1152]{1,0:T(8,128)(2,1)S(1)}, bf16[128,1152]{1,0:T(8,128)(2,1)S(1)}, u32[]{:S(2)}, u32[]{:S(2)}) collective-permute-start(bf16[128,1152]{1,0:T(8,128)(2,1)S(1)} %get-tuple-element.30), channel_id=1, source_target_pairs={{0,1},{1,0},{2,3},{3,2},{4,5},{5,4},{6,7},{7,6},{8,9},{9,8},{10,11... | collective-permute-start | bytes 884744 | tf_op jit(solution)/shard_map/ppermute | solution.py:296
  40.3 1.2 %collective-permute-done.away_ref = bf16[128,1152]{1,0:T(8,128)(2,1)S(1)} collective-permute-done((bf16[128,1152]{1,0:T(8,128)(2,1)S(1)}, bf16[128,1152]{1,0:T(8,128)(2,1)S(1)}, u32[]{:S(2)}, u32[]{:S(2)}) %collective-permute-start) | collective-permute-done | bytes 294944 | tf_op jit(solution)/shard_map/ppermute | solution.py:296
  41.5 0.4 shard_map.107
  41.9 0.0 copy-start.1
  41.9 15.2 %all_to_all.26.terms_ref = bf16[32,8,1152]{2,1,0:T(8,128)(2,1)S(1)} all-to-all(bf16[32,8,1152]{2,1,0:T(8,128)(2,1)S(1)} %shard_map.107), channel_id=1, replica_groups=mesh['batch'=16,'hist'=32] {'hist'}, dimensions={0} | all-to-all | bytes 1179648 | tf_op jit(solution)/shard_map/all_to_all | solution.py:225
  57.1 0.7 shard_map.109
  57.9 4.0 %all-to-all-start.3 = ((bf16[4,16,1152]{2,1,0:T(8,128)(2,1)}), bf16[4,16,1152]{2,1,0:T(8,128)(2,1)S(1)}, u32[]{:S(2)}, u32[]{:S(2)}) async-start(bf16[4,16,1152]{2,1,0:T(8,128)(2,1)} %shard_map.109), calls=%async_computation.3 | async-start | bytes 294912 | tf_op jit(solution)/shard_map/all_to_all | solution.py:225
  61.9 2.7 %shard_map.108 = (bf16[32,16,1536]{2,1,0:T(8,128)(2,1)}, bf16[128,768]{1,0:T(8,128)(2,1)S(1)}) custom-call(bf16[128,768]{1,0:T(8,128)(2,1)S(1)} %get-tuple-element.31.pre_ref, bf16[768,768]{1,0:T(8,128)(2,1)S(1)} %copy-done, bf16[128,512]{1,0:T(8,128)(2,1)S(1)} %copy-done.5, bf16[512,384]{1,0:T(8,128)(2,1)S(1)} %get-tuple-element.33.pick_in.pick_ref, ...), custom_call_target="tpu_custom_call" | custom-call | tf_op jit(solution)/shard_map/pallas_call | solution.py:212
  64.6 4.2 %all-to-all-done.3.near_ref = bf16[4,16,1152]{2,1,0:T(8,128)(2,1)S(1)} async-done(((bf16[4,16,1152]{2,1,0:T(8,128)(2,1)}), bf16[4,16,1152]{2,1,0:T(8,128)(2,1)S(1)}, u32[]{:S(2)}, u32[]{:S(2)}) %all-to-all-start.3) | async-done | bytes 147488 | tf_op jit(solution)/shard_map/all_to_all | solution.py:225
  68.8 5.8 %all-to-all-start.4 = ((bf16[32,16,1536]{2,1,0:T(8,128)(2,1)}), bf16[32,16,1536]{2,1,0:T(8,128)(2,1)S(1)}, u32[]{:S(2)}, u32[]{:S(2)}) async-start(bf16[32,16,1536]{2,1,0:T(8,128)(2,1)} %get-tuple-element.36), calls=%async_computation.4 | async-start | bytes 3145728 | tf_op jit(solution)/shard_map/all_to_all | solution.py:225
  74.6 24.4 %all-gather = bf16[64,1152]{1,0:T(8,128)(2,1)S(1)} all-gather(bf16[16,1152]{1,0:T(8,128)(2,1)S(1)} %shard_map.110), channel_id=2, replica_groups={{0,128,256,384},{32,160,288,416},{64,192,320,448},{96,224,352,480},{1,1..., dimensions={0}, use_global_device_ids=true | all-gather | bytes 184320 | tf_op jit(solution)/shard_map/all_gather | solution.py:328
  99.1 1.1 %shard_map.111 = (bf16[128,768]{1,0:T(8,128)(2,1)}, f32[24,768]{1,0:T(8,128)}) custom-call(bf16[32,16,1536]{2,1,0:T(8,128)(2,1)S(1)} %all-to-all-done.4.back_ref, bf16[512,384]{1,0:T(8,128)(2,1)S(1)} %get-tuple-element.33.pick_in.pick_ref, bf16[128,512]{1,0:T(8,128)(2,1)S(1)} %copy-done.3, bf16[128,768]{1,0:T(8,128)(2,1)S(1)} %get-tuple-element.37.mixed_ref, ...), custom_call_target="tpu_custom_call" | custom-call | tf_op jit(solution)/shard_map/pallas_call | solution.py:212
  (10 shorter events, 0.0 us)
Async XLA Ops:
  2.3 14.9 %all-to-all-start = ((s32[32,1,128]{2,1,0:T(1,128)}), s32[32,1,128]{2,1,0:T(1,128)S(1)}, u32[]{:S(2)}, u32[]{:S(2)}) async-start(s32[32,1,128]{2,1,0:T(1,128)} %shard_map.103), calls=%async_computation | async-start | bytes 32768 | tf_op jit(solution)/shard_map/all_to_all | solution.py:225
  13.7 22.2 %copy-start = (bf16[768,768]{1,0:T(8,128)(2,1)S(1)}, bf16[768,768]{1,0:T(8,128)(2,1)}, u32[]{:S(2)}) copy-start(bf16[768,768]{1,0:T(8,128)(2,1)} %weight_ref.3) | copy-start | bytes 3538948
  13.7 22.2 %copy-start.2 = (bf16[1,128,768]{2,1,0:T(8,128)(2,1)S(1)}, bf16[1,128,768]{2,1,0:T(8,128)(2,1)}, u32[]{:S(2)}) copy-start(bf16[1,128,768]{2,1,0:T(8,128)(2,1)} %param.8) | copy-start | bytes 589828
  13.7 22.2 %copy-start.4 = (bf16[1,128,768]{2,1,0:T(8,128)(2,1)S(1)}, bf16[1,128,768]{2,1,0:T(8,128)(2,1)}, u32[]{:S(2)}) copy-start(bf16[1,128,768]{2,1,0:T(8,128)(2,1)} %param.15) | copy-start | bytes 589828
  15.9 20.0 %copy-start.3 = (bf16[128,512]{1,0:T(8,128)(2,1)S(1)}, bf16[128,512]{1,0:T(8,128)(2,1)}, u32[]{:S(2)}) copy-start(bf16[128,512]{1,0:T(8,128)(2,1)} %get-tuple-element.26.all_ref) | copy-start | bytes 393220
  37.2 4.3 %collective-permute-start = (bf16[128,1152]{1,0:T(8,128)(2,1)S(1)}, bf16[128,1152]{1,0:T(8,128)(2,1)S(1)}, u32[]{:S(2)}, u32[]{:S(2)}) collective-permute-start(bf16[128,1152]{1,0:T(8,128)(2,1)S(1)} %get-tuple-element.30), channel_id=1, source_target_pairs={{0,1},{1,0},{2,3},{3,2},{4,5},{5,4},{6,7},{7,6},{8,9},{9,8},{10,11... | collective-permute-start | bytes 884744 | tf_op jit(solution)/shard_map/ppermute | solution.py:296
  41.9 20.0 %copy-start.1 = (bf16[256,1536]{1,0:T(8,128)(2,1)S(1)}, bf16[256,1536]{1,0:T(8,128)(2,1)}, u32[]{:S(2)}) copy-start(bf16[256,1536]{1,0:T(8,128)(2,1)} %history_in.1) | copy-start | bytes 2359300
  41.9 20.0 %copy-start.5 = (bf16[128,512]{1,0:T(8,128)(2,1)S(1)}, bf16[128,512]{1,0:T(8,128)(2,1)}, u32[]{:S(2)}) copy-start(bf16[128,512]{1,0:T(8,128)(2,1)} %get-tuple-element.32.inside_ref) | copy-start | bytes 393220
  57.9 10.9 %all-to-all-start.3 = ((bf16[4,16,1152]{2,1,0:T(8,128)(2,1)}), bf16[4,16,1152]{2,1,0:T(8,128)(2,1)S(1)}, u32[]{:S(2)}, u32[]{:S(2)}) async-start(bf16[4,16,1152]{2,1,0:T(8,128)(2,1)} %shard_map.109), calls=%async_computation.3 | async-start | bytes 294912 | tf_op jit(solution)/shard_map/all_to_all | solution.py:225
  68.8 30.2 %all-to-all-start.4 = ((bf16[32,16,1536]{2,1,0:T(8,128)(2,1)}), bf16[32,16,1536]{2,1,0:T(8,128)(2,1)S(1)}, u32[]{:S(2)}, u32[]{:S(2)}) async-start(bf16[32,16,1536]{2,1,0:T(8,128)(2,1)} %get-tuple-element.36), calls=%async_computation.4 | async-start | bytes 3145728 | tf_op jit(solution)/shard_map/all_to_all | solution.py:225

commit v6 on v5

--- a/solution.py
+++ b/solution.py
@@ -25,15 +25,19 @@
     return jnp.where(first_tile == 0, values, swapped)
 
 
-def slot_places(owners, peers):
+def earlier_slots(slots):
+    earlier = (
+        lax.broadcasted_iota(jnp.int32, (slots, slots), 0)
+        < lax.broadcasted_iota(jnp.int32, (slots, slots), 1)
+    )
+    return jnp.where(earlier, 1.0, 0.0).astype(BF16)
+
+
+def slot_places(owners, peers, earlier):
     slots = owners.shape[1]
     named = lax.broadcasted_iota(jnp.int32, (peers, slots), 0) == owners
     named = jnp.where(named, 1.0, 0.0)
-    earlier = (
-        lax.broadcasted_iota(jnp.int32, (slots, slots), 0)
-        < lax.broadcasted_iota(jnp.int32, (slots, slots), 1)
-    )
-    rank = dot(named.astype(BF16), jnp.where(earlier, 1.0, 0.0).astype(BF16))
+    rank = dot(named.astype(BF16), earlier)
     return named, jnp.sum(named * rank, axis=0, keepdims=True).astype(jnp.int32)
 
 
@@ -45,13 +49,14 @@
     ]
     for copy in copies:
         copy.start()
+    earlier = earlier_slots(owner_ref.shape[1])
     for copy in copies:
         copy.wait()
     peers = ids_ref.shape[0]
     first = tile_ref[0, 0]
     owners = in_edge_order(first, owner_ref[...])
     rows = in_edge_order(first, row_ref[...])
-    named, place = slot_places(owners, peers)
+    named, place = slot_places(owners, peers, earlier)
     spot = lax.broadcasted_iota(jnp.int32, (LANES, rows.shape[1]), 0) == place
     spot = jnp.where(spot, 1.0, 0.0).astype(BF16)
     low = (rows % LANES).astype(F32)
@@ -90,12 +95,13 @@
     ]
     for copy in copies:
         copy.start()
+    earlier = earlier_slots(owner_ref.shape[1])
     for copy in copies:
         copy.wait()
     first = tile_ref[0, 0]
     owners = in_edge_order(first, owner_ref[...])
     rows = in_edge_order(first, row_ref[...])
-    _, place = slot_places(owners, peers)
+    _, place = slot_places(owners, peers, earlier)
     target = owners * CAP + place
     at = lax.broadcasted_iota(jnp.int32, (peers * CAP, target.shape[1]), 0) == target
     moved = jnp.where(at, 1.0, 0.0)
@@ -111,30 +117,26 @@
     weight_ref,
     grad_ref,
     out_ref,
-    pre_ref,
-    own_ref,
-    away_ref,
+    pair_ref,
 ):
     width = feats_ref.shape[1]
-    half = width // 2
     pulled = pulled_ref[...].reshape(-1, width)
     mixed = (feats_ref[...].astype(F32) + dot(all_ref[...], pulled)).astype(BF16)
     pre = dot(mixed, weight_ref[...])
     gate = jax.nn.sigmoid(pre)
     grad_pre = (grad_ref[...].astype(F32) * gate * (1.0 + pre * (1.0 - gate))).astype(BF16)
+    pair_ref[:, :width] = mixed
+    pair_ref[:, width:] = grad_pre
+    out_ref[...] = (pre * gate).astype(BF16)
+
+
+def term_kernel(peers, width, pairs_ref, term_ref):
+    half = width // 2
     second_core = lax.axis_index("hist") % 2 == 1
-    left, right = grad_pre[:, :half], grad_pre[:, half:]
-    own_ref[:, :width] = mixed
-    own_ref[:, width:] = jnp.where(second_core, right, left)
-    away_ref[:, :width] = mixed
-    away_ref[:, width:] = jnp.where(second_core, left, right)
-    pre_ref[...] = grad_pre
-    out_ref[...] = (pre * gate).astype(BF16)
-
-
-def term_kernel(peers, width, own_ref, away_ref, term_ref):
-    mixed = jnp.concatenate([own_ref[:, :width], away_ref[:, :width]], axis=0)
-    grad_pre = jnp.concatenate([own_ref[:, width:], away_ref[:, width:]], axis=0)
+    pairs = pairs_ref[...].reshape(-1, 2 * width)
+    mixed = pairs[:, :width]
+    left, right = pairs[:, width : width + half], pairs[:, width + half :]
+    grad_pre = jnp.where(second_core, right, left)
     share = width // peers
     step = 8
     term = dot(mixed, grad_pre, COLS_T)
@@ -146,7 +148,7 @@
 
 
 def backward_kernel(
-    pre_ref, weight_ref, inside_ref, pick_in, history_in, send_ref, mixed_ref, pick, aux, sems
+    pair_ref, weight_ref, inside_ref, pick_in, history_in, send_ref, mixed_ref, pick, aux, sems
 ):
     node_rows, width = mixed_ref.shape
     peers = send_ref.shape[0]
@@ -154,7 +156,7 @@
     load_aux = pltpu.make_async_copy(history_in.at[:, width:], aux, sems.at[1])
     load_pick.start()
     load_aux.start()
-    grad_mixed = dot(pre_ref[...], weight_ref[...], ROWS_T).astype(BF16)
+    grad_mixed = dot(pair_ref[:, width:], weight_ref[...], ROWS_T).astype(BF16)
     mixed_ref[...] = grad_mixed
     slot_grad = dot(inside_ref[...], grad_mixed, COLS_T).astype(BF16)
     send_ref[:, :, :width] = slot_grad.reshape(peers, CAP, width)
@@ -176,13 +178,13 @@
 
 
 def add_kernel(near_ref, sum_ref):
-    sum_ref[...] = jnp.sum(near_ref[...].astype(F32), axis=0).astype(BF16)
+    sum_ref[...] = jnp.sum(near_ref[...].astype(F32), axis=0)
 
 
 def final_kernel(
     back_ref, pick_ref, all_ref, mixed_ref, far_ref, grad_ref, share_ref
 ):
-    total = jnp.sum(far_ref[...].astype(F32), axis=0)
+    total = jnp.sum(far_ref[...], axis=0)
     share, width = share_ref.shape
     half = width // 2
     step = total.shape[0] // 2
@@ -279,33 +281,28 @@
         jnp.concatenate([feats[0], history[:, :width]], axis=0),
     )
     pulled = swap(taken)
-    out_rows, grad_pre, own, away = call(
+    out_rows, pair = call(
         forward_kernel,
-        [
-            shape((node_rows, width), BF16),
-            shape((node_rows, width), BF16),
-            shape((node_rows, width + width // 2), BF16),
-            shape((node_rows, width + width // 2), BF16),
-        ],
+        [shape((node_rows, width), BF16), shape((node_rows, 2 * width), BF16)],
         pulled,
         coef,
         feats[0],
         weight,
         grad_out[0],
     )
-    away = lax.ppermute(away, "hist", [(i, i ^ 1) for i in range(peers)])
+    chips = [[i, i + 1] for i in range(0, peers, 2)]
+    pairs = lax.all_gather(pair, "hist", axis=0, axis_index_groups=chips)
     terms = call(
         functools.partial(term_kernel, peers, width),
         shape((peers, 8, share * width // 16), BF16),
-        own,
-        away,
-    )
-    grad_pre, terms = lax.optimization_barrier((grad_pre, terms))
+        pairs,
+    )
+    pair, terms = lax.optimization_barrier((pair, terms))
     terms = swap(terms)
     sent, grad_mixed = call(
         backward_kernel,
         [shape((peers, CAP, 2 * width), BF16), shape((node_rows, width), BF16)],
-        grad_pre,
+        pair,
         weight,
         coef_inside,
         pick,
@@ -323,7 +320,7 @@
     term = swap(term, "batch", near)
     sent, term = lax.optimization_barrier((sent, term))
     back = swap(sent)
-    term = call(add_kernel, shape(term.shape[1:], BF16), term)
+    term = call(add_kernel, shape(term.shape[1:], F32), term)
     far = [[a + side * i for i in range(planes // side)] for a in range(side)]
     term = lax.all_gather(term, "batch", axis=0, axis_index_groups=far)
     grad_rows, weight_share = call(

time: 101 us -> 103 us (1.020); the launches traced: 100 us -> 101 us
  blocking collectives: 57.7 us -> 62.8 us
  starting transfers between devices: 22.3 us -> 19.1 us
  waiting for transfers between devices: 6.7 us -> 5.52 us
    all_gather x0 -> x1, blocking collectives: none -> 3.21 us  [body(): pairs = lax.all_gather(pair, 'hist', axis=0, axis_index_groups=chips)]
    ppermute x1 -> x0, starting transfers between devices: 3.1 us -> none  [body(): away = lax.ppermute(away, 'hist', [(i, i ^ 1) for i in range(peers)])]
    all_gather x1, blocking collectives: 24.4 us -> 26.4 us  [body(): term = lax.all_gather(term, 'batch', axis=0, axis_index_groups=far)]
    ppermute x1 -> x0, waiting for transfers between devices: 1.19 us -> none  [body(): away = lax.ppermute(away, 'hist', [(i, i ^ 1) for i in range(peers)])]
  transfers between devices with their start and end apart: 4 -> 3, of which waited for: 3 -> 2; matrix products, arithmetic and copies ran while one was open for 2% -> 2% of each run, Pallas kernels for 5% -> 5%
where the time goes in v6:
time: 103 us; the launch traced here: 101 us
  blocking collectives  62.8 us (61%)
  starting transfers between devices  19.1 us (19%)
  Pallas kernels  10.7 us (10%)
  waiting for transfers between devices  5.52 us (5%)
  local copies, waits for them, and re-layouts  1.06 us (1%)
    all_to_all x2, blocking collectives, swap(): lax.all_to_all(values, axis, split_axis=0, concat_axis=0, tiled=True, axi...  33.2 us
    all_gather x1, blocking collectives, body(): term = lax.all_gather(term, 'batch', axis=0, axis_index_groups=far)  26.4 us
    all_to_all x3, starting transfers between devices, swap(): lax.all_to_all(values, axis, split_axis=0, concat_axis=0, tiled=True, axi...  19.1 us
    pallas_call x9, Pallas kernels, call(): pl.pallas_call(kernel, out_shape=out_shape, in_specs=[pl.BlockSpec(memory...  10.7 us
    all_to_all x3, waiting for transfers between devices, swap(): lax.all_to_all(values, axis, split_axis=0, concat_axis=0, tiled=True, axi...  5.52 us
    all_gather x1, blocking collectives, body(): pairs = lax.all_gather(pair, 'hist', axis=0, axis_index_groups=chips)  3.21 us
  transfers between devices with their start and end apart: 3, of which 2 were waited for; matrix products, arithmetic and copies ran while one was open for 2% of the time, Pallas kernels for 5%

profile of v6, /device:TPU:6, one launch (start us, length us, event | category | flops | bytes accessed | tf_op | source)
XLA Modules:
  0.0 101.0 jit_solution(17809585839545294715)
XLA Ops:
  0.6 1.7 %shard_map.103 = s32[32,1,128]{2,1,0:T(1,128)} custom-call(s32[1,2]{1,0:T(1,128)} %tile_in.3, s32[1,256]{1,0:T(1,128)} %bitcast.14, s32[1,256]{1,0:T(1,128)} %row_in.3), custom_call_target="tpu_custom_call" | custom-call | tf_op jit(solution)/shard_map/pallas_call | solution.py:214
  2.3 9.4 %all-to-all-start = ((s32[32,1,128]{2,1,0:T(1,128)}), s32[32,1,128]{2,1,0:T(1,128)S(1)}, u32[]{:S(2)}, u32[]{:S(2)}) async-start(s32[32,1,128]{2,1,0:T(1,128)} %shard_map.103), calls=%async_computation | async-start | bytes 32768 | tf_op jit(solution)/shard_map/all_to_all | solution.py:227
  11.7 1.0 %slice.3 = bf16[256,768]{1,0:T(8,128)(2,1)S(1)} slice(bf16[256,1536]{1,0:T(8,128)(2,1)} %history_in.1), slice={[0:256], [0:768]} | slice | bytes 786432 | tf_op jit(solution)/shard_map/slice | solution.py:281
  12.7 1.0 pad_maximum_fusion.table_ref
  13.7 0.0 copy-start
  13.7 0.0 copy-start.2
  13.7 0.0 copy-start.4
  13.7 2.2 %shard_map.104 = (bf16[128,512]{1,0:T(8,128)(2,1)}, bf16[128,512]{1,0:T(8,128)(2,1)}) custom-call(s32[1,2]{1,0:T(1,128)} %tile_in.3, s32[1,256]{1,0:T(1,128)} %bitcast.15, s32[1,256]{1,0:T(1,128)} %row_in.3, bf16[128,256]{1,0:T(8,128)(2,1)} %bitcast.13), custom_call_target="tpu_custom_call" | custom-call | tf_op jit(solution)/shard_map/pallas_call | solution.py:214
  15.9 0.0 copy-start.3
  15.9 1.3 %all-to-all-done.ids_ref = s32[32,1,128]{2,1,0:T(1,128)S(1)} async-done(((s32[32,1,128]{2,1,0:T(1,128)}), s32[32,1,128]{2,1,0:T(1,128)S(1)}, u32[]{:S(2)}, u32[]{:S(2)}) %all-to-all-start) | async-done | bytes 16416 | tf_op jit(solution)/shard_map/all_to_all | solution.py:227
  17.2 0.7 shard_map.105
  17.9 18.0 %all_to_all.25.pulled_ref = bf16[32,16,768]{2,1,0:T(8,128)(2,1)S(1)} all-to-all(bf16[32,16,768]{2,1,0:T(8,128)(2,1)S(1)} %get-tuple-element.23), channel_id=1, replica_groups=mesh['batch'=16,'hist'=32] {'hist'}, dimensions={0} | all-to-all | bytes 1572864 | tf_op jit(solution)/shard_map/all_to_all | solution.py:227
  35.9 1.2 %shard_map.106 = (bf16[128,768]{1,0:T(8,128)(2,1)}, bf16[128,1536]{1,0:T(8,128)(2,1)S(1)}) custom-call(bf16[32,16,768]{2,1,0:T(8,128)(2,1)S(1)} %all_to_all.25.pulled_ref, bf16[128,512]{1,0:T(8,128)(2,1)S(1)} %copy-done.3, bf16[128,768]{1,0:T(8,128)(2,1)S(1)} %bitcast.11, bf16[768,768]{1,0:T(8,128)(2,1)S(1)} %copy-done, bf16[128,768]{1,0:T(8,128)(2,1)S(1)} %bitcast.12), custom_call_target="tpu_custom_call" | custom-call | tf_op jit(solution)/shard_map/pallas_call | solution.py:214
  37.2 3.2 %all-gather = bf16[256,1536]{1,0:T(8,128)(2,1)S(1)} all-gather(bf16[128,1536]{1,0:T(8,128)(2,1)S(1)} %get-tuple-element.27.pair_ref), channel_id=2, replica_groups={{0,1},{2,3},{4,5},{6,7},{8,9},{10,11},{12,13},{14,15},{16,17},{18,19},{..., dimensions={0}, use_global_device_ids=true | all-gather | bytes 1179648 | tf_op jit(solution)/shard_map/all_gather | solution.py:294
  40.4 0.4 shard_map.107
  40.8 0.0 copy-start.1
  40.8 15.2 %all_to_all.26.terms_ref = bf16[32,8,1152]{2,1,0:T(8,128)(2,1)S(1)} all-to-all(bf16[32,8,1152]{2,1,0:T(8,128)(2,1)S(1)} %shard_map.107), channel_id=1, replica_groups=mesh['batch'=16,'hist'=32] {'hist'}, dimensions={0} | all-to-all | bytes 1179648 | tf_op jit(solution)/shard_map/all_to_all | solution.py:227
  56.0 0.7 shard_map.109
  56.8 4.0 %all-to-all-start.3 = ((bf16[4,16,1152]{2,1,0:T(8,128)(2,1)}), bf16[4,16,1152]{2,1,0:T(8,128)(2,1)S(1)}, u32[]{:S(2)}, u32[]{:S(2)}) async-start(bf16[4,16,1152]{2,1,0:T(8,128)(2,1)} %shard_map.109), calls=%async_computation.3 | async-start | bytes 294912 | tf_op jit(solution)/shard_map/all_to_all | solution.py:227
  60.8 2.7 %shard_map.108 = (bf16[32,16,1536]{2,1,0:T(8,128)(2,1)}, bf16[128,768]{1,0:T(8,128)(2,1)S(1)}) custom-call(bf16[128,1536]{1,0:T(8,128)(2,1)S(1)} %get-tuple-element.27.pair_ref, bf16[768,768]{1,0:T(8,128)(2,1)S(1)} %copy-done, bf16[128,512]{1,0:T(8,128)(2,1)S(1)} %copy-done.5, bf16[512,384]{1,0:T(8,128)(2,1)S(1)} %get-tuple-element.29.pick_in.pick_ref, ...), custom_call_target="tpu_custom_call" | custom-call | tf_op jit(solution)/shard_map/pallas_call | solution.py:214
  63.5 4.2 %all-to-all-done.3.near_ref = bf16[4,16,1152]{2,1,0:T(8,128)(2,1)S(1)} async-done(((bf16[4,16,1152]{2,1,0:T(8,128)(2,1)}), bf16[4,16,1152]{2,1,0:T(8,128)(2,1)S(1)}, u32[]{:S(2)}, u32[]{:S(2)}) %all-to-all-start.3) | async-done | bytes 147488 | tf_op jit(solution)/shard_map/all_to_all | solution.py:227
  67.7 5.8 %all-to-all-start.4 = ((bf16[32,16,1536]{2,1,0:T(8,128)(2,1)}), bf16[32,16,1536]{2,1,0:T(8,128)(2,1)S(1)}, u32[]{:S(2)}, u32[]{:S(2)}) async-start(bf16[32,16,1536]{2,1,0:T(8,128)(2,1)} %get-tuple-element.32), calls=%async_computation.4 | async-start | bytes 3145728 | tf_op jit(solution)/shard_map/all_to_all | solution.py:227
  73.5 26.4 %all-gather.1 = f32[64,1152]{1,0:T(8,128)S(1)} all-gather(f32[16,1152]{1,0:T(8,128)S(1)} %shard_map.110), channel_id=3, replica_groups={{0,128,256,384},{32,160,288,416},{64,192,320,448},{96,224,352,480},{1,1..., dimensions={0}, use_global_device_ids=true | all-gather | bytes 368640 | tf_op jit(solution)/shard_map/all_gather | solution.py:325
  99.9 1.1 %shard_map.111 = (bf16[128,768]{1,0:T(8,128)(2,1)}, f32[24,768]{1,0:T(8,128)}) custom-call(bf16[32,16,1536]{2,1,0:T(8,128)(2,1)S(1)} %all-to-all-done.4.back_ref, bf16[512,384]{1,0:T(8,128)(2,1)S(1)} %get-tuple-element.29.pick_in.pick_ref, bf16[128,512]{1,0:T(8,128)(2,1)S(1)} %copy-done.3, bf16[128,768]{1,0:T(8,128)(2,1)S(1)} %get-tuple-element.33.mixed_ref, ...), custom_call_target="tpu_custom_call" | custom-call | tf_op jit(solution)/shard_map/pallas_call | solution.py:214
  (9 shorter events, 0.0 us)
Async XLA Ops:
  2.3 14.9 %all-to-all-start = ((s32[32,1,128]{2,1,0:T(1,128)}), s32[32,1,128]{2,1,0:T(1,128)S(1)}, u32[]{:S(2)}, u32[]{:S(2)}) async-start(s32[32,1,128]{2,1,0:T(1,128)} %shard_map.103), calls=%async_computation | async-start | bytes 32768 | tf_op jit(solution)/shard_map/all_to_all | solution.py:227
  13.7 22.2 %copy-start = (bf16[768,768]{1,0:T(8,128)(2,1)S(1)}, bf16[768,768]{1,0:T(8,128)(2,1)}, u32[]{:S(2)}) copy-start(bf16[768,768]{1,0:T(8,128)(2,1)} %weight_ref.3) | copy-start | bytes 3538948
  13.7 22.2 %copy-start.2 = (bf16[1,128,768]{2,1,0:T(8,128)(2,1)S(1)}, bf16[1,128,768]{2,1,0:T(8,128)(2,1)}, u32[]{:S(2)}) copy-start(bf16[1,128,768]{2,1,0:T(8,128)(2,1)} %param.8) | copy-start | bytes 589828
  13.7 22.2 %copy-start.4 = (bf16[1,128,768]{2,1,0:T(8,128)(2,1)S(1)}, bf16[1,128,768]{2,1,0:T(8,128)(2,1)}, u32[]{:S(2)}) copy-start(bf16[1,128,768]{2,1,0:T(8,128)(2,1)} %param.15) | copy-start | bytes 589828
  15.9 20.0 %copy-start.3 = (bf16[128,512]{1,0:T(8,128)(2,1)S(1)}, bf16[128,512]{1,0:T(8,128)(2,1)}, u32[]{:S(2)}) copy-start(bf16[128,512]{1,0:T(8,128)(2,1)} %get-tuple-element.24.all_ref) | copy-start | bytes 393220
  40.8 20.0 %copy-start.1 = (bf16[256,1536]{1,0:T(8,128)(2,1)S(1)}, bf16[256,1536]{1,0:T(8,128)(2,1)}, u32[]{:S(2)}) copy-start(bf16[256,1536]{1,0:T(8,128)(2,1)} %history_in.1) | copy-start | bytes 2359300
  40.8 20.0 %copy-start.5 = (bf16[128,512]{1,0:T(8,128)(2,1)S(1)}, bf16[128,512]{1,0:T(8,128)(2,1)}, u32[]{:S(2)}) copy-start(bf16[128,512]{1,0:T(8,128)(2,1)} %get-tuple-element.28.inside_ref) | copy-start | bytes 393220
  56.8 10.9 %all-to-all-start.3 = ((bf16[4,16,1152]{2,1,0:T(8,128)(2,1)}), bf16[4,16,1152]{2,1,0:T(8,128)(2,1)S(1)}, u32[]{:S(2)}, u32[]{:S(2)}) async-start(bf16[4,16,1152]{2,1,0:T(8,128)(2,1)} %shard_map.109), calls=%async_computation.3 | async-start | bytes 294912 | tf_op jit(solution)/shard_map/all_to_all | solution.py:227
  67.7 32.2 %all-to-all-start.4 = ((bf16[32,16,1536]{2,1,0:T(8,128)(2,1)}), bf16[32,16,1536]{2,1,0:T(8,128)(2,1)S(1)}, u32[]{:S(2)}, u32[]{:S(2)}) async-start(bf16[32,16,1536]{2,1,0:T(8,128)(2,1)} %get-tuple-element.32), calls=%async_computation.4 | async-start | bytes 3145728 | tf_op jit(solution)/shard_map/all_to_all | solution.py:227

commit v7 on v6

--- a/solution.py
+++ b/solution.py
@@ -178,13 +178,13 @@
 
 
 def add_kernel(near_ref, sum_ref):
-    sum_ref[...] = jnp.sum(near_ref[...].astype(F32), axis=0)
+    sum_ref[...] = jnp.sum(near_ref[...].astype(F32), axis=0).astype(BF16)
 
 
 def final_kernel(
     back_ref, pick_ref, all_ref, mixed_ref, far_ref, grad_ref, share_ref
 ):
-    total = jnp.sum(far_ref[...], axis=0)
+    total = jnp.sum(far_ref[...].astype(F32), axis=0)
     share, width = share_ref.shape
     half = width // 2
     step = total.shape[0] // 2
@@ -320,7 +320,7 @@
     term = swap(term, "batch", near)
     sent, term = lax.optimization_barrier((sent, term))
     back = swap(sent)
-    term = call(add_kernel, shape(term.shape[1:], F32), term)
+    term = call(add_kernel, shape(term.shape[1:], BF16), term)
     far = [[a + side * i for i in range(planes // side)] for a in range(side)]
     term = lax.all_gather(term, "batch", axis=0, axis_index_groups=far)
     grad_rows, weight_share = call(

time: 103 us -> 99.6 us (0.967); the launches traced: 101 us -> 99 us
  blocking collectives: 62.8 us -> 60.9 us
    all_gather x1, blocking collectives: 26.4 us -> 24.5 us  [body(): term = lax.all_gather(term, 'batch', axis=0, axis_index_groups=far)]
where the time goes in v7:
time: 99.6 us; the launch traced here: 99 us
  blocking collectives  60.9 us (61%)
  starting transfers between devices  19.1 us (19%)
  Pallas kernels  10.7 us (11%)
  waiting for transfers between devices  5.52 us (6%)
  local copies, waits for them, and re-layouts  1.06 us (1%)
    all_to_all x2, blocking collectives, swap(): lax.all_to_all(values, axis, split_axis=0, concat_axis=0, tiled=True, axi...  33.2 us
    all_gather x1, blocking collectives, body(): term = lax.all_gather(term, 'batch', axis=0, axis_index_groups=far)  24.5 us
    all_to_all x3, starting transfers between devices, swap(): lax.all_to_all(values, axis, split_axis=0, concat_axis=0, tiled=True, axi...  19.1 us
    pallas_call x9, Pallas kernels, call(): pl.pallas_call(kernel, out_shape=out_shape, in_specs=[pl.BlockSpec(memory...  10.7 us
    all_to_all x3, waiting for transfers between devices, swap(): lax.all_to_all(values, axis, split_axis=0, concat_axis=0, tiled=True, axi...  5.52 us
    all_gather x1, blocking collectives, body(): pairs = lax.all_gather(pair, 'hist', axis=0, axis_index_groups=chips)  3.21 us
  transfers between devices with their start and end apart: 3, of which 2 were waited for; matrix products, arithmetic and copies ran while one was open for 2% of the time, Pallas kernels for 5%

profile of v7, /device:TPU:6, one launch (start us, length us, event | category | flops | bytes accessed | tf_op | source)
XLA Modules:
  0.0 99.0 jit_solution(2302964461743171874)
XLA Ops:
  0.6 1.7 %shard_map.103 = s32[32,1,128]{2,1,0:T(1,128)} custom-call(s32[1,2]{1,0:T(1,128)} %tile_in.3, s32[1,256]{1,0:T(1,128)} %bitcast.14, s32[1,256]{1,0:T(1,128)} %row_in.3), custom_call_target="tpu_custom_call" | custom-call | tf_op jit(solution)/shard_map/pallas_call | solution.py:214
  2.3 9.4 %all-to-all-start = ((s32[32,1,128]{2,1,0:T(1,128)}), s32[32,1,128]{2,1,0:T(1,128)S(1)}, u32[]{:S(2)}, u32[]{:S(2)}) async-start(s32[32,1,128]{2,1,0:T(1,128)} %shard_map.103), calls=%async_computation | async-start | bytes 32768 | tf_op jit(solution)/shard_map/all_to_all | solution.py:227
  11.7 1.0 %slice.3 = bf16[256,768]{1,0:T(8,128)(2,1)S(1)} slice(bf16[256,1536]{1,0:T(8,128)(2,1)} %history_in.1), slice={[0:256], [0:768]} | slice | bytes 786432 | tf_op jit(solution)/shard_map/slice | solution.py:281
  12.7 1.0 pad_maximum_fusion.table_ref
  13.7 0.0 copy-start
  13.7 0.0 copy-start.2
  13.7 0.0 copy-start.4
  13.7 2.2 %shard_map.104 = (bf16[128,512]{1,0:T(8,128)(2,1)}, bf16[128,512]{1,0:T(8,128)(2,1)}) custom-call(s32[1,2]{1,0:T(1,128)} %tile_in.3, s32[1,256]{1,0:T(1,128)} %bitcast.15, s32[1,256]{1,0:T(1,128)} %row_in.3, bf16[128,256]{1,0:T(8,128)(2,1)} %bitcast.13), custom_call_target="tpu_custom_call" | custom-call | tf_op jit(solution)/shard_map/pallas_call | solution.py:214
  15.9 0.0 copy-start.3
  15.9 1.3 %all-to-all-done.ids_ref = s32[32,1,128]{2,1,0:T(1,128)S(1)} async-done(((s32[32,1,128]{2,1,0:T(1,128)}), s32[32,1,128]{2,1,0:T(1,128)S(1)}, u32[]{:S(2)}, u32[]{:S(2)}) %all-to-all-start) | async-done | bytes 16416 | tf_op jit(solution)/shard_map/all_to_all | solution.py:227
  17.2 0.7 shard_map.105
  17.9 18.0 %all_to_all.25.pulled_ref = bf16[32,16,768]{2,1,0:T(8,128)(2,1)S(1)} all-to-all(bf16[32,16,768]{2,1,0:T(8,128)(2,1)S(1)} %get-tuple-element.23), channel_id=1, replica_groups=mesh['batch'=16,'hist'=32] {'hist'}, dimensions={0} | all-to-all | bytes 1572864 | tf_op jit(solution)/shard_map/all_to_all | solution.py:227
  35.9 1.2 %shard_map.106 = (bf16[128,768]{1,0:T(8,128)(2,1)}, bf16[128,1536]{1,0:T(8,128)(2,1)S(1)}) custom-call(bf16[32,16,768]{2,1,0:T(8,128)(2,1)S(1)} %all_to_all.25.pulled_ref, bf16[128,512]{1,0:T(8,128)(2,1)S(1)} %copy-done.3, bf16[128,768]{1,0:T(8,128)(2,1)S(1)} %bitcast.10, bf16[768,768]{1,0:T(8,128)(2,1)S(1)} %copy-done, bf16[128,768]{1,0:T(8,128)(2,1)S(1)} %bitcast.12), custom_call_target="tpu_custom_call" | custom-call | tf_op jit(solution)/shard_map/pallas_call | solution.py:214
  37.2 3.2 %all-gather = bf16[256,1536]{1,0:T(8,128)(2,1)S(1)} all-gather(bf16[128,1536]{1,0:T(8,128)(2,1)S(1)} %get-tuple-element.27.pair_ref), channel_id=2, replica_groups={{0,1},{2,3},{4,5},{6,7},{8,9},{10,11},{12,13},{14,15},{16,17},{18,19},{..., dimensions={0}, use_global_device_ids=true | all-gather | bytes 1179648 | tf_op jit(solution)/shard_map/all_gather | solution.py:294
  40.4 0.4 shard_map.107
  40.8 0.0 copy-start.1
  40.8 15.2 %all_to_all.26.terms_ref = bf16[32,8,1152]{2,1,0:T(8,128)(2,1)S(1)} all-to-all(bf16[32,8,1152]{2,1,0:T(8,128)(2,1)S(1)} %shard_map.107), channel_id=1, replica_groups=mesh['batch'=16,'hist'=32] {'hist'}, dimensions={0} | all-to-all | bytes 1179648 | tf_op jit(solution)/shard_map/all_to_all | solution.py:227
  56.0 0.7 shard_map.109
  56.8 4.0 %all-to-all-start.3 = ((bf16[4,16,1152]{2,1,0:T(8,128)(2,1)}), bf16[4,16,1152]{2,1,0:T(8,128)(2,1)S(1)}, u32[]{:S(2)}, u32[]{:S(2)}) async-start(bf16[4,16,1152]{2,1,0:T(8,128)(2,1)} %shard_map.109), calls=%async_computation.3 | async-start | bytes 294912 | tf_op jit(solution)/shard_map/all_to_all | solution.py:227
  60.8 2.7 %shard_map.108 = (bf16[32,16,1536]{2,1,0:T(8,128)(2,1)}, bf16[128,768]{1,0:T(8,128)(2,1)S(1)}) custom-call(bf16[128,1536]{1,0:T(8,128)(2,1)S(1)} %get-tuple-element.27.pair_ref, bf16[768,768]{1,0:T(8,128)(2,1)S(1)} %copy-done, bf16[128,512]{1,0:T(8,128)(2,1)S(1)} %copy-done.5, bf16[512,384]{1,0:T(8,128)(2,1)S(1)} %get-tuple-element.29.pick_in.pick_ref, ...), custom_call_target="tpu_custom_call" | custom-call | tf_op jit(solution)/shard_map/pallas_call | solution.py:214
  63.5 4.2 %all-to-all-done.3.near_ref = bf16[4,16,1152]{2,1,0:T(8,128)(2,1)S(1)} async-done(((bf16[4,16,1152]{2,1,0:T(8,128)(2,1)}), bf16[4,16,1152]{2,1,0:T(8,128)(2,1)S(1)}, u32[]{:S(2)}, u32[]{:S(2)}) %all-to-all-start.3) | async-done | bytes 147488 | tf_op jit(solution)/shard_map/all_to_all | solution.py:227
  67.7 5.8 %all-to-all-start.4 = ((bf16[32,16,1536]{2,1,0:T(8,128)(2,1)}), bf16[32,16,1536]{2,1,0:T(8,128)(2,1)S(1)}, u32[]{:S(2)}, u32[]{:S(2)}) async-start(bf16[32,16,1536]{2,1,0:T(8,128)(2,1)} %get-tuple-element.32), calls=%async_computation.4 | async-start | bytes 3145728 | tf_op jit(solution)/shard_map/all_to_all | solution.py:227
  73.5 24.5 %all-gather.1 = bf16[64,1152]{1,0:T(8,128)(2,1)S(1)} all-gather(bf16[16,1152]{1,0:T(8,128)(2,1)S(1)} %shard_map.110), channel_id=3, replica_groups={{0,128,256,384},{32,160,288,416},{64,192,320,448},{96,224,352,480},{1,1..., dimensions={0}, use_global_device_ids=true | all-gather | bytes 184320 | tf_op jit(solution)/shard_map/all_gather | solution.py:325
  97.9 1.1 %shard_map.111 = (bf16[128,768]{1,0:T(8,128)(2,1)}, f32[24,768]{1,0:T(8,128)}) custom-call(bf16[32,16,1536]{2,1,0:T(8,128)(2,1)S(1)} %all-to-all-done.4.back_ref, bf16[512,384]{1,0:T(8,128)(2,1)S(1)} %get-tuple-element.29.pick_in.pick_ref, bf16[128,512]{1,0:T(8,128)(2,1)S(1)} %copy-done.3, bf16[128,768]{1,0:T(8,128)(2,1)S(1)} %get-tuple-element.33.mixed_ref, ...), custom_call_target="tpu_custom_call" | custom-call | tf_op jit(solution)/shard_map/pallas_call | solution.py:214
  (9 shorter events, 0.0 us)
Async XLA Ops:
  2.3 14.9 %all-to-all-start = ((s32[32,1,128]{2,1,0:T(1,128)}), s32[32,1,128]{2,1,0:T(1,128)S(1)}, u32[]{:S(2)}, u32[]{:S(2)}) async-start(s32[32,1,128]{2,1,0:T(1,128)} %shard_map.103), calls=%async_computation | async-start | bytes 32768 | tf_op jit(solution)/shard_map/all_to_all | solution.py:227
  13.7 22.2 %copy-start = (bf16[768,768]{1,0:T(8,128)(2,1)S(1)}, bf16[768,768]{1,0:T(8,128)(2,1)}, u32[]{:S(2)}) copy-start(bf16[768,768]{1,0:T(8,128)(2,1)} %weight_ref.3) | copy-start | bytes 3538948
  13.7 22.2 %copy-start.2 = (bf16[1,128,768]{2,1,0:T(8,128)(2,1)S(1)}, bf16[1,128,768]{2,1,0:T(8,128)(2,1)}, u32[]{:S(2)}) copy-start(bf16[1,128,768]{2,1,0:T(8,128)(2,1)} %param.8) | copy-start | bytes 589828
  13.7 22.2 %copy-start.4 = (bf16[1,128,768]{2,1,0:T(8,128)(2,1)S(1)}, bf16[1,128,768]{2,1,0:T(8,128)(2,1)}, u32[]{:S(2)}) copy-start(bf16[1,128,768]{2,1,0:T(8,128)(2,1)} %param.15) | copy-start | bytes 589828
  15.9 20.0 %copy-start.3 = (bf16[128,512]{1,0:T(8,128)(2,1)S(1)}, bf16[128,512]{1,0:T(8,128)(2,1)}, u32[]{:S(2)}) copy-start(bf16[128,512]{1,0:T(8,128)(2,1)} %get-tuple-element.24.all_ref) | copy-start | bytes 393220
  40.8 20.0 %copy-start.1 = (bf16[256,1536]{1,0:T(8,128)(2,1)S(1)}, bf16[256,1536]{1,0:T(8,128)(2,1)}, u32[]{:S(2)}) copy-start(bf16[256,1536]{1,0:T(8,128)(2,1)} %history_in.1) | copy-start | bytes 2359300
  40.8 20.0 %copy-start.5 = (bf16[128,512]{1,0:T(8,128)(2,1)S(1)}, bf16[128,512]{1,0:T(8,128)(2,1)}, u32[]{:S(2)}) copy-start(bf16[128,512]{1,0:T(8,128)(2,1)} %get-tuple-element.28.inside_ref) | copy-start | bytes 393220
  56.8 10.9 %all-to-all-start.3 = ((bf16[4,16,1152]{2,1,0:T(8,128)(2,1)}), bf16[4,16,1152]{2,1,0:T(8,128)(2,1)S(1)}, u32[]{:S(2)}, u32[]{:S(2)}) async-start(bf16[4,16,1152]{2,1,0:T(8,128)(2,1)} %shard_map.109), calls=%async_computation.3 | async-start | bytes 294912 | tf_op jit(solution)/shard_map/all_to_all | solution.py:227
  67.7 30.3 %all-to-all-start.4 = ((bf16[32,16,1536]{2,1,0:T(8,128)(2,1)}), bf16[32,16,1536]{2,1,0:T(8,128)(2,1)S(1)}, u32[]{:S(2)}, u32[]{:S(2)}) async-start(bf16[32,16,1536]{2,1,0:T(8,128)(2,1)} %get-tuple-element.32), calls=%async_computation.4 | async-start | bytes 3145728 | tf_op jit(solution)/shard_map/all_to_all | solution.py:227

commit v8 on v7

--- a/solution.py
+++ b/solution.py
@@ -116,7 +116,6 @@
     feats_ref,
     weight_ref,
     grad_ref,
-    out_ref,
     pair_ref,
 ):
     width = feats_ref.shape[1]
@@ -127,7 +126,6 @@
     grad_pre = (grad_ref[...].astype(F32) * gate * (1.0 + pre * (1.0 - gate))).astype(BF16)
     pair_ref[:, :width] = mixed
     pair_ref[:, width:] = grad_pre
-    out_ref[...] = (pre * gate).astype(BF16)
 
 
 def term_kernel(peers, width, pairs_ref, term_ref):
@@ -148,7 +146,17 @@
 
 
 def backward_kernel(
-    pair_ref, weight_ref, inside_ref, pick_in, history_in, send_ref, mixed_ref, pick, aux, sems
+    pair_ref,
+    weight_ref,
+    inside_ref,
+    pick_in,
+    history_in,
+    send_ref,
+    mixed_ref,
+    out_ref,
+    pick,
+    aux,
+    sems,
 ):
     node_rows, width = mixed_ref.shape
     peers = send_ref.shape[0]
@@ -160,6 +168,8 @@
     mixed_ref[...] = grad_mixed
     slot_grad = dot(inside_ref[...], grad_mixed, COLS_T).astype(BF16)
     send_ref[:, :, :width] = slot_grad.reshape(peers, CAP, width)
+    pre = dot(pair_ref[:, :width], weight_ref[...])
+    out_ref[...] = (pre * jax.nn.sigmoid(pre)).astype(BF16)
     load_pick.wait()
     load_aux.wait()
     taken = dot(pick[:, node_rows:], aux[...]).astype(BF16)
@@ -281,9 +291,9 @@
         jnp.concatenate([feats[0], history[:, :width]], axis=0),
     )
     pulled = swap(taken)
-    out_rows, pair = call(
+    pair = call(
         forward_kernel,
-        [shape((node_rows, width), BF16), shape((node_rows, 2 * width), BF16)],
+        shape((node_rows, 2 * width), BF16),
         pulled,
         coef,
         feats[0],
@@ -299,9 +309,13 @@
     )
     pair, terms = lax.optimization_barrier((pair, terms))
     terms = swap(terms)
-    sent, grad_mixed = call(
+    sent, grad_mixed, out_rows = call(
         backward_kernel,
-        [shape((peers, CAP, 2 * width), BF16), shape((node_rows, width), BF16)],
+        [
+            shape((peers, CAP, 2 * width), BF16),
+            shape((node_rows, width), BF16),
+            shape((node_rows, width), BF16),
+        ],
         pair,
         weight,
         coef_inside,
@@ -314,6 +328,7 @@
             pltpu.SemaphoreType.DMA((2,)),
         ),
     )
+    sent, terms = lax.optimization_barrier((sent, terms))
     side = 4
     near = [[a * side + i for i in range(side)] for a in range(planes // side)]
     term = call(weight_kernel, shape((side, 16, share * width // 16), BF16), terms)

time: 99.6 us -> 99.4 us (level)
  blocking collectives: 60.9 us -> 56.8 us
  local copies, waits for them, and re-layouts: 1.06 us -> 3.8 us
  starting transfers between devices: 19.1 us -> 20.4 us
  Pallas kernels: 10.7 us -> 9.49 us
  waiting for transfers between devices: 5.52 us -> 6.64 us
    all_to_all x2, blocking collectives: 33.2 us -> 29.5 us  [swap(): lax.all_to_all(values, axis, split_axis=0, concat_axis=0, tiled=True, axi...]
    unnamed x12 -> x18, local copies, waits for them, and re-layouts: 0.04 us -> 2.77 us
    all_to_all x3, starting transfers between devices: 19.1 us -> 20.4 us  [swap(): lax.all_to_all(values, axis, split_axis=0, concat_axis=0, tiled=True, axi...]
    pallas_call x9, Pallas kernels: 10.7 us -> 9.49 us  [call(): pl.pallas_call(kernel, out_shape=out_shape, in_specs=[pl.BlockSpec(memory...]
    all_to_all x3, waiting for transfers between devices: 5.52 us -> 6.64 us  [swap(): lax.all_to_all(values, axis, split_axis=0, concat_axis=0, tiled=True, axi...]
  transfers between devices with their start and end apart: 3 -> 3, of which waited for: 2 -> 2; matrix products, arithmetic and copies ran while one was open for 2% -> 2% of each run, Pallas kernels for 5% -> 4%
where the time goes in v8:
time: 99.4 us; the launch traced here: 98.9 us
  blocking collectives  56.8 us (57%)
  starting transfers between devices  20.4 us (21%)
  Pallas kernels  9.49 us (10%)
  waiting for transfers between devices  6.64 us (7%)
  local copies, waits for them, and re-layouts  3.8 us (4%)
    all_to_all x2, blocking collectives, swap(): lax.all_to_all(values, axis, split_axis=0, concat_axis=0, tiled=True, axi...  29.5 us
    all_gather x1, blocking collectives, body(): term = lax.all_gather(term, 'batch', axis=0, axis_index_groups=far)  24.1 us
    all_to_all x3, starting transfers between devices, swap(): lax.all_to_all(values, axis, split_axis=0, concat_axis=0, tiled=True, axi...  20.4 us
    pallas_call x9, Pallas kernels, call(): pl.pallas_call(kernel, out_shape=out_shape, in_specs=[pl.BlockSpec(memory...  9.49 us
    all_to_all x3, waiting for transfers between devices, swap(): lax.all_to_all(values, axis, split_axis=0, concat_axis=0, tiled=True, axi...  6.64 us
    all_gather x1, blocking collectives, body(): pairs = lax.all_gather(pair, 'hist', axis=0, axis_index_groups=chips)  3.2 us
    unnamed x18, local copies, waits for them, and re-layouts  2.77 us
  transfers between devices with their start and end apart: 3, of which 2 were waited for; matrix products, arithmetic and copies ran while one was open for 2% of the time, Pallas kernels for 4%

profile of v8, /device:TPU:6, one launch (start us, length us, event | category | flops | bytes accessed | tf_op | source)
XLA Modules:
  0.0 98.9 jit_solution(2968460473030400847)
XLA Ops:
  0.6 1.7 %shard_map.103 = s32[32,1,128]{2,1,0:T(1,128)} custom-call(s32[1,2]{1,0:T(1,128)} %tile_in.3, s32[1,256]{1,0:T(1,128)} %bitcast.14, s32[1,256]{1,0:T(1,128)} %row_in.3), custom_call_target="tpu_custom_call" | custom-call | tf_op jit(solution)/shard_map/pallas_call | solution.py:224
  2.3 9.4 %all-to-all-start = ((s32[32,1,128]{2,1,0:T(1,128)}), s32[32,1,128]{2,1,0:T(1,128)S(1)}, u32[]{:S(2)}, u32[]{:S(2)}) async-start(s32[32,1,128]{2,1,0:T(1,128)} %shard_map.103), calls=%async_computation | async-start | bytes 32768 | tf_op jit(solution)/shard_map/all_to_all | solution.py:237
  11.7 1.0 %slice.3 = bf16[256,768]{1,0:T(8,128)(2,1)S(1)} slice(bf16[256,1536]{1,0:T(8,128)(2,1)} %history_in.1), slice={[0:256], [0:768]} | slice | bytes 786432 | tf_op jit(solution)/shard_map/slice | solution.py:291
  12.7 1.0 pad_maximum_fusion.table_ref
  13.7 0.0 copy-start
  13.7 0.0 copy-start.3
  13.7 2.2 %shard_map.104 = (bf16[128,512]{1,0:T(8,128)(2,1)}, bf16[128,512]{1,0:T(8,128)(2,1)}) custom-call(s32[1,2]{1,0:T(1,128)} %tile_in.3, s32[1,256]{1,0:T(1,128)} %bitcast.15, s32[1,256]{1,0:T(1,128)} %row_in.3, bf16[128,256]{1,0:T(8,128)(2,1)} %bitcast.13), custom_call_target="tpu_custom_call" | custom-call | tf_op jit(solution)/shard_map/pallas_call | solution.py:224
  15.9 1.3 %all-to-all-done.ids_ref = s32[32,1,128]{2,1,0:T(1,128)S(1)} async-done(((s32[32,1,128]{2,1,0:T(1,128)}), s32[32,1,128]{2,1,0:T(1,128)S(1)}, u32[]{:S(2)}, u32[]{:S(2)}) %all-to-all-start) | async-done | bytes 16416 | tf_op jit(solution)/shard_map/all_to_all | solution.py:237
  17.2 0.7 shard_map.105
  17.9 18.0 %all_to_all.25.pulled_ref = bf16[32,16,768]{2,1,0:T(8,128)(2,1)S(1)} all-to-all(bf16[32,16,768]{2,1,0:T(8,128)(2,1)S(1)} %get-tuple-element.24), channel_id=1, replica_groups=mesh['batch'=16,'hist'=32] {'hist'}, dimensions={0} | all-to-all | bytes 1572864 | tf_op jit(solution)/shard_map/all_to_all | solution.py:237
  35.9 0.5 shard_map.106.pair_ref
  36.5 3.2 %all-gather = bf16[256,1536]{1,0:T(8,128)(2,1)S(1)} all-gather(bf16[128,1536]{1,0:T(8,128)(2,1)S(1)} %shard_map.106.pair_ref), channel_id=2, replica_groups={{0,1},{2,3},{4,5},{6,7},{8,9},{10,11},{12,13},{14,15},{16,17},{18,19},{..., dimensions={0}, use_global_device_ids=true | all-gather | bytes 1179648 | tf_op jit(solution)/shard_map/all_gather | solution.py:304
  39.7 1.2 %shard_map.107 = bf16[32,8,1152]{2,1,0:T(8,128)(2,1)} custom-call(bf16[2,128,1536]{2,1,0:T(8,128)(2,1)S(1)} %bitcast.8), custom_call_target="tpu_custom_call" | custom-call | tf_op jit(solution)/shard_map/pallas_call | solution.py:224
  40.9 5.5 %all-to-all-start.2 = ((bf16[32,8,1152]{2,1,0:T(8,128)(2,1)}), bf16[32,8,1152]{2,1,0:T(8,128)(2,1)S(1)}, u32[]{:S(2)}, u32[]{:S(2)}) async-start(bf16[32,8,1152]{2,1,0:T(8,128)(2,1)} %shard_map.107), calls=%async_computation.2 | async-start | bytes 1179648 | tf_op jit(solution)/shard_map/all_to_all | solution.py:237
  46.5 0.9 copy-done.8
  47.4 2.0 %shard_map.108 = (bf16[32,16,1536]{2,1,0:T(8,128)(2,1)S(1)}, bf16[128,768]{1,0:T(8,128)(2,1)S(1)}, bf16[128,768]{1,0:T(8,128)(2,1)}) custom-call(bf16[128,1536]{1,0:T(8,128)(2,1)S(1)} %shard_map.106.pair_ref, bf16[768,768]{1,0:T(8,128)(2,1)S(1)} %copy-done, bf16[128,512]{1,0:T(8,128)(2,1)S(1)} %copy-done.8, ...), custom_call_target="tpu_custom_call" | custom-call | tf_op jit(solution)/shard_map/pallas_call | solution.py:224
  49.4 1.2 %copy-done.2 = bf16[32,16,1536]{2,1,0:T(8,128)(2,1)} copy-done((bf16[32,16,1536]{2,1,0:T(8,128)(2,1)}, bf16[32,16,1536]{2,1,0:T(8,128)(2,1)S(1)}, u32[]{:S(2)}) %copy-start.2) | copy-done | bytes 1572888
  50.5 0.7 copy-done.6
  51.2 5.3 %all-to-all-done.2.terms_ref = bf16[32,8,1152]{2,1,0:T(8,128)(2,1)S(1)} async-done(((bf16[32,8,1152]{2,1,0:T(8,128)(2,1)}), bf16[32,8,1152]{2,1,0:T(8,128)(2,1)S(1)}, u32[]{:S(2)}, u32[]{:S(2)}) %all-to-all-start.2) | async-done | bytes 589856 | tf_op jit(solution)/shard_map/all_to_all | solution.py:237
  56.5 0.1 shard_map.109
  56.6 11.5 %all_to_all.26.near_ref = bf16[4,16,1152]{2,1,0:T(8,128)(2,1)S(1)} all-to-all(bf16[4,16,1152]{2,1,0:T(8,128)(2,1)S(1)} %shard_map.109), channel_id=1, replica_groups={{0,32,64,96},{128,160,192,224},{256,288,320,352},{384,416,448,480},{1,3..., dimensions={0} | all-to-all | bytes 294912 | tf_op jit(solution)/shard_map/all_to_all | solution.py:237
  68.1 5.5 %all-to-all-start.4 = ((bf16[32,16,1536]{2,1,0:T(8,128)(2,1)}), bf16[32,16,1536]{2,1,0:T(8,128)(2,1)S(1)}, u32[]{:S(2)}, u32[]{:S(2)}) async-start(bf16[32,16,1536]{2,1,0:T(8,128)(2,1)} %copy-done.2), calls=%async_computation.4 | async-start | bytes 3145728 | tf_op jit(solution)/shard_map/all_to_all | solution.py:237
  73.7 24.1 %all-gather.1 = bf16[64,1152]{1,0:T(8,128)(2,1)S(1)} all-gather(bf16[16,1152]{1,0:T(8,128)(2,1)S(1)} %shard_map.110), channel_id=3, replica_groups={{0,128,256,384},{32,160,288,416},{64,192,320,448},{96,224,352,480},{1,1..., dimensions={0}, use_global_device_ids=true | all-gather | bytes 184320 | tf_op jit(solution)/shard_map/all_gather | solution.py:340
  97.8 1.1 %shard_map.111 = (bf16[128,768]{1,0:T(8,128)(2,1)}, f32[24,768]{1,0:T(8,128)}) custom-call(bf16[32,16,1536]{2,1,0:T(8,128)(2,1)S(1)} %all-to-all-done.4.back_ref, bf16[512,384]{1,0:T(8,128)(2,1)S(1)} %get-tuple-element.28.pick_in.pick_ref, bf16[128,512]{1,0:T(8,128)(2,1)S(1)} %copy-done.4, bf16[128,768]{1,0:T(8,128)(2,1)S(1)} %copy-done.7, ...), custom_call_target="tpu_custom_call" | custom-call | tf_op jit(solution)/shard_map/pallas_call | solution.py:224
  (15 shorter events, 0.1 us)
Async XLA Ops:
  2.3 14.9 %all-to-all-start = ((s32[32,1,128]{2,1,0:T(1,128)}), s32[32,1,128]{2,1,0:T(1,128)S(1)}, u32[]{:S(2)}, u32[]{:S(2)}) async-start(s32[32,1,128]{2,1,0:T(1,128)} %shard_map.103), calls=%async_computation | async-start | bytes 32768 | tf_op jit(solution)/shard_map/all_to_all | solution.py:237
  13.7 22.2 %copy-start = (bf16[768,768]{1,0:T(8,128)(2,1)S(1)}, bf16[768,768]{1,0:T(8,128)(2,1)}, u32[]{:S(2)}) copy-start(bf16[768,768]{1,0:T(8,128)(2,1)} %weight_ref.3) | copy-start | bytes 3538948
  13.7 22.2 %copy-start.3 = (bf16[1,128,768]{2,1,0:T(8,128)(2,1)S(1)}, bf16[1,128,768]{2,1,0:T(8,128)(2,1)}, u32[]{:S(2)}) copy-start(bf16[1,128,768]{2,1,0:T(8,128)(2,1)} %param.8) | copy-start | bytes 589828
  13.7 22.2 %copy-start.5 = (bf16[1,128,768]{2,1,0:T(8,128)(2,1)S(1)}, bf16[1,128,768]{2,1,0:T(8,128)(2,1)}, u32[]{:S(2)}) copy-start(bf16[1,128,768]{2,1,0:T(8,128)(2,1)} %param.15) | copy-start | bytes 589828
  15.9 20.0 %copy-start.4 = (bf16[128,512]{1,0:T(8,128)(2,1)S(1)}, bf16[128,512]{1,0:T(8,128)(2,1)}, u32[]{:S(2)}) copy-start(bf16[128,512]{1,0:T(8,128)(2,1)} %get-tuple-element.25.all_ref) | copy-start | bytes 393220
  39.7 6.8 %copy-start.1 = (bf16[256,1536]{1,0:T(8,128)(2,1)S(1)}, bf16[256,1536]{1,0:T(8,128)(2,1)}, u32[]{:S(2)}) copy-start(bf16[256,1536]{1,0:T(8,128)(2,1)} %history_in.1) | copy-start | bytes 2359300
  40.9 15.7 %all-to-all-start.2 = ((bf16[32,8,1152]{2,1,0:T(8,128)(2,1)}), bf16[32,8,1152]{2,1,0:T(8,128)(2,1)S(1)}, u32[]{:S(2)}, u32[]{:S(2)}) async-start(bf16[32,8,1152]{2,1,0:T(8,128)(2,1)} %shard_map.107), calls=%async_computation.2 | async-start | bytes 1179648 | tf_op jit(solution)/shard_map/all_to_all | solution.py:237
  46.5 0.9 copy-start.8
  49.4 1.2 %copy-start.2 = (bf16[32,16,1536]{2,1,0:T(8,128)(2,1)}, bf16[32,16,1536]{2,1,0:T(8,128)(2,1)S(1)}, u32[]{:S(2)}) copy-start(bf16[32,16,1536]{2,1,0:T(8,128)(2,1)S(1)} %get-tuple-element.34) | copy-start | bytes 4718596
  50.5 0.7 copy-start.6
  68.1 29.7 %copy-start.7 = (bf16[128,768]{1,0:T(8,128)(2,1)S(1)}, bf16[128,768]{1,0:T(8,128)(2,1)}, u32[]{:S(2)}) copy-start(bf16[128,768]{1,0:T(8,128)(2,1)} %copy-done.6) | copy-start | bytes 589828
  68.1 29.7 %all-to-all-start.4 = ((bf16[32,16,1536]{2,1,0:T(8,128)(2,1)}), bf16[32,16,1536]{2,1,0:T(8,128)(2,1)S(1)}, u32[]{:S(2)}, u32[]{:S(2)}) async-start(bf16[32,16,1536]{2,1,0:T(8,128)(2,1)} %copy-done.2), calls=%async_computation.4 | async-start | bytes 3145728 | tf_op jit(solution)/shard_map/all_to_all | solution.py:237

commit v9 on v8

--- a/solution.py
+++ b/solution.py
@@ -328,7 +328,6 @@
             pltpu.SemaphoreType.DMA((2,)),
         ),
     )
-    sent, terms = lax.optimization_barrier((sent, terms))
     side = 4
     near = [[a * side + i for i in range(side)] for a in range(planes // side)]
     term = call(weight_kernel, shape((side, 16, share * width // 16), BF16), terms)

time: 99.4 us -> 98.9 us (level)
  blocking collectives: 56.8 us -> 60.9 us
  waiting for transfers between devices: 6.64 us -> 5.05 us
  local copies, waits for them, and re-layouts: 3.8 us -> 2.23 us
  starting transfers between devices: 20.4 us -> 19.1 us
    all_to_all x2, blocking collectives: 29.5 us -> 33.2 us  [swap(): lax.all_to_all(values, axis, split_axis=0, concat_axis=0, tiled=True, axi...]
    all_to_all x3, waiting for transfers between devices: 6.64 us -> 5.05 us  [swap(): lax.all_to_all(values, axis, split_axis=0, concat_axis=0, tiled=True, axi...]
    unnamed x18 -> x14, local copies, waits for them, and re-layouts: 2.77 us -> 1.21 us
    all_to_all x3, starting transfers between devices: 20.4 us -> 19.1 us  [swap(): lax.all_to_all(values, axis, split_axis=0, concat_axis=0, tiled=True, axi...]
where the time goes in v9:
time: 98.9 us; the launch traced here: 98.4 us
  blocking collectives  60.9 us (62%)
  starting transfers between devices  19.1 us (19%)
  Pallas kernels  9.31 us (9%)
  waiting for transfers between devices  5.05 us (5%)
  local copies, waits for them, and re-layouts  2.23 us (2%)
    all_to_all x2, blocking collectives, swap(): lax.all_to_all(values, axis, split_axis=0, concat_axis=0, tiled=True, axi...  33.2 us
    all_gather x1, blocking collectives, body(): term = lax.all_gather(term, 'batch', axis=0, axis_index_groups=far)  24.4 us
    all_to_all x3, starting transfers between devices, swap(): lax.all_to_all(values, axis, split_axis=0, concat_axis=0, tiled=True, axi...  19.1 us
    pallas_call x9, Pallas kernels, call(): pl.pallas_call(kernel, out_shape=out_shape, in_specs=[pl.BlockSpec(memory...  9.31 us
    all_to_all x3, waiting for transfers between devices, swap(): lax.all_to_all(values, axis, split_axis=0, concat_axis=0, tiled=True, axi...  5.05 us
    all_gather x1, blocking collectives, body(): pairs = lax.all_gather(pair, 'hist', axis=0, axis_index_groups=chips)  3.2 us
  transfers between devices with their start and end apart: 3, of which 2 were waited for; matrix products, arithmetic and copies ran while one was open for 2% of the time, Pallas kernels for 4%

profile of v9, /device:TPU:6, one launch (start us, length us, event | category | flops | bytes accessed | tf_op | source)
XLA Modules:
  0.0 98.4 jit_solution(14009600786851227470)
XLA Ops:
  0.6 1.7 %shard_map.103 = s32[32,1,128]{2,1,0:T(1,128)} custom-call(s32[1,2]{1,0:T(1,128)} %tile_in.3, s32[1,256]{1,0:T(1,128)} %bitcast.14, s32[1,256]{1,0:T(1,128)} %row_in.3), custom_call_target="tpu_custom_call" | custom-call | tf_op jit(solution)/shard_map/pallas_call | solution.py:224
  2.3 9.4 %all-to-all-start = ((s32[32,1,128]{2,1,0:T(1,128)}), s32[32,1,128]{2,1,0:T(1,128)S(1)}, u32[]{:S(2)}, u32[]{:S(2)}) async-start(s32[32,1,128]{2,1,0:T(1,128)} %shard_map.103), calls=%async_computation | async-start | bytes 32768 | tf_op jit(solution)/shard_map/all_to_all | solution.py:237
  11.7 1.0 %slice.3 = bf16[256,768]{1,0:T(8,128)(2,1)S(1)} slice(bf16[256,1536]{1,0:T(8,128)(2,1)} %history_in.1), slice={[0:256], [0:768]} | slice | bytes 786432 | tf_op jit(solution)/shard_map/slice | solution.py:291
  12.7 1.0 pad_maximum_fusion.table_ref
  13.7 0.0 copy-start
  13.7 0.0 copy-start.3
  13.7 2.2 %shard_map.104 = (bf16[128,512]{1,0:T(8,128)(2,1)}, bf16[128,512]{1,0:T(8,128)(2,1)}) custom-call(s32[1,2]{1,0:T(1,128)} %tile_in.3, s32[1,256]{1,0:T(1,128)} %bitcast.15, s32[1,256]{1,0:T(1,128)} %row_in.3, bf16[128,256]{1,0:T(8,128)(2,1)} %bitcast.13), custom_call_target="tpu_custom_call" | custom-call | tf_op jit(solution)/shard_map/pallas_call | solution.py:224
  15.9 0.0 copy-start.4
  15.9 1.3 %all-to-all-done.ids_ref = s32[32,1,128]{2,1,0:T(1,128)S(1)} async-done(((s32[32,1,128]{2,1,0:T(1,128)}), s32[32,1,128]{2,1,0:T(1,128)S(1)}, u32[]{:S(2)}, u32[]{:S(2)}) %all-to-all-start) | async-done | bytes 16416 | tf_op jit(solution)/shard_map/all_to_all | solution.py:237
  17.2 0.7 shard_map.105
  17.9 18.0 %all_to_all.25.pulled_ref = bf16[32,16,768]{2,1,0:T(8,128)(2,1)S(1)} all-to-all(bf16[32,16,768]{2,1,0:T(8,128)(2,1)S(1)} %get-tuple-element.22), channel_id=1, replica_groups=mesh['batch'=16,'hist'=32] {'hist'}, dimensions={0} | all-to-all | bytes 1572864 | tf_op jit(solution)/shard_map/all_to_all | solution.py:237
  35.9 0.5 shard_map.106.pair_ref
  36.5 3.2 %all-gather = bf16[256,1536]{1,0:T(8,128)(2,1)S(1)} all-gather(bf16[128,1536]{1,0:T(8,128)(2,1)S(1)} %shard_map.106.pair_ref), channel_id=2, replica_groups={{0,1},{2,3},{4,5},{6,7},{8,9},{10,11},{12,13},{14,15},{16,17},{18,19},{..., dimensions={0}, use_global_device_ids=true | all-gather | bytes 1179648 | tf_op jit(solution)/shard_map/all_gather | solution.py:304
  39.7 0.4 shard_map.107
  40.1 0.0 copy-start.1
  40.1 15.2 %all_to_all.26.terms_ref = bf16[32,8,1152]{2,1,0:T(8,128)(2,1)S(1)} all-to-all(bf16[32,8,1152]{2,1,0:T(8,128)(2,1)S(1)} %shard_map.107), channel_id=1, replica_groups=mesh['batch'=16,'hist'=32] {'hist'}, dimensions={0} | all-to-all | bytes 1179648 | tf_op jit(solution)/shard_map/all_to_all | solution.py:237
  55.3 0.7 shard_map.109
  56.1 4.0 %all-to-all-start.3 = ((bf16[4,16,1152]{2,1,0:T(8,128)(2,1)}), bf16[4,16,1152]{2,1,0:T(8,128)(2,1)S(1)}, u32[]{:S(2)}, u32[]{:S(2)}) async-start(bf16[4,16,1152]{2,1,0:T(8,128)(2,1)} %shard_map.109), calls=%async_computation.3 | async-start | bytes 294912 | tf_op jit(solution)/shard_map/all_to_all | solution.py:237
  60.1 2.0 %shard_map.108 = (bf16[32,16,1536]{2,1,0:T(8,128)(2,1)S(1)}, bf16[128,768]{1,0:T(8,128)(2,1)S(1)}, bf16[128,768]{1,0:T(8,128)(2,1)}) custom-call(bf16[128,1536]{1,0:T(8,128)(2,1)S(1)} %shard_map.106.pair_ref, bf16[768,768]{1,0:T(8,128)(2,1)S(1)} %copy-done, bf16[128,512]{1,0:T(8,128)(2,1)S(1)} %copy-done.6, ...), custom_call_target="tpu_custom_call" | custom-call | tf_op jit(solution)/shard_map/pallas_call | solution.py:224
  62.1 1.2 %copy-done.2 = bf16[32,16,1536]{2,1,0:T(8,128)(2,1)} copy-done((bf16[32,16,1536]{2,1,0:T(8,128)(2,1)}, bf16[32,16,1536]{2,1,0:T(8,128)(2,1)S(1)}, u32[]{:S(2)}) %copy-start.2) | copy-done | bytes 1572888
  63.3 3.7 %all-to-all-done.3.near_ref = bf16[4,16,1152]{2,1,0:T(8,128)(2,1)S(1)} async-done(((bf16[4,16,1152]{2,1,0:T(8,128)(2,1)}), bf16[4,16,1152]{2,1,0:T(8,128)(2,1)S(1)}, u32[]{:S(2)}, u32[]{:S(2)}) %all-to-all-start.3) | async-done | bytes 147488 | tf_op jit(solution)/shard_map/all_to_all | solution.py:237
  67.0 5.8 %all-to-all-start.4 = ((bf16[32,16,1536]{2,1,0:T(8,128)(2,1)}), bf16[32,16,1536]{2,1,0:T(8,128)(2,1)S(1)}, u32[]{:S(2)}, u32[]{:S(2)}) async-start(bf16[32,16,1536]{2,1,0:T(8,128)(2,1)} %copy-done.2), calls=%async_computation.4 | async-start | bytes 3145728 | tf_op jit(solution)/shard_map/all_to_all | solution.py:237
  72.8 24.4 %all-gather.1 = bf16[64,1152]{1,0:T(8,128)(2,1)S(1)} all-gather(bf16[16,1152]{1,0:T(8,128)(2,1)S(1)} %shard_map.110), channel_id=3, replica_groups={{0,128,256,384},{32,160,288,416},{64,192,320,448},{96,224,352,480},{1,1..., dimensions={0}, use_global_device_ids=true | all-gather | bytes 184320 | tf_op jit(solution)/shard_map/all_gather | solution.py:339
  97.3 1.1 %shard_map.111 = (bf16[128,768]{1,0:T(8,128)(2,1)}, f32[24,768]{1,0:T(8,128)}) custom-call(bf16[32,16,1536]{2,1,0:T(8,128)(2,1)S(1)} %all-to-all-done.4.back_ref, bf16[512,384]{1,0:T(8,128)(2,1)S(1)} %get-tuple-element.26.pick_in.pick_ref, bf16[128,512]{1,0:T(8,128)(2,1)S(1)} %copy-done.4, bf16[128,768]{1,0:T(8,128)(2,1)S(1)} %get-tuple-element.31.mixed_ref, ...), custom_call_target="tpu_custom_call" | custom-call | tf_op jit(solution)/shard_map/pallas_call | solution.py:224
  (11 shorter events, 0.0 us)
Async XLA Ops:
  2.3 14.9 %all-to-all-start = ((s32[32,1,128]{2,1,0:T(1,128)}), s32[32,1,128]{2,1,0:T(1,128)S(1)}, u32[]{:S(2)}, u32[]{:S(2)}) async-start(s32[32,1,128]{2,1,0:T(1,128)} %shard_map.103), calls=%async_computation | async-start | bytes 32768 | tf_op jit(solution)/shard_map/all_to_all | solution.py:237
  13.7 22.2 %copy-start = (bf16[768,768]{1,0:T(8,128)(2,1)S(1)}, bf16[768,768]{1,0:T(8,128)(2,1)}, u32[]{:S(2)}) copy-start(bf16[768,768]{1,0:T(8,128)(2,1)} %weight_ref.3) | copy-start | bytes 3538948
  13.7 22.2 %copy-start.3 = (bf16[1,128,768]{2,1,0:T(8,128)(2,1)S(1)}, bf16[1,128,768]{2,1,0:T(8,128)(2,1)}, u32[]{:S(2)}) copy-start(bf16[1,128,768]{2,1,0:T(8,128)(2,1)} %param.8) | copy-start | bytes 589828
  13.7 22.2 %copy-start.5 = (bf16[1,128,768]{2,1,0:T(8,128)(2,1)S(1)}, bf16[1,128,768]{2,1,0:T(8,128)(2,1)}, u32[]{:S(2)}) copy-start(bf16[1,128,768]{2,1,0:T(8,128)(2,1)} %param.15) | copy-start | bytes 589828
  15.9 20.0 %copy-start.4 = (bf16[128,512]{1,0:T(8,128)(2,1)S(1)}, bf16[128,512]{1,0:T(8,128)(2,1)}, u32[]{:S(2)}) copy-start(bf16[128,512]{1,0:T(8,128)(2,1)} %get-tuple-element.23.all_ref) | copy-start | bytes 393220
  40.1 20.0 %copy-start.1 = (bf16[256,1536]{1,0:T(8,128)(2,1)S(1)}, bf16[256,1536]{1,0:T(8,128)(2,1)}, u32[]{:S(2)}) copy-start(bf16[256,1536]{1,0:T(8,128)(2,1)} %history_in.1) | copy-start | bytes 2359300
  40.1 20.0 %copy-start.6 = (bf16[128,512]{1,0:T(8,128)(2,1)S(1)}, bf16[128,512]{1,0:T(8,128)(2,1)}, u32[]{:S(2)}) copy-start(bf16[128,512]{1,0:T(8,128)(2,1)} %get-tuple-element.25.inside_ref) | copy-start | bytes 393220
  56.1 10.9 %all-to-all-start.3 = ((bf16[4,16,1152]{2,1,0:T(8,128)(2,1)}), bf16[4,16,1152]{2,1,0:T(8,128)(2,1)S(1)}, u32[]{:S(2)}, u32[]{:S(2)}) async-start(bf16[4,16,1152]{2,1,0:T(8,128)(2,1)} %shard_map.109), calls=%async_computation.3 | async-start | bytes 294912 | tf_op jit(solution)/shard_map/all_to_all | solution.py:237
  62.1 1.2 %copy-start.2 = (bf16[32,16,1536]{2,1,0:T(8,128)(2,1)}, bf16[32,16,1536]{2,1,0:T(8,128)(2,1)S(1)}, u32[]{:S(2)}) copy-start(bf16[32,16,1536]{2,1,0:T(8,128)(2,1)S(1)} %get-tuple-element.30) | copy-start | bytes 4718596
  67.0 30.2 %all-to-all-start.4 = ((bf16[32,16,1536]{2,1,0:T(8,128)(2,1)}), bf16[32,16,1536]{2,1,0:T(8,128)(2,1)S(1)}, u32[]{:S(2)}, u32[]{:S(2)}) async-start(bf16[32,16,1536]{2,1,0:T(8,128)(2,1)} %copy-done.2), calls=%async_computation.4 | async-start | bytes 3145728 | tf_op jit(solution)/shard_map/all_to_all | solution.py:237

commit v10 on v8

--- a/solution.py
+++ b/solution.py
@@ -59,11 +59,10 @@
     named, place = slot_places(owners, peers, earlier)
     spot = lax.broadcasted_iota(jnp.int32, (LANES, rows.shape[1]), 0) == place
     spot = jnp.where(spot, 1.0, 0.0).astype(BF16)
-    low = (rows % LANES).astype(F32)
-    high = (rows // LANES).astype(F32)
-    ids = dot((named * low).astype(BF16), spot, ROWS_T) + LANES * dot(
-        (named * high).astype(BF16), spot, ROWS_T
-    )
+    low = named * (rows % LANES).astype(F32)
+    high = named * (rows // LANES).astype(F32)
+    ids = dot(jnp.concatenate([low, high], axis=0).astype(BF16), spot, ROWS_T)
+    ids = ids[:peers] + LANES * ids[peers:]
     ids_ref[...] = ids.astype(jnp.int32).reshape(ids_ref.shape)
 
 
@@ -128,21 +127,34 @@
     pair_ref[:, width:] = grad_pre
 
 
-def term_kernel(peers, width, pairs_ref, term_ref):
+def term_kernel(peers, width, pairs_ref, term_out, term_ref, sems):
     half = width // 2
     second_core = lax.axis_index("hist") % 2 == 1
     pairs = pairs_ref[...].reshape(-1, 2 * width)
-    mixed = pairs[:, :width]
     left, right = pairs[:, width : width + half], pairs[:, width + half :]
     grad_pre = jnp.where(second_core, right, left)
     share = width // peers
     step = 8
-    term = dot(mixed, grad_pre, COLS_T)
-    for peer in range(peers):
-        blocks = [
-            term[peer * share + i : peer * share + i + step, :] for i in range(0, share, step)
-        ]
-        term_ref[peer] = jnp.concatenate(blocks, axis=1).astype(BF16)
+    copies = []
+    terms = dot(pairs[:, :width], grad_pre, COLS_T)
+    for part in range(2):
+        term = terms[part * half : (part + 1) * half, :]
+        first = part * (peers // 2)
+        for peer in range(peers // 2):
+            blocks = [
+                term[peer * share + i : peer * share + i + step, :] for i in range(0, share, step)
+            ]
+            term_ref[first + peer] = jnp.concatenate(blocks, axis=1).astype(BF16)
+        copies.append(
+            pltpu.make_async_copy(
+                term_ref.at[first : first + peers // 2],
+                term_out.at[first : first + peers // 2],
+                sems.at[part],
+            )
+        )
+        copies[-1].start()
+    for copy in copies:
+        copy.wait()
 
 
 def backward_kernel(
@@ -306,6 +318,11 @@
         functools.partial(term_kernel, peers, width),
         shape((peers, 8, share * width // 16), BF16),
         pairs,
+        hbm_out=(0,),
+        scratch=(
+            pltpu.VMEM((peers, 8, share * width // 16), BF16),
+            pltpu.SemaphoreType.DMA((2,)),
+        ),
     )
     pair, terms = lax.optimization_barrier((pair, terms))
     terms = swap(terms)

time: 99.4 us -> 99.3 us (level)
  no operation moved by 1% of the time
where the time goes in v10:
time: 99.3 us; the launch traced here: 98.8 us
  blocking collectives  56.8 us (57%)
  starting transfers between devices  20.4 us (21%)
  Pallas kernels  9.38 us (9%)
  waiting for transfers between devices  6.65 us (7%)
  local copies, waits for them, and re-layouts  3.8 us (4%)
    all_to_all x2, blocking collectives, swap(): lax.all_to_all(values, axis, split_axis=0, concat_axis=0, tiled=True, axi...  29.5 us
    all_gather x1, blocking collectives, body(): term = lax.all_gather(term, 'batch', axis=0, axis_index_groups=far)  24.1 us
    all_to_all x3, starting transfers between devices, swap(): lax.all_to_all(values, axis, split_axis=0, concat_axis=0, tiled=True, axi...  20.4 us
    pallas_call x9, Pallas kernels, call(): pl.pallas_call(kernel, out_shape=out_shape, in_specs=[pl.BlockSpec(memory...  9.38 us
    all_to_all x3, waiting for transfers between devices, swap(): lax.all_to_all(values, axis, split_axis=0, concat_axis=0, tiled=True, axi...  6.65 us
    all_gather x1, blocking collectives, body(): pairs = lax.all_gather(pair, 'hist', axis=0, axis_index_groups=chips)  3.22 us
    unnamed x18, local copies, waits for them, and re-layouts  2.77 us
  transfers between devices with their start and end apart: 3, of which 2 were waited for; matrix products, arithmetic and copies ran while one was open for 2% of the time, Pallas kernels for 4%

profile of v10, /device:TPU:6, one launch (start us, length us, event | category | flops | bytes accessed | tf_op | source)
XLA Modules:
  0.0 98.8 jit_solution(12505365746290256420)
XLA Ops:
  0.6 1.7 %shard_map.103 = s32[32,1,128]{2,1,0:T(1,128)} custom-call(s32[1,2]{1,0:T(1,128)} %tile_in.3, s32[1,256]{1,0:T(1,128)} %bitcast.14, s32[1,256]{1,0:T(1,128)} %row_in.3), custom_call_target="tpu_custom_call" | custom-call | tf_op jit(solution)/shard_map/pallas_call | solution.py:236
  2.3 9.4 %all-to-all-start = ((s32[32,1,128]{2,1,0:T(1,128)}), s32[32,1,128]{2,1,0:T(1,128)S(1)}, u32[]{:S(2)}, u32[]{:S(2)}) async-start(s32[32,1,128]{2,1,0:T(1,128)} %shard_map.103), calls=%async_computation | async-start | bytes 32768 | tf_op jit(solution)/shard_map/all_to_all | solution.py:249
  11.7 1.0 %slice.3 = bf16[256,768]{1,0:T(8,128)(2,1)S(1)} slice(bf16[256,1536]{1,0:T(8,128)(2,1)} %history_in.1), slice={[0:256], [0:768]} | slice | bytes 786432 | tf_op jit(solution)/shard_map/slice | solution.py:303
  12.7 1.0 pad_maximum_fusion.table_ref
  13.7 0.0 copy-start
  13.7 0.0 copy-start.5
  13.7 2.2 %shard_map.104 = (bf16[128,512]{1,0:T(8,128)(2,1)}, bf16[128,512]{1,0:T(8,128)(2,1)}) custom-call(s32[1,2]{1,0:T(1,128)} %tile_in.3, s32[1,256]{1,0:T(1,128)} %bitcast.15, s32[1,256]{1,0:T(1,128)} %row_in.3, bf16[128,256]{1,0:T(8,128)(2,1)} %bitcast.13), custom_call_target="tpu_custom_call" | custom-call | tf_op jit(solution)/shard_map/pallas_call | solution.py:236
  15.9 1.3 %all-to-all-done.ids_ref = s32[32,1,128]{2,1,0:T(1,128)S(1)} async-done(((s32[32,1,128]{2,1,0:T(1,128)}), s32[32,1,128]{2,1,0:T(1,128)S(1)}, u32[]{:S(2)}, u32[]{:S(2)}) %all-to-all-start) | async-done | bytes 16416 | tf_op jit(solution)/shard_map/all_to_all | solution.py:249
  17.2 0.7 shard_map.105
  17.9 18.0 %all_to_all.25.pulled_ref = bf16[32,16,768]{2,1,0:T(8,128)(2,1)S(1)} all-to-all(bf16[32,16,768]{2,1,0:T(8,128)(2,1)S(1)} %get-tuple-element.24), channel_id=1, replica_groups=mesh['batch'=16,'hist'=32] {'hist'}, dimensions={0} | all-to-all | bytes 1572864 | tf_op jit(solution)/shard_map/all_to_all | solution.py:249
  35.9 0.5 shard_map.106.pair_ref
  36.4 3.2 %all-gather = bf16[256,1536]{1,0:T(8,128)(2,1)S(1)} all-gather(bf16[128,1536]{1,0:T(8,128)(2,1)S(1)} %shard_map.106.pair_ref), channel_id=2, replica_groups={{0,1},{2,3},{4,5},{6,7},{8,9},{10,11},{12,13},{14,15},{16,17},{18,19},{..., dimensions={0}, use_global_device_ids=true | all-gather | bytes 1179648 | tf_op jit(solution)/shard_map/all_gather | solution.py:316
  39.7 1.1 %shard_map.107 = bf16[32,8,1152]{2,1,0:T(8,128)(2,1)} custom-call(bf16[2,128,1536]{2,1,0:T(8,128)(2,1)S(1)} %bitcast.8), custom_call_target="tpu_custom_call" | custom-call | tf_op jit(solution)/shard_map/pallas_call | solution.py:236
  40.8 5.5 %all-to-all-start.2 = ((bf16[32,8,1152]{2,1,0:T(8,128)(2,1)}), bf16[32,8,1152]{2,1,0:T(8,128)(2,1)S(1)}, u32[]{:S(2)}, u32[]{:S(2)}) async-start(bf16[32,8,1152]{2,1,0:T(8,128)(2,1)} %shard_map.107), calls=%async_computation.2 | async-start | bytes 1179648 | tf_op jit(solution)/shard_map/all_to_all | solution.py:249
  46.4 0.9 copy-done.8
  47.3 2.0 %shard_map.108 = (bf16[32,16,1536]{2,1,0:T(8,128)(2,1)S(1)}, bf16[128,768]{1,0:T(8,128)(2,1)S(1)}, bf16[128,768]{1,0:T(8,128)(2,1)}) custom-call(bf16[128,1536]{1,0:T(8,128)(2,1)S(1)} %shard_map.106.pair_ref, bf16[768,768]{1,0:T(8,128)(2,1)S(1)} %copy-done, bf16[128,512]{1,0:T(8,128)(2,1)S(1)} %copy-done.8, ...), custom_call_target="tpu_custom_call" | custom-call | tf_op jit(solution)/shard_map/pallas_call | solution.py:236
  49.3 1.2 %copy-done.2 = bf16[32,16,1536]{2,1,0:T(8,128)(2,1)} copy-done((bf16[32,16,1536]{2,1,0:T(8,128)(2,1)}, bf16[32,16,1536]{2,1,0:T(8,128)(2,1)S(1)}, u32[]{:S(2)}) %copy-start.2) | copy-done | bytes 1572888
  50.4 0.7 copy-done.6
  51.1 5.3 %all-to-all-done.2.terms_ref = bf16[32,8,1152]{2,1,0:T(8,128)(2,1)S(1)} async-done(((bf16[32,8,1152]{2,1,0:T(8,128)(2,1)}), bf16[32,8,1152]{2,1,0:T(8,128)(2,1)S(1)}, u32[]{:S(2)}, u32[]{:S(2)}) %all-to-all-start.2) | async-done | bytes 589856 | tf_op jit(solution)/shard_map/all_to_all | solution.py:249
  56.5 0.1 shard_map.109
  56.5 11.5 %all_to_all.26.near_ref = bf16[4,16,1152]{2,1,0:T(8,128)(2,1)S(1)} all-to-all(bf16[4,16,1152]{2,1,0:T(8,128)(2,1)S(1)} %shard_map.109), channel_id=1, replica_groups={{0,32,64,96},{128,160,192,224},{256,288,320,352},{384,416,448,480},{1,3..., dimensions={0} | all-to-all | bytes 294912 | tf_op jit(solution)/shard_map/all_to_all | solution.py:249
  68.0 5.5 %all-to-all-start.4 = ((bf16[32,16,1536]{2,1,0:T(8,128)(2,1)}), bf16[32,16,1536]{2,1,0:T(8,128)(2,1)S(1)}, u32[]{:S(2)}, u32[]{:S(2)}) async-start(bf16[32,16,1536]{2,1,0:T(8,128)(2,1)} %copy-done.2), calls=%async_computation.4 | async-start | bytes 3145728 | tf_op jit(solution)/shard_map/all_to_all | solution.py:249
  73.6 24.1 %all-gather.1 = bf16[64,1152]{1,0:T(8,128)(2,1)S(1)} all-gather(bf16[16,1152]{1,0:T(8,128)(2,1)S(1)} %shard_map.110), channel_id=3, replica_groups={{0,128,256,384},{32,160,288,416},{64,192,320,448},{96,224,352,480},{1,1..., dimensions={0}, use_global_device_ids=true | all-gather | bytes 184320 | tf_op jit(solution)/shard_map/all_gather | solution.py:357
  97.7 1.1 %shard_map.111 = (bf16[128,768]{1,0:T(8,128)(2,1)}, f32[24,768]{1,0:T(8,128)}) custom-call(bf16[32,16,1536]{2,1,0:T(8,128)(2,1)S(1)} %all-to-all-done.4.back_ref, bf16[512,384]{1,0:T(8,128)(2,1)S(1)} %get-tuple-element.28.pick_in.pick_ref, bf16[128,512]{1,0:T(8,128)(2,1)S(1)} %copy-done.4, bf16[128,768]{1,0:T(8,128)(2,1)S(1)} %copy-done.7, ...), custom_call_target="tpu_custom_call" | custom-call | tf_op jit(solution)/shard_map/pallas_call | solution.py:236
  (15 shorter events, 0.1 us)
Async XLA Ops:
  2.3 14.9 %all-to-all-start = ((s32[32,1,128]{2,1,0:T(1,128)}), s32[32,1,128]{2,1,0:T(1,128)S(1)}, u32[]{:S(2)}, u32[]{:S(2)}) async-start(s32[32,1,128]{2,1,0:T(1,128)} %shard_map.103), calls=%async_computation | async-start | bytes 32768 | tf_op jit(solution)/shard_map/all_to_all | solution.py:249
  13.7 22.2 %copy-start = (bf16[768,768]{1,0:T(8,128)(2,1)S(1)}, bf16[768,768]{1,0:T(8,128)(2,1)}, u32[]{:S(2)}) copy-start(bf16[768,768]{1,0:T(8,128)(2,1)} %weight_ref.3) | copy-start | bytes 3538948
  13.7 22.2 %copy-start.3 = (bf16[1,128,768]{2,1,0:T(8,128)(2,1)S(1)}, bf16[1,128,768]{2,1,0:T(8,128)(2,1)}, u32[]{:S(2)}) copy-start(bf16[1,128,768]{2,1,0:T(8,128)(2,1)} %param.8) | copy-start | bytes 589828
  13.7 22.2 %copy-start.5 = (bf16[1,128,768]{2,1,0:T(8,128)(2,1)S(1)}, bf16[1,128,768]{2,1,0:T(8,128)(2,1)}, u32[]{:S(2)}) copy-start(bf16[1,128,768]{2,1,0:T(8,128)(2,1)} %param.15) | copy-start | bytes 589828
  15.9 20.0 %copy-start.4 = (bf16[128,512]{1,0:T(8,128)(2,1)S(1)}, bf16[128,512]{1,0:T(8,128)(2,1)}, u32[]{:S(2)}) copy-start(bf16[128,512]{1,0:T(8,128)(2,1)} %get-tuple-element.25.all_ref) | copy-start | bytes 393220
  39.7 6.7 %copy-start.1 = (bf16[256,1536]{1,0:T(8,128)(2,1)S(1)}, bf16[256,1536]{1,0:T(8,128)(2,1)}, u32[]{:S(2)}) copy-start(bf16[256,1536]{1,0:T(8,128)(2,1)} %history_in.1) | copy-start | bytes 2359300
  40.8 15.6 %all-to-all-start.2 = ((bf16[32,8,1152]{2,1,0:T(8,128)(2,1)}), bf16[32,8,1152]{2,1,0:T(8,128)(2,1)S(1)}, u32[]{:S(2)}, u32[]{:S(2)}) async-start(bf16[32,8,1152]{2,1,0:T(8,128)(2,1)} %shard_map.107), calls=%async_computation.2 | async-start | bytes 1179648 | tf_op jit(solution)/shard_map/all_to_all | solution.py:249
  46.4 0.9 copy-start.8
  49.3 1.2 %copy-start.2 = (bf16[32,16,1536]{2,1,0:T(8,128)(2,1)}, bf16[32,16,1536]{2,1,0:T(8,128)(2,1)S(1)}, u32[]{:S(2)}) copy-start(bf16[32,16,1536]{2,1,0:T(8,128)(2,1)S(1)} %get-tuple-element.34) | copy-start | bytes 4718596
  50.4 0.7 copy-start.6
  68.0 29.7 %copy-start.7 = (bf16[128,768]{1,0:T(8,128)(2,1)S(1)}, bf16[128,768]{1,0:T(8,128)(2,1)}, u32[]{:S(2)}) copy-start(bf16[128,768]{1,0:T(8,128)(2,1)} %copy-done.6) | copy-start | bytes 589828
  68.0 29.7 %all-to-all-start.4 = ((bf16[32,16,1536]{2,1,0:T(8,128)(2,1)}), bf16[32,16,1536]{2,1,0:T(8,128)(2,1)S(1)}, u32[]{:S(2)}, u32[]{:S(2)}) async-start(bf16[32,16,1536]{2,1,0:T(8,128)(2,1)} %copy-done.2), calls=%async_computation.4 | async-start | bytes 3145728 | tf_op jit(solution)/shard_map/all_to_all | solution.py:249

commit v11 on v10

--- a/solution.py
+++ b/solution.py
@@ -194,9 +194,7 @@
         total = terms_ref[core].astype(F32)
         for peer in range(core + 2, peers, 2):
             total = total + terms_ref[peer].astype(F32)
-        total = total.astype(BF16)
-        for plane in range(sum_ref.shape[0]):
-            sum_ref[plane, core * step : (core + 1) * step, :] = total
+        sum_ref[core * step : (core + 1) * step, :] = total.astype(BF16)
 
 
 def add_kernel(near_ref, sum_ref):
@@ -346,13 +344,13 @@
         ),
     )
     sent, terms = lax.optimization_barrier((sent, terms))
+    back = swap(sent)
     side = 4
-    near = [[a * side + i for i in range(side)] for a in range(planes // side)]
-    term = call(weight_kernel, shape((side, 16, share * width // 16), BF16), terms)
-    term = swap(term, "batch", near)
-    sent, term = lax.optimization_barrier((sent, term))
-    back = swap(sent)
-    term = call(add_kernel, shape(term.shape[1:], BF16), term)
+    term = call(weight_kernel, shape((16, share * width // 16), BF16), terms)
+    for bit in (1, 2):
+        twins = [[i, i + bit] for i in range(planes) if not i & bit]
+        term = lax.all_gather(term, "batch", axis=0, axis_index_groups=twins)
+        term = call(add_kernel, shape(term.shape[1:], BF16), term)
     far = [[a + side * i for i in range(planes // side)] for a in range(side)]
     term = lax.all_gather(term, "batch", axis=0, axis_index_groups=far)
     grad_rows, weight_share = call(

time: 99.3 us -> 98.9 us (level)
  blocking collectives: 56.8 us -> 55.5 us
    all_to_all x2 -> x1, blocking collectives: 29.5 us -> 18 us  [swap(): lax.all_to_all(values, axis, split_axis=0, concat_axis=0, tiled=True, axi...]
    all_gather x0 -> x2, blocking collectives: none -> 10.4 us  [body(): term = lax.all_gather(term, 'batch', axis=0, axis_index_groups=twins)]
    pallas_call x9 -> x10, Pallas kernels: 9.38 us -> 9.38 us  [call(): pl.pallas_call(kernel, out_shape=out_shape, in_specs=[pl.BlockSpec(memory...]
where the time goes in v11:
time: 98.9 us; the launch traced here: 98.4 us
  blocking collectives  55.5 us (56%)
  starting transfers between devices  21.3 us (22%)
  Pallas kernels  9.38 us (9%)
  waiting for transfers between devices  6.65 us (7%)
  local copies, waits for them, and re-layouts  3.8 us (4%)
    all_gather x1, blocking collectives, body(): term = lax.all_gather(term, 'batch', axis=0, axis_index_groups=far)  24 us
    all_to_all x3, starting transfers between devices, swap(): lax.all_to_all(values, axis, split_axis=0, concat_axis=0, tiled=True, axi...  21.3 us
    all_to_all x1, blocking collectives, swap(): lax.all_to_all(values, axis, split_axis=0, concat_axis=0, tiled=True, axi...  18 us
    all_gather x2, blocking collectives, body(): term = lax.all_gather(term, 'batch', axis=0, axis_index_groups=twins)  10.4 us
    pallas_call x10, Pallas kernels, call(): pl.pallas_call(kernel, out_shape=out_shape, in_specs=[pl.BlockSpec(memory...  9.38 us
    all_to_all x3, waiting for transfers between devices, swap(): lax.all_to_all(values, axis, split_axis=0, concat_axis=0, tiled=True, axi...  6.65 us
    all_gather x1, blocking collectives, body(): pairs = lax.all_gather(pair, 'hist', axis=0, axis_index_groups=chips)  3.22 us
    unnamed x18, local copies, waits for them, and re-layouts  2.77 us
  transfers between devices with their start and end apart: 3, of which 2 were waited for; matrix products, arithmetic and copies ran while one was open for 2% of the time, Pallas kernels for 4%

profile of v11, /device:TPU:6, one launch (start us, length us, event | category | flops | bytes accessed | tf_op | source)
XLA Modules:
  0.0 98.4 jit_solution(6525253302751872036)
XLA Ops:
  0.6 1.7 %shard_map.103 = s32[32,1,128]{2,1,0:T(1,128)} custom-call(s32[1,2]{1,0:T(1,128)} %tile_in.3, s32[1,256]{1,0:T(1,128)} %bitcast.18, s32[1,256]{1,0:T(1,128)} %row_in.3), custom_call_target="tpu_custom_call" | custom-call | tf_op jit(solution)/shard_map/pallas_call | solution.py:234
  2.3 9.4 %all-to-all-start = ((s32[32,1,128]{2,1,0:T(1,128)}), s32[32,1,128]{2,1,0:T(1,128)S(1)}, u32[]{:S(2)}, u32[]{:S(2)}) async-start(s32[32,1,128]{2,1,0:T(1,128)} %shard_map.103), calls=%async_computation | async-start | bytes 32768 | tf_op jit(solution)/shard_map/all_to_all | solution.py:247
  11.7 1.0 %slice.3 = bf16[256,768]{1,0:T(8,128)(2,1)S(1)} slice(bf16[256,1536]{1,0:T(8,128)(2,1)} %history_in.1), slice={[0:256], [0:768]} | slice | bytes 786432 | tf_op jit(solution)/shard_map/slice | solution.py:301
  12.7 1.0 pad_maximum_fusion.table_ref
  13.7 0.0 copy-start.5
  13.7 2.2 %shard_map.104 = (bf16[128,512]{1,0:T(8,128)(2,1)}, bf16[128,512]{1,0:T(8,128)(2,1)}) custom-call(s32[1,2]{1,0:T(1,128)} %tile_in.3, s32[1,256]{1,0:T(1,128)} %bitcast.19, s32[1,256]{1,0:T(1,128)} %row_in.3, bf16[128,256]{1,0:T(8,128)(2,1)} %bitcast.17), custom_call_target="tpu_custom_call" | custom-call | tf_op jit(solution)/shard_map/pallas_call | solution.py:234
  15.9 1.3 %all-to-all-done.ids_ref = s32[32,1,128]{2,1,0:T(1,128)S(1)} async-done(((s32[32,1,128]{2,1,0:T(1,128)}), s32[32,1,128]{2,1,0:T(1,128)S(1)}, u32[]{:S(2)}, u32[]{:S(2)}) %all-to-all-start) | async-done | bytes 16416 | tf_op jit(solution)/shard_map/all_to_all | solution.py:247
  17.2 0.7 shard_map.105
  17.9 18.0 %all_to_all.20.pulled_ref = bf16[32,16,768]{2,1,0:T(8,128)(2,1)S(1)} all-to-all(bf16[32,16,768]{2,1,0:T(8,128)(2,1)S(1)} %get-tuple-element.22), channel_id=1, replica_groups=mesh['batch'=16,'hist'=32] {'hist'}, dimensions={0} | all-to-all | bytes 1572864 | tf_op jit(solution)/shard_map/all_to_all | solution.py:247
  35.9 0.5 shard_map.106.pair_ref
  36.4 3.2 %all-gather = bf16[256,1536]{1,0:T(8,128)(2,1)S(1)} all-gather(bf16[128,1536]{1,0:T(8,128)(2,1)S(1)} %shard_map.106.pair_ref), channel_id=2, replica_groups={{0,1},{2,3},{4,5},{6,7},{8,9},{10,11},{12,13},{14,15},{16,17},{18,19},{..., dimensions={0}, use_global_device_ids=true | all-gather | bytes 1179648 | tf_op jit(solution)/shard_map/all_gather | solution.py:314
  39.7 1.1 %shard_map.107 = bf16[32,8,1152]{2,1,0:T(8,128)(2,1)} custom-call(bf16[2,128,1536]{2,1,0:T(8,128)(2,1)S(1)} %bitcast.10), custom_call_target="tpu_custom_call" | custom-call | tf_op jit(solution)/shard_map/pallas_call | solution.py:234
  40.8 5.5 %all-to-all-start.2 = ((bf16[32,8,1152]{2,1,0:T(8,128)(2,1)}), bf16[32,8,1152]{2,1,0:T(8,128)(2,1)S(1)}, u32[]{:S(2)}, u32[]{:S(2)}) async-start(bf16[32,8,1152]{2,1,0:T(8,128)(2,1)} %shard_map.107), calls=%async_computation.2 | async-start | bytes 1179648 | tf_op jit(solution)/shard_map/all_to_all | solution.py:247
  46.4 0.9 copy-done.8
  47.3 2.0 %shard_map.108 = (bf16[32,16,1536]{2,1,0:T(8,128)(2,1)S(1)}, bf16[128,768]{1,0:T(8,128)(2,1)S(1)}, bf16[128,768]{1,0:T(8,128)(2,1)}) custom-call(bf16[128,1536]{1,0:T(8,128)(2,1)S(1)} %shard_map.106.pair_ref, bf16[768,768]{1,0:T(8,128)(2,1)S(1)} %copy-done, bf16[128,512]{1,0:T(8,128)(2,1)S(1)} %copy-done.8, ...), custom_call_target="tpu_custom_call" | custom-call | tf_op jit(solution)/shard_map/pallas_call | solution.py:234
  49.3 1.2 %copy-done.2 = bf16[32,16,1536]{2,1,0:T(8,128)(2,1)} copy-done((bf16[32,16,1536]{2,1,0:T(8,128)(2,1)}, bf16[32,16,1536]{2,1,0:T(8,128)(2,1)S(1)}, u32[]{:S(2)}) %copy-start.2) | copy-done | bytes 1572888
  50.4 0.7 copy-done.6
  51.1 5.3 %all-to-all-done.2.terms_ref = bf16[32,8,1152]{2,1,0:T(8,128)(2,1)S(1)} async-done(((bf16[32,8,1152]{2,1,0:T(8,128)(2,1)}), bf16[32,8,1152]{2,1,0:T(8,128)(2,1)S(1)}, u32[]{:S(2)}, u32[]{:S(2)}) %all-to-all-start.2) | async-done | bytes 589856 | tf_op jit(solution)/shard_map/all_to_all | solution.py:247
  56.5 6.4 %all-to-all-start.3 = ((bf16[32,16,1536]{2,1,0:T(8,128)(2,1)}), bf16[32,16,1536]{2,1,0:T(8,128)(2,1)S(1)}, u32[]{:S(2)}, u32[]{:S(2)}) async-start(bf16[32,16,1536]{2,1,0:T(8,128)(2,1)} %copy-done.2), calls=%async_computation.3 | async-start | bytes 3145728 | tf_op jit(solution)/shard_map/all_to_all | solution.py:247
  62.9 0.1 shard_map.109
  63.0 4.6 %all-gather.1 = bf16[32,1152]{1,0:T(8,128)(2,1)S(1)} all-gather(bf16[16,1152]{1,0:T(8,128)(2,1)S(1)} %shard_map.109), channel_id=3, replica_groups={{0,32},{64,96},{128,160},{192,224},{256,288},{320,352},{384,416},{448,4..., dimensions={0}, use_global_device_ids=true | all-gather | bytes 110592 | tf_op jit(solution)/shard_map/all_gather | solution.py:352
  67.6 5.7 %all-gather.2 = bf16[32,1152]{1,0:T(8,128)(2,1)S(1)} all-gather(bf16[16,1152]{1,0:T(8,128)(2,1)S(1)} %shard_map.110), channel_id=4, replica_groups={{0,64},{32,96},{128,192},{160,224},{256,320},{288,352},{384,448},{416,4..., dimensions={0}, use_global_device_ids=true | all-gather | bytes 110592 | tf_op jit(solution)/shard_map/all_gather | solution.py:352
  73.4 24.0 %all-gather.3 = bf16[64,1152]{1,0:T(8,128)(2,1)S(1)} all-gather(bf16[16,1152]{1,0:T(8,128)(2,1)S(1)} %shard_map.111), channel_id=5, replica_groups={{0,128,256,384},{32,160,288,416},{64,192,320,448},{96,224,352,480},{1,1..., dimensions={0}, use_global_device_ids=true | all-gather | bytes 184320 | tf_op jit(solution)/shard_map/all_gather | solution.py:355
  97.3 1.1 %shard_map.112 = (bf16[128,768]{1,0:T(8,128)(2,1)}, f32[24,768]{1,0:T(8,128)}) custom-call(bf16[32,16,1536]{2,1,0:T(8,128)(2,1)S(1)} %all-to-all-done.3.back_ref, bf16[512,384]{1,0:T(8,128)(2,1)S(1)} %get-tuple-element.26.pick_in.pick_ref, bf16[128,512]{1,0:T(8,128)(2,1)S(1)} %copy-done.4, bf16[128,768]{1,0:T(8,128)(2,1)S(1)} %copy-done.7, ...), custom_call_target="tpu_custom_call" | custom-call | tf_op jit(solution)/shard_map/pallas_call | solution.py:234
  (17 shorter events, 0.1 us)
Async XLA Ops:
  2.3 14.9 %all-to-all-start = ((s32[32,1,128]{2,1,0:T(1,128)}), s32[32,1,128]{2,1,0:T(1,128)S(1)}, u32[]{:S(2)}, u32[]{:S(2)}) async-start(s32[32,1,128]{2,1,0:T(1,128)} %shard_map.103), calls=%async_computation | async-start | bytes 32768 | tf_op jit(solution)/shard_map/all_to_all | solution.py:247
  13.7 22.2 %copy-start = (bf16[768,768]{1,0:T(8,128)(2,1)S(1)}, bf16[768,768]{1,0:T(8,128)(2,1)}, u32[]{:S(2)}) copy-start(bf16[768,768]{1,0:T(8,128)(2,1)} %weight_ref.3) | copy-start | bytes 3538948
  13.7 22.2 %copy-start.3 = (bf16[1,128,768]{2,1,0:T(8,128)(2,1)S(1)}, bf16[1,128,768]{2,1,0:T(8,128)(2,1)}, u32[]{:S(2)}) copy-start(bf16[1,128,768]{2,1,0:T(8,128)(2,1)} %param.8) | copy-start | bytes 589828
  13.7 22.2 %copy-start.5 = (bf16[1,128,768]{2,1,0:T(8,128)(2,1)S(1)}, bf16[1,128,768]{2,1,0:T(8,128)(2,1)}, u32[]{:S(2)}) copy-start(bf16[1,128,768]{2,1,0:T(8,128)(2,1)} %param.15) | copy-start | bytes 589828
  15.9 20.0 %copy-start.4 = (bf16[128,512]{1,0:T(8,128)(2,1)S(1)}, bf16[128,512]{1,0:T(8,128)(2,1)}, u32[]{:S(2)}) copy-start(bf16[128,512]{1,0:T(8,128)(2,1)} %get-tuple-element.23.all_ref) | copy-start | bytes 393220
  39.7 6.7 %copy-start.1 = (bf16[256,1536]{1,0:T(8,128)(2,1)S(1)}, bf16[256,1536]{1,0:T(8,128)(2,1)}, u32[]{:S(2)}) copy-start(bf16[256,1536]{1,0:T(8,128)(2,1)} %history_in.1) | copy-start | bytes 2359300
  40.8 15.6 %all-to-all-start.2 = ((bf16[32,8,1152]{2,1,0:T(8,128)(2,1)}), bf16[32,8,1152]{2,1,0:T(8,128)(2,1)S(1)}, u32[]{:S(2)}, u32[]{:S(2)}) async-start(bf16[32,8,1152]{2,1,0:T(8,128)(2,1)} %shard_map.107), calls=%async_computation.2 | async-start | bytes 1179648 | tf_op jit(solution)/shard_map/all_to_all | solution.py:247
  46.4 0.9 copy-start.8
  49.3 1.2 %copy-start.2 = (bf16[32,16,1536]{2,1,0:T(8,128)(2,1)}, bf16[32,16,1536]{2,1,0:T(8,128)(2,1)S(1)}, u32[]{:S(2)}) copy-start(bf16[32,16,1536]{2,1,0:T(8,128)(2,1)S(1)} %get-tuple-element.30) | copy-start | bytes 4718596
  50.4 0.7 copy-start.6
  56.5 40.9 %all-to-all-start.3 = ((bf16[32,16,1536]{2,1,0:T(8,128)(2,1)}), bf16[32,16,1536]{2,1,0:T(8,128)(2,1)S(1)}, u32[]{:S(2)}, u32[]{:S(2)}) async-start(bf16[32,16,1536]{2,1,0:T(8,128)(2,1)} %copy-done.2), calls=%async_computation.3 | async-start | bytes 3145728 | tf_op jit(solution)/shard_map/all_to_all | solution.py:247
  62.9 34.5 %copy-start.7 = (bf16[128,768]{1,0:T(8,128)(2,1)S(1)}, bf16[128,768]{1,0:T(8,128)(2,1)}, u32[]{:S(2)}) copy-start(bf16[128,768]{1,0:T(8,128)(2,1)} %copy-done.6) | copy-start | bytes 589828

commit v12 on v11

--- a/solution.py
+++ b/solution.py
@@ -351,7 +351,8 @@
         twins = [[i, i + bit] for i in range(planes) if not i & bit]
         term = lax.all_gather(term, "batch", axis=0, axis_index_groups=twins)
         term = call(add_kernel, shape(term.shape[1:], BF16), term)
-    far = [[a + side * i for i in range(planes // side)] for a in range(side)]
+    late = planes // 2
+    far = [[(late + a + side * i) % planes for i in range(planes // side)] for a in range(side)]
     term = lax.all_gather(term, "batch", axis=0, axis_index_groups=far)
     grad_rows, weight_share = call(
         final_kernel,

time: 98.9 us -> 98.9 us (level)
  no operation moved by 1% of the time
where the time goes in v12:
time: 98.9 us; the launch traced here: 98.4 us
  blocking collectives  55.5 us (56%)
  starting transfers between devices  21.3 us (22%)
  Pallas kernels  9.38 us (9%)
  waiting for transfers between devices  6.65 us (7%)
  local copies, waits for them, and re-layouts  3.8 us (4%)
    all_gather x1, blocking collectives, body(): term = lax.all_gather(term, 'batch', axis=0, axis_index_groups=far)  24 us
    all_to_all x3, starting transfers between devices, swap(): lax.all_to_all(values, axis, split_axis=0, concat_axis=0, tiled=True, axi...  21.3 us
    all_to_all x1, blocking collectives, swap(): lax.all_to_all(values, axis, split_axis=0, concat_axis=0, tiled=True, axi...  18 us
    all_gather x2, blocking collectives, body(): term = lax.all_gather(term, 'batch', axis=0, axis_index_groups=twins)  10.4 us
    pallas_call x10, Pallas kernels, call(): pl.pallas_call(kernel, out_shape=out_shape, in_specs=[pl.BlockSpec(memory...  9.38 us
    all_to_all x3, waiting for transfers between devices, swap(): lax.all_to_all(values, axis, split_axis=0, concat_axis=0, tiled=True, axi...  6.65 us
    all_gather x1, blocking collectives, body(): pairs = lax.all_gather(pair, 'hist', axis=0, axis_index_groups=chips)  3.22 us
    unnamed x18, local copies, waits for them, and re-layouts  2.77 us
  transfers between devices with their start and end apart: 3, of which 2 were waited for; matrix products, arithmetic and copies ran while one was open for 2% of the time, Pallas kernels for 4%

profile of v12, /device:TPU:6, one launch (start us, length us, event | category | flops | bytes accessed | tf_op | source)
XLA Modules:
  0.0 98.4 jit_solution(10551269883317125628)
XLA Ops:
  0.6 1.7 %shard_map.103 = s32[32,1,128]{2,1,0:T(1,128)} custom-call(s32[1,2]{1,0:T(1,128)} %tile_in.3, s32[1,256]{1,0:T(1,128)} %bitcast.18, s32[1,256]{1,0:T(1,128)} %row_in.3), custom_call_target="tpu_custom_call" | custom-call | tf_op jit(solution)/shard_map/pallas_call | solution.py:234
  2.3 9.4 %all-to-all-start = ((s32[32,1,128]{2,1,0:T(1,128)}), s32[32,1,128]{2,1,0:T(1,128)S(1)}, u32[]{:S(2)}, u32[]{:S(2)}) async-start(s32[32,1,128]{2,1,0:T(1,128)} %shard_map.103), calls=%async_computation | async-start | bytes 32768 | tf_op jit(solution)/shard_map/all_to_all | solution.py:247
  11.7 1.0 %slice.3 = bf16[256,768]{1,0:T(8,128)(2,1)S(1)} slice(bf16[256,1536]{1,0:T(8,128)(2,1)} %history_in.1), slice={[0:256], [0:768]} | slice | bytes 786432 | tf_op jit(solution)/shard_map/slice | solution.py:301
  12.7 1.0 pad_maximum_fusion.table_ref
  13.7 0.0 copy-start.5
  13.7 2.2 %shard_map.104 = (bf16[128,512]{1,0:T(8,128)(2,1)}, bf16[128,512]{1,0:T(8,128)(2,1)}) custom-call(s32[1,2]{1,0:T(1,128)} %tile_in.3, s32[1,256]{1,0:T(1,128)} %bitcast.19, s32[1,256]{1,0:T(1,128)} %row_in.3, bf16[128,256]{1,0:T(8,128)(2,1)} %bitcast.17), custom_call_target="tpu_custom_call" | custom-call | tf_op jit(solution)/shard_map/pallas_call | solution.py:234
  15.9 1.3 %all-to-all-done.ids_ref = s32[32,1,128]{2,1,0:T(1,128)S(1)} async-done(((s32[32,1,128]{2,1,0:T(1,128)}), s32[32,1,128]{2,1,0:T(1,128)S(1)}, u32[]{:S(2)}, u32[]{:S(2)}) %all-to-all-start) | async-done | bytes 16416 | tf_op jit(solution)/shard_map/all_to_all | solution.py:247
  17.2 0.7 shard_map.105
  17.9 18.0 %all_to_all.20.pulled_ref = bf16[32,16,768]{2,1,0:T(8,128)(2,1)S(1)} all-to-all(bf16[32,16,768]{2,1,0:T(8,128)(2,1)S(1)} %get-tuple-element.22), channel_id=1, replica_groups=mesh['batch'=16,'hist'=32] {'hist'}, dimensions={0} | all-to-all | bytes 1572864 | tf_op jit(solution)/shard_map/all_to_all | solution.py:247
  35.9 0.5 shard_map.106.pair_ref
  36.4 3.2 %all-gather = bf16[256,1536]{1,0:T(8,128)(2,1)S(1)} all-gather(bf16[128,1536]{1,0:T(8,128)(2,1)S(1)} %shard_map.106.pair_ref), channel_id=2, replica_groups={{0,1},{2,3},{4,5},{6,7},{8,9},{10,11},{12,13},{14,15},{16,17},{18,19},{..., dimensions={0}, use_global_device_ids=true | all-gather | bytes 1179648 | tf_op jit(solution)/shard_map/all_gather | solution.py:314
  39.7 1.1 %shard_map.107 = bf16[32,8,1152]{2,1,0:T(8,128)(2,1)} custom-call(bf16[2,128,1536]{2,1,0:T(8,128)(2,1)S(1)} %bitcast.10), custom_call_target="tpu_custom_call" | custom-call | tf_op jit(solution)/shard_map/pallas_call | solution.py:234
  40.8 5.5 %all-to-all-start.2 = ((bf16[32,8,1152]{2,1,0:T(8,128)(2,1)}), bf16[32,8,1152]{2,1,0:T(8,128)(2,1)S(1)}, u32[]{:S(2)}, u32[]{:S(2)}) async-start(bf16[32,8,1152]{2,1,0:T(8,128)(2,1)} %shard_map.107), calls=%async_computation.2 | async-start | bytes 1179648 | tf_op jit(solution)/shard_map/all_to_all | solution.py:247
  46.4 0.9 copy-done.8
  47.3 2.0 %shard_map.108 = (bf16[32,16,1536]{2,1,0:T(8,128)(2,1)S(1)}, bf16[128,768]{1,0:T(8,128)(2,1)S(1)}, bf16[128,768]{1,0:T(8,128)(2,1)}) custom-call(bf16[128,1536]{1,0:T(8,128)(2,1)S(1)} %shard_map.106.pair_ref, bf16[768,768]{1,0:T(8,128)(2,1)S(1)} %copy-done, bf16[128,512]{1,0:T(8,128)(2,1)S(1)} %copy-done.8, ...), custom_call_target="tpu_custom_call" | custom-call | tf_op jit(solution)/shard_map/pallas_call | solution.py:234
  49.3 1.2 %copy-done.2 = bf16[32,16,1536]{2,1,0:T(8,128)(2,1)} copy-done((bf16[32,16,1536]{2,1,0:T(8,128)(2,1)}, bf16[32,16,1536]{2,1,0:T(8,128)(2,1)S(1)}, u32[]{:S(2)}) %copy-start.2) | copy-done | bytes 1572888
  50.4 0.7 copy-done.6
  51.1 5.3 %all-to-all-done.2.terms_ref = bf16[32,8,1152]{2,1,0:T(8,128)(2,1)S(1)} async-done(((bf16[32,8,1152]{2,1,0:T(8,128)(2,1)}), bf16[32,8,1152]{2,1,0:T(8,128)(2,1)S(1)}, u32[]{:S(2)}, u32[]{:S(2)}) %all-to-all-start.2) | async-done | bytes 589856 | tf_op jit(solution)/shard_map/all_to_all | solution.py:247
  56.5 6.4 %all-to-all-start.3 = ((bf16[32,16,1536]{2,1,0:T(8,128)(2,1)}), bf16[32,16,1536]{2,1,0:T(8,128)(2,1)S(1)}, u32[]{:S(2)}, u32[]{:S(2)}) async-start(bf16[32,16,1536]{2,1,0:T(8,128)(2,1)} %copy-done.2), calls=%async_computation.3 | async-start | bytes 3145728 | tf_op jit(solution)/shard_map/all_to_all | solution.py:247
  62.9 0.1 shard_map.109
  63.0 4.6 %all-gather.1 = bf16[32,1152]{1,0:T(8,128)(2,1)S(1)} all-gather(bf16[16,1152]{1,0:T(8,128)(2,1)S(1)} %shard_map.109), channel_id=3, replica_groups={{0,32},{64,96},{128,160},{192,224},{256,288},{320,352},{384,416},{448,4..., dimensions={0}, use_global_device_ids=true | all-gather | bytes 110592 | tf_op jit(solution)/shard_map/all_gather | solution.py:352
  67.6 5.7 %all-gather.2 = bf16[32,1152]{1,0:T(8,128)(2,1)S(1)} all-gather(bf16[16,1152]{1,0:T(8,128)(2,1)S(1)} %shard_map.110), channel_id=4, replica_groups={{0,64},{32,96},{128,192},{160,224},{256,320},{288,352},{384,448},{416,4..., dimensions={0}, use_global_device_ids=true | all-gather | bytes 110592 | tf_op jit(solution)/shard_map/all_gather | solution.py:352
  73.4 24.0 %all-gather.3 = bf16[64,1152]{1,0:T(8,128)(2,1)S(1)} all-gather(bf16[16,1152]{1,0:T(8,128)(2,1)S(1)} %shard_map.111), channel_id=5, replica_groups={{256,384,0,128},{288,416,32,160},{320,448,64,192},{352,480,96,224},{257..., dimensions={0}, use_global_device_ids=true | all-gather | bytes 184320 | tf_op jit(solution)/shard_map/all_gather | solution.py:356
  97.3 1.1 %shard_map.112 = (bf16[128,768]{1,0:T(8,128)(2,1)}, f32[24,768]{1,0:T(8,128)}) custom-call(bf16[32,16,1536]{2,1,0:T(8,128)(2,1)S(1)} %all-to-all-done.3.back_ref, bf16[512,384]{1,0:T(8,128)(2,1)S(1)} %get-tuple-element.26.pick_in.pick_ref, bf16[128,512]{1,0:T(8,128)(2,1)S(1)} %copy-done.4, bf16[128,768]{1,0:T(8,128)(2,1)S(1)} %copy-done.7, ...), custom_call_target="tpu_custom_call" | custom-call | tf_op jit(solution)/shard_map/pallas_call | solution.py:234
  (17 shorter events, 0.1 us)
Async XLA Ops:
  2.3 14.9 %all-to-all-start = ((s32[32,1,128]{2,1,0:T(1,128)}), s32[32,1,128]{2,1,0:T(1,128)S(1)}, u32[]{:S(2)}, u32[]{:S(2)}) async-start(s32[32,1,128]{2,1,0:T(1,128)} %shard_map.103), calls=%async_computation | async-start | bytes 32768 | tf_op jit(solution)/shard_map/all_to_all | solution.py:247
  13.7 22.2 %copy-start = (bf16[768,768]{1,0:T(8,128)(2,1)S(1)}, bf16[768,768]{1,0:T(8,128)(2,1)}, u32[]{:S(2)}) copy-start(bf16[768,768]{1,0:T(8,128)(2,1)} %weight_ref.3) | copy-start | bytes 3538948
  13.7 22.2 %copy-start.3 = (bf16[1,128,768]{2,1,0:T(8,128)(2,1)S(1)}, bf16[1,128,768]{2,1,0:T(8,128)(2,1)}, u32[]{:S(2)}) copy-start(bf16[1,128,768]{2,1,0:T(8,128)(2,1)} %param.8) | copy-start | bytes 589828
  13.7 22.2 %copy-start.5 = (bf16[1,128,768]{2,1,0:T(8,128)(2,1)S(1)}, bf16[1,128,768]{2,1,0:T(8,128)(2,1)}, u32[]{:S(2)}) copy-start(bf16[1,128,768]{2,1,0:T(8,128)(2,1)} %param.15) | copy-start | bytes 589828
  15.9 20.0 %copy-start.4 = (bf16[128,512]{1,0:T(8,128)(2,1)S(1)}, bf16[128,512]{1,0:T(8,128)(2,1)}, u32[]{:S(2)}) copy-start(bf16[128,512]{1,0:T(8,128)(2,1)} %get-tuple-element.23.all_ref) | copy-start | bytes 393220
  39.7 6.7 %copy-start.1 = (bf16[256,1536]{1,0:T(8,128)(2,1)S(1)}, bf16[256,1536]{1,0:T(8,128)(2,1)}, u32[]{:S(2)}) copy-start(bf16[256,1536]{1,0:T(8,128)(2,1)} %history_in.1) | copy-start | bytes 2359300
  40.8 15.6 %all-to-all-start.2 = ((bf16[32,8,1152]{2,1,0:T(8,128)(2,1)}), bf16[32,8,1152]{2,1,0:T(8,128)(2,1)S(1)}, u32[]{:S(2)}, u32[]{:S(2)}) async-start(bf16[32,8,1152]{2,1,0:T(8,128)(2,1)} %shard_map.107), calls=%async_computation.2 | async-start | bytes 1179648 | tf_op jit(solution)/shard_map/all_to_all | solution.py:247
  46.4 0.9 copy-start.8
  49.3 1.2 %copy-start.2 = (bf16[32,16,1536]{2,1,0:T(8,128)(2,1)}, bf16[32,16,1536]{2,1,0:T(8,128)(2,1)S(1)}, u32[]{:S(2)}) copy-start(bf16[32,16,1536]{2,1,0:T(8,128)(2,1)S(1)} %get-tuple-element.30) | copy-start | bytes 4718596
  50.4 0.7 copy-start.6
  56.5 40.9 %all-to-all-start.3 = ((bf16[32,16,1536]{2,1,0:T(8,128)(2,1)}), bf16[32,16,1536]{2,1,0:T(8,128)(2,1)S(1)}, u32[]{:S(2)}, u32[]{:S(2)}) async-start(bf16[32,16,1536]{2,1,0:T(8,128)(2,1)} %copy-done.2), calls=%async_computation.3 | async-start | bytes 3145728 | tf_op jit(solution)/shard_map/all_to_all | solution.py:247
  62.9 34.5 %copy-start.7 = (bf16[128,768]{1,0:T(8,128)(2,1)S(1)}, bf16[128,768]{1,0:T(8,128)(2,1)}, u32[]{:S(2)}) copy-start(bf16[128,768]{1,0:T(8,128)(2,1)} %copy-done.6) | copy-start | bytes 589828

commit v13 on v9

--- a/solution.py
+++ b/solution.py
@@ -17,6 +17,10 @@
 
 def dot(a, b, dims=(((1,), (0,)), ((), ()))):
     return lax.dot_general(a, b, dims, preferred_element_type=F32)
+
+
+def sigmoid(values):
+    return 1.0 / (1.0 + jnp.exp(-values))
 
 
 def in_edge_order(first_tile, values):
@@ -122,7 +126,7 @@
     pulled = pulled_ref[...].reshape(-1, width)
     mixed = (feats_ref[...].astype(F32) + dot(all_ref[...], pulled)).astype(BF16)
     pre = dot(mixed, weight_ref[...])
-    gate = jax.nn.sigmoid(pre)
+    gate = sigmoid(pre)
     grad_pre = (grad_ref[...].astype(F32) * gate * (1.0 + pre * (1.0 - gate))).astype(BF16)
     pair_ref[:, :width] = mixed
     pair_ref[:, width:] = grad_pre
@@ -169,7 +173,7 @@
     slot_grad = dot(inside_ref[...], grad_mixed, COLS_T).astype(BF16)
     send_ref[:, :, :width] = slot_grad.reshape(peers, CAP, width)
     pre = dot(pair_ref[:, :width], weight_ref[...])
-    out_ref[...] = (pre * jax.nn.sigmoid(pre)).astype(BF16)
+    out_ref[...] = (pre * sigmoid(pre)).astype(BF16)
     load_pick.wait()
     load_aux.wait()
     taken = dot(pick[:, node_rows:], aux[...]).astype(BF16)

time: 98.9 us -> 99 us (level)
  no operation moved by 1% of the time
where the time goes in v13:
time: 99 us; the launch traced here: 98.4 us
  blocking collectives  60.9 us (62%)
  starting transfers between devices  19.1 us (19%)
  Pallas kernels  9.35 us (9%)
  waiting for transfers between devices  5.04 us (5%)
  local copies, waits for them, and re-layouts  2.23 us (2%)
    all_to_all x2, blocking collectives, swap(): lax.all_to_all(values, axis, split_axis=0, concat_axis=0, tiled=True, axi...  33.2 us
    all_gather x1, blocking collectives, body(): term = lax.all_gather(term, 'batch', axis=0, axis_index_groups=far)  24.5 us
    all_to_all x3, starting transfers between devices, swap(): lax.all_to_all(values, axis, split_axis=0, concat_axis=0, tiled=True, axi...  19.1 us
    pallas_call x9, Pallas kernels, call(): pl.pallas_call(kernel, out_shape=out_shape, in_specs=[pl.BlockSpec(memory...  9.35 us
    all_to_all x3, waiting for transfers between devices, swap(): lax.all_to_all(values, axis, split_axis=0, concat_axis=0, tiled=True, axi...  5.04 us
    all_gather x1, blocking collectives, body(): pairs = lax.all_gather(pair, 'hist', axis=0, axis_index_groups=chips)  3.21 us
  transfers between devices with their start and end apart: 3, of which 2 were waited for; matrix products, arithmetic and copies ran while one was open for 2% of the time, Pallas kernels for 4%

profile of v13, /device:TPU:6, one launch (start us, length us, event | category | flops | bytes accessed | tf_op | source)
XLA Modules:
  0.0 98.4 jit_solution(3551173366790744977)
XLA Ops:
  0.6 1.7 %shard_map.103 = s32[32,1,128]{2,1,0:T(1,128)} custom-call(s32[1,2]{1,0:T(1,128)} %tile_in.3, s32[1,256]{1,0:T(1,128)} %bitcast.14, s32[1,256]{1,0:T(1,128)} %row_in.3), custom_call_target="tpu_custom_call" | custom-call | tf_op jit(solution)/shard_map/pallas_call | solution.py:228
  2.3 9.4 %all-to-all-start = ((s32[32,1,128]{2,1,0:T(1,128)}), s32[32,1,128]{2,1,0:T(1,128)S(1)}, u32[]{:S(2)}, u32[]{:S(2)}) async-start(s32[32,1,128]{2,1,0:T(1,128)} %shard_map.103), calls=%async_computation | async-start | bytes 32768 | tf_op jit(solution)/shard_map/all_to_all | solution.py:241
  11.7 1.0 %slice.3 = bf16[256,768]{1,0:T(8,128)(2,1)S(1)} slice(bf16[256,1536]{1,0:T(8,128)(2,1)} %history_in.1), slice={[0:256], [0:768]} | slice | bytes 786432 | tf_op jit(solution)/shard_map/slice | solution.py:295
  12.7 1.0 pad_maximum_fusion.table_ref
  13.7 0.0 copy-start
  13.7 0.0 copy-start.3
  13.7 2.2 %shard_map.104 = (bf16[128,512]{1,0:T(8,128)(2,1)}, bf16[128,512]{1,0:T(8,128)(2,1)}) custom-call(s32[1,2]{1,0:T(1,128)} %tile_in.3, s32[1,256]{1,0:T(1,128)} %bitcast.15, s32[1,256]{1,0:T(1,128)} %row_in.3, bf16[128,256]{1,0:T(8,128)(2,1)} %bitcast.13), custom_call_target="tpu_custom_call" | custom-call | tf_op jit(solution)/shard_map/pallas_call | solution.py:228
  15.9 0.0 copy-start.4
  15.9 1.3 %all-to-all-done.ids_ref = s32[32,1,128]{2,1,0:T(1,128)S(1)} async-done(((s32[32,1,128]{2,1,0:T(1,128)}), s32[32,1,128]{2,1,0:T(1,128)S(1)}, u32[]{:S(2)}, u32[]{:S(2)}) %all-to-all-start) | async-done | bytes 16416 | tf_op jit(solution)/shard_map/all_to_all | solution.py:241
  17.2 0.7 shard_map.105
  17.9 18.0 %all_to_all.25.pulled_ref = bf16[32,16,768]{2,1,0:T(8,128)(2,1)S(1)} all-to-all(bf16[32,16,768]{2,1,0:T(8,128)(2,1)S(1)} %get-tuple-element.22), channel_id=1, replica_groups=mesh['batch'=16,'hist'=32] {'hist'}, dimensions={0} | all-to-all | bytes 1572864 | tf_op jit(solution)/shard_map/all_to_all | solution.py:241
  35.9 0.6 shard_map.106.pair_ref
  36.5 3.2 %all-gather = bf16[256,1536]{1,0:T(8,128)(2,1)S(1)} all-gather(bf16[128,1536]{1,0:T(8,128)(2,1)S(1)} %shard_map.106.pair_ref), channel_id=2, replica_groups={{0,1},{2,3},{4,5},{6,7},{8,9},{10,11},{12,13},{14,15},{16,17},{18,19},{..., dimensions={0}, use_global_device_ids=true | all-gather | bytes 1179648 | tf_op jit(solution)/shard_map/all_gather | solution.py:308
  39.7 0.4 shard_map.107
  40.1 0.0 copy-start.1
  40.1 15.2 %all_to_all.26.terms_ref = bf16[32,8,1152]{2,1,0:T(8,128)(2,1)S(1)} all-to-all(bf16[32,8,1152]{2,1,0:T(8,128)(2,1)S(1)} %shard_map.107), channel_id=1, replica_groups=mesh['batch'=16,'hist'=32] {'hist'}, dimensions={0} | all-to-all | bytes 1179648 | tf_op jit(solution)/shard_map/all_to_all | solution.py:241
  55.4 0.7 shard_map.109
  56.1 4.0 %all-to-all-start.3 = ((bf16[4,16,1152]{2,1,0:T(8,128)(2,1)}), bf16[4,16,1152]{2,1,0:T(8,128)(2,1)S(1)}, u32[]{:S(2)}, u32[]{:S(2)}) async-start(bf16[4,16,1152]{2,1,0:T(8,128)(2,1)} %shard_map.109), calls=%async_computation.3 | async-start | bytes 294912 | tf_op jit(solution)/shard_map/all_to_all | solution.py:241
  60.1 2.0 %shard_map.108 = (bf16[32,16,1536]{2,1,0:T(8,128)(2,1)S(1)}, bf16[128,768]{1,0:T(8,128)(2,1)S(1)}, bf16[128,768]{1,0:T(8,128)(2,1)}) custom-call(bf16[128,1536]{1,0:T(8,128)(2,1)S(1)} %shard_map.106.pair_ref, bf16[768,768]{1,0:T(8,128)(2,1)S(1)} %copy-done, bf16[128,512]{1,0:T(8,128)(2,1)S(1)} %copy-done.6, ...), custom_call_target="tpu_custom_call" | custom-call | tf_op jit(solution)/shard_map/pallas_call | solution.py:228
  62.1 1.2 %copy-done.2 = bf16[32,16,1536]{2,1,0:T(8,128)(2,1)} copy-done((bf16[32,16,1536]{2,1,0:T(8,128)(2,1)}, bf16[32,16,1536]{2,1,0:T(8,128)(2,1)S(1)}, u32[]{:S(2)}) %copy-start.2) | copy-done | bytes 1572888
  63.3 3.7 %all-to-all-done.3.near_ref = bf16[4,16,1152]{2,1,0:T(8,128)(2,1)S(1)} async-done(((bf16[4,16,1152]{2,1,0:T(8,128)(2,1)}), bf16[4,16,1152]{2,1,0:T(8,128)(2,1)S(1)}, u32[]{:S(2)}, u32[]{:S(2)}) %all-to-all-start.3) | async-done | bytes 147488 | tf_op jit(solution)/shard_map/all_to_all | solution.py:241
  67.1 5.8 %all-to-all-start.4 = ((bf16[32,16,1536]{2,1,0:T(8,128)(2,1)}), bf16[32,16,1536]{2,1,0:T(8,128)(2,1)S(1)}, u32[]{:S(2)}, u32[]{:S(2)}) async-start(bf16[32,16,1536]{2,1,0:T(8,128)(2,1)} %copy-done.2), calls=%async_computation.4 | async-start | bytes 3145728 | tf_op jit(solution)/shard_map/all_to_all | solution.py:241
  72.9 24.5 %all-gather.1 = bf16[64,1152]{1,0:T(8,128)(2,1)S(1)} all-gather(bf16[16,1152]{1,0:T(8,128)(2,1)S(1)} %shard_map.110), channel_id=3, replica_groups={{0,128,256,384},{32,160,288,416},{64,192,320,448},{96,224,352,480},{1,1..., dimensions={0}, use_global_device_ids=true | all-gather | bytes 184320 | tf_op jit(solution)/shard_map/all_gather | solution.py:343
  97.3 1.1 %shard_map.111 = (bf16[128,768]{1,0:T(8,128)(2,1)}, f32[24,768]{1,0:T(8,128)}) custom-call(bf16[32,16,1536]{2,1,0:T(8,128)(2,1)S(1)} %all-to-all-done.4.back_ref, bf16[512,384]{1,0:T(8,128)(2,1)S(1)} %get-tuple-element.26.pick_in.pick_ref, bf16[128,512]{1,0:T(8,128)(2,1)S(1)} %copy-done.4, bf16[128,768]{1,0:T(8,128)(2,1)S(1)} %get-tuple-element.31.mixed_ref, ...), custom_call_target="tpu_custom_call" | custom-call | tf_op jit(solution)/shard_map/pallas_call | solution.py:228
  (11 shorter events, 0.0 us)
Async XLA Ops:
  2.3 14.9 %all-to-all-start = ((s32[32,1,128]{2,1,0:T(1,128)}), s32[32,1,128]{2,1,0:T(1,128)S(1)}, u32[]{:S(2)}, u32[]{:S(2)}) async-start(s32[32,1,128]{2,1,0:T(1,128)} %shard_map.103), calls=%async_computation | async-start | bytes 32768 | tf_op jit(solution)/shard_map/all_to_all | solution.py:241
  13.7 22.2 %copy-start = (bf16[768,768]{1,0:T(8,128)(2,1)S(1)}, bf16[768,768]{1,0:T(8,128)(2,1)}, u32[]{:S(2)}) copy-start(bf16[768,768]{1,0:T(8,128)(2,1)} %weight_ref.3) | copy-start | bytes 3538948
  13.7 22.2 %copy-start.3 = (bf16[1,128,768]{2,1,0:T(8,128)(2,1)S(1)}, bf16[1,128,768]{2,1,0:T(8,128)(2,1)}, u32[]{:S(2)}) copy-start(bf16[1,128,768]{2,1,0:T(8,128)(2,1)} %param.8) | copy-start | bytes 589828
  13.7 22.2 %copy-start.5 = (bf16[1,128,768]{2,1,0:T(8,128)(2,1)S(1)}, bf16[1,128,768]{2,1,0:T(8,128)(2,1)}, u32[]{:S(2)}) copy-start(bf16[1,128,768]{2,1,0:T(8,128)(2,1)} %param.15) | copy-start | bytes 589828
  15.9 20.0 %copy-start.4 = (bf16[128,512]{1,0:T(8,128)(2,1)S(1)}, bf16[128,512]{1,0:T(8,128)(2,1)}, u32[]{:S(2)}) copy-start(bf16[128,512]{1,0:T(8,128)(2,1)} %get-tuple-element.23.all_ref) | copy-start | bytes 393220
  40.1 20.0 %copy-start.1 = (bf16[256,1536]{1,0:T(8,128)(2,1)S(1)}, bf16[256,1536]{1,0:T(8,128)(2,1)}, u32[]{:S(2)}) copy-start(bf16[256,1536]{1,0:T(8,128)(2,1)} %history_in.1) | copy-start | bytes 2359300
  40.1 20.0 %copy-start.6 = (bf16[128,512]{1,0:T(8,128)(2,1)S(1)}, bf16[128,512]{1,0:T(8,128)(2,1)}, u32[]{:S(2)}) copy-start(bf16[128,512]{1,0:T(8,128)(2,1)} %get-tuple-element.25.inside_ref) | copy-start | bytes 393220
  56.1 10.9 %all-to-all-start.3 = ((bf16[4,16,1152]{2,1,0:T(8,128)(2,1)}), bf16[4,16,1152]{2,1,0:T(8,128)(2,1)S(1)}, u32[]{:S(2)}, u32[]{:S(2)}) async-start(bf16[4,16,1152]{2,1,0:T(8,128)(2,1)} %shard_map.109), calls=%async_computation.3 | async-start | bytes 294912 | tf_op jit(solution)/shard_map/all_to_all | solution.py:241
  62.1 1.2 %copy-start.2 = (bf16[32,16,1536]{2,1,0:T(8,128)(2,1)}, bf16[32,16,1536]{2,1,0:T(8,128)(2,1)S(1)}, u32[]{:S(2)}) copy-start(bf16[32,16,1536]{2,1,0:T(8,128)(2,1)S(1)} %get-tuple-element.30) | copy-start | bytes 4718596
  67.1 30.3 %all-to-all-start.4 = ((bf16[32,16,1536]{2,1,0:T(8,128)(2,1)}), bf16[32,16,1536]{2,1,0:T(8,128)(2,1)S(1)}, u32[]{:S(2)}, u32[]{:S(2)}) async-start(bf16[32,16,1536]{2,1,0:T(8,128)(2,1)} %copy-done.2), calls=%async_computation.4 | async-start | bytes 3145728 | tf_op jit(solution)/shard_map/all_to_all | solution.py:241

commit v14 on v11

--- a/solution.py
+++ b/solution.py
@@ -17,6 +17,10 @@
 
 def dot(a, b, dims=(((1,), (0,)), ((), ()))):
     return lax.dot_general(a, b, dims, preferred_element_type=F32)
+
+
+def sigmoid(values):
+    return 1.0 / (1.0 + jnp.exp(-values))
 
 
 def in_edge_order(first_tile, values):
@@ -121,7 +125,7 @@
     pulled = pulled_ref[...].reshape(-1, width)
     mixed = (feats_ref[...].astype(F32) + dot(all_ref[...], pulled)).astype(BF16)
     pre = dot(mixed, weight_ref[...])
-    gate = jax.nn.sigmoid(pre)
+    gate = sigmoid(pre)
     grad_pre = (grad_ref[...].astype(F32) * gate * (1.0 + pre * (1.0 - gate))).astype(BF16)
     pair_ref[:, :width] = mixed
     pair_ref[:, width:] = grad_pre
@@ -135,20 +139,21 @@
     grad_pre = jnp.where(second_core, right, left)
     share = width // peers
     step = 8
+    terms = dot(pairs[:, :width], grad_pre, COLS_T)
+    parts = sems.shape[0]
     copies = []
-    terms = dot(pairs[:, :width], grad_pre, COLS_T)
-    for part in range(2):
-        term = terms[part * half : (part + 1) * half, :]
-        first = part * (peers // 2)
-        for peer in range(peers // 2):
+    for part in range(parts):
+        group = peers // parts
+        first = part * group
+        for peer in range(first, first + group):
             blocks = [
-                term[peer * share + i : peer * share + i + step, :] for i in range(0, share, step)
+                terms[peer * share + i : peer * share + i + step, :] for i in range(0, share, step)
             ]
-            term_ref[first + peer] = jnp.concatenate(blocks, axis=1).astype(BF16)
+            term_ref[peer] = jnp.concatenate(blocks, axis=1).astype(BF16)
         copies.append(
             pltpu.make_async_copy(
-                term_ref.at[first : first + peers // 2],
-                term_out.at[first : first + peers // 2],
+                term_ref.at[first : first + group],
+                term_out.at[first : first + group],
                 sems.at[part],
             )
         )
@@ -181,7 +186,7 @@
     slot_grad = dot(inside_ref[...], grad_mixed, COLS_T).astype(BF16)
     send_ref[:, :, :width] = slot_grad.reshape(peers, CAP, width)
     pre = dot(pair_ref[:, :width], weight_ref[...])
-    out_ref[...] = (pre * jax.nn.sigmoid(pre)).astype(BF16)
+    out_ref[...] = (pre * sigmoid(pre)).astype(BF16)
     load_pick.wait()
     load_aux.wait()
     taken = dot(pick[:, node_rows:], aux[...]).astype(BF16)
@@ -319,7 +324,7 @@
         hbm_out=(0,),
         scratch=(
             pltpu.VMEM((peers, 8, share * width // 16), BF16),
-            pltpu.SemaphoreType.DMA((2,)),
+            pltpu.SemaphoreType.DMA((4,)),
         ),
     )
     pair, terms = lax.optimization_barrier((pair, terms))

time: 98.9 us -> 98.9 us (level)
  no operation moved by 1% of the time
where the time goes in v14:
time: 98.9 us; the launch traced here: 98.4 us
  blocking collectives  55.5 us (56%)
  starting transfers between devices  21.3 us (22%)
  Pallas kernels  9.4 us (10%)
  waiting for transfers between devices  6.63 us (7%)
  local copies, waits for them, and re-layouts  3.8 us (4%)
    all_gather x1, blocking collectives, body(): term = lax.all_gather(term, 'batch', axis=0, axis_index_groups=far)  24 us
    all_to_all x3, starting transfers between devices, swap(): lax.all_to_all(values, axis, split_axis=0, concat_axis=0, tiled=True, axi...  21.3 us
    all_to_all x1, blocking collectives, swap(): lax.all_to_all(values, axis, split_axis=0, concat_axis=0, tiled=True, axi...  18 us
    all_gather x2, blocking collectives, body(): term = lax.all_gather(term, 'batch', axis=0, axis_index_groups=twins)  10.4 us
    pallas_call x10, Pallas kernels, call(): pl.pallas_call(kernel, out_shape=out_shape, in_specs=[pl.BlockSpec(memory...  9.4 us
    all_to_all x3, waiting for transfers between devices, swap(): lax.all_to_all(values, axis, split_axis=0, concat_axis=0, tiled=True, axi...  6.63 us
    all_gather x1, blocking collectives, body(): pairs = lax.all_gather(pair, 'hist', axis=0, axis_index_groups=chips)  3.22 us
    unnamed x18, local copies, waits for them, and re-layouts  2.77 us
  transfers between devices with their start and end apart: 3, of which 2 were waited for; matrix products, arithmetic and copies ran while one was open for 2% of the time, Pallas kernels for 4%

profile of v14, /device:TPU:6, one launch (start us, length us, event | category | flops | bytes accessed | tf_op | source)
XLA Modules:
  0.0 98.4 jit_solution(11240420479222214602)
XLA Ops:
  0.6 1.7 %shard_map.103 = s32[32,1,128]{2,1,0:T(1,128)} custom-call(s32[1,2]{1,0:T(1,128)} %tile_in.3, s32[1,256]{1,0:T(1,128)} %bitcast.18, s32[1,256]{1,0:T(1,128)} %row_in.3), custom_call_target="tpu_custom_call" | custom-call | tf_op jit(solution)/shard_map/pallas_call | solution.py:239
  2.3 9.4 %all-to-all-start = ((s32[32,1,128]{2,1,0:T(1,128)}), s32[32,1,128]{2,1,0:T(1,128)S(1)}, u32[]{:S(2)}, u32[]{:S(2)}) async-start(s32[32,1,128]{2,1,0:T(1,128)} %shard_map.103), calls=%async_computation | async-start | bytes 32768 | tf_op jit(solution)/shard_map/all_to_all | solution.py:252
  11.7 1.0 %slice.3 = bf16[256,768]{1,0:T(8,128)(2,1)S(1)} slice(bf16[256,1536]{1,0:T(8,128)(2,1)} %history_in.1), slice={[0:256], [0:768]} | slice | bytes 786432 | tf_op jit(solution)/shard_map/slice | solution.py:306
  12.7 1.0 pad_maximum_fusion.table_ref
  13.7 0.0 copy-start.5
  13.7 2.2 %shard_map.104 = (bf16[128,512]{1,0:T(8,128)(2,1)}, bf16[128,512]{1,0:T(8,128)(2,1)}) custom-call(s32[1,2]{1,0:T(1,128)} %tile_in.3, s32[1,256]{1,0:T(1,128)} %bitcast.19, s32[1,256]{1,0:T(1,128)} %row_in.3, bf16[128,256]{1,0:T(8,128)(2,1)} %bitcast.17), custom_call_target="tpu_custom_call" | custom-call | tf_op jit(solution)/shard_map/pallas_call | solution.py:239
  15.9 1.3 %all-to-all-done.ids_ref = s32[32,1,128]{2,1,0:T(1,128)S(1)} async-done(((s32[32,1,128]{2,1,0:T(1,128)}), s32[32,1,128]{2,1,0:T(1,128)S(1)}, u32[]{:S(2)}, u32[]{:S(2)}) %all-to-all-start) | async-done | bytes 16416 | tf_op jit(solution)/shard_map/all_to_all | solution.py:252
  17.2 0.7 shard_map.105
  17.9 18.0 %all_to_all.20.pulled_ref = bf16[32,16,768]{2,1,0:T(8,128)(2,1)S(1)} all-to-all(bf16[32,16,768]{2,1,0:T(8,128)(2,1)S(1)} %get-tuple-element.22), channel_id=1, replica_groups=mesh['batch'=16,'hist'=32] {'hist'}, dimensions={0} | all-to-all | bytes 1572864 | tf_op jit(solution)/shard_map/all_to_all | solution.py:252
  35.9 0.6 shard_map.106.pair_ref
  36.5 3.2 %all-gather = bf16[256,1536]{1,0:T(8,128)(2,1)S(1)} all-gather(bf16[128,1536]{1,0:T(8,128)(2,1)S(1)} %shard_map.106.pair_ref), channel_id=2, replica_groups={{0,1},{2,3},{4,5},{6,7},{8,9},{10,11},{12,13},{14,15},{16,17},{18,19},{..., dimensions={0}, use_global_device_ids=true | all-gather | bytes 1179648 | tf_op jit(solution)/shard_map/all_gather | solution.py:319
  39.7 1.1 %shard_map.107 = bf16[32,8,1152]{2,1,0:T(8,128)(2,1)} custom-call(bf16[2,128,1536]{2,1,0:T(8,128)(2,1)S(1)} %bitcast.10), custom_call_target="tpu_custom_call" | custom-call | tf_op jit(solution)/shard_map/pallas_call | solution.py:239
  40.8 5.5 %all-to-all-start.2 = ((bf16[32,8,1152]{2,1,0:T(8,128)(2,1)}), bf16[32,8,1152]{2,1,0:T(8,128)(2,1)S(1)}, u32[]{:S(2)}, u32[]{:S(2)}) async-start(bf16[32,8,1152]{2,1,0:T(8,128)(2,1)} %shard_map.107), calls=%async_computation.2 | async-start | bytes 1179648 | tf_op jit(solution)/shard_map/all_to_all | solution.py:252
  46.4 0.9 copy-done.8
  47.3 2.0 %shard_map.108 = (bf16[32,16,1536]{2,1,0:T(8,128)(2,1)S(1)}, bf16[128,768]{1,0:T(8,128)(2,1)S(1)}, bf16[128,768]{1,0:T(8,128)(2,1)}) custom-call(bf16[128,1536]{1,0:T(8,128)(2,1)S(1)} %shard_map.106.pair_ref, bf16[768,768]{1,0:T(8,128)(2,1)S(1)} %copy-done, bf16[128,512]{1,0:T(8,128)(2,1)S(1)} %copy-done.8, ...), custom_call_target="tpu_custom_call" | custom-call | tf_op jit(solution)/shard_map/pallas_call | solution.py:239
  49.3 1.2 %copy-done.2 = bf16[32,16,1536]{2,1,0:T(8,128)(2,1)} copy-done((bf16[32,16,1536]{2,1,0:T(8,128)(2,1)}, bf16[32,16,1536]{2,1,0:T(8,128)(2,1)S(1)}, u32[]{:S(2)}) %copy-start.2) | copy-done | bytes 1572888
  50.5 0.7 copy-done.6
  51.1 5.3 %all-to-all-done.2.terms_ref = bf16[32,8,1152]{2,1,0:T(8,128)(2,1)S(1)} async-done(((bf16[32,8,1152]{2,1,0:T(8,128)(2,1)}), bf16[32,8,1152]{2,1,0:T(8,128)(2,1)S(1)}, u32[]{:S(2)}, u32[]{:S(2)}) %all-to-all-start.2) | async-done | bytes 589856 | tf_op jit(solution)/shard_map/all_to_all | solution.py:252
  56.5 6.4 %all-to-all-start.3 = ((bf16[32,16,1536]{2,1,0:T(8,128)(2,1)}), bf16[32,16,1536]{2,1,0:T(8,128)(2,1)S(1)}, u32[]{:S(2)}, u32[]{:S(2)}) async-start(bf16[32,16,1536]{2,1,0:T(8,128)(2,1)} %copy-done.2), calls=%async_computation.3 | async-start | bytes 3145728 | tf_op jit(solution)/shard_map/all_to_all | solution.py:252
  62.9 0.1 shard_map.109
  63.0 4.6 %all-gather.1 = bf16[32,1152]{1,0:T(8,128)(2,1)S(1)} all-gather(bf16[16,1152]{1,0:T(8,128)(2,1)S(1)} %shard_map.109), channel_id=3, replica_groups={{0,32},{64,96},{128,160},{192,224},{256,288},{320,352},{384,416},{448,4..., dimensions={0}, use_global_device_ids=true | all-gather | bytes 110592 | tf_op jit(solution)/shard_map/all_gather | solution.py:357
  67.6 5.7 %all-gather.2 = bf16[32,1152]{1,0:T(8,128)(2,1)S(1)} all-gather(bf16[16,1152]{1,0:T(8,128)(2,1)S(1)} %shard_map.110), channel_id=4, replica_groups={{0,64},{32,96},{128,192},{160,224},{256,320},{288,352},{384,448},{416,4..., dimensions={0}, use_global_device_ids=true | all-gather | bytes 110592 | tf_op jit(solution)/shard_map/all_gather | solution.py:357
  73.4 24.0 %all-gather.3 = bf16[64,1152]{1,0:T(8,128)(2,1)S(1)} all-gather(bf16[16,1152]{1,0:T(8,128)(2,1)S(1)} %shard_map.111), channel_id=5, replica_groups={{0,128,256,384},{32,160,288,416},{64,192,320,448},{96,224,352,480},{1,1..., dimensions={0}, use_global_device_ids=true | all-gather | bytes 184320 | tf_op jit(solution)/shard_map/all_gather | solution.py:360
  97.3 1.1 %shard_map.112 = (bf16[128,768]{1,0:T(8,128)(2,1)}, f32[24,768]{1,0:T(8,128)}) custom-call(bf16[32,16,1536]{2,1,0:T(8,128)(2,1)S(1)} %all-to-all-done.3.back_ref, bf16[512,384]{1,0:T(8,128)(2,1)S(1)} %get-tuple-element.26.pick_in.pick_ref, bf16[128,512]{1,0:T(8,128)(2,1)S(1)} %copy-done.4, bf16[128,768]{1,0:T(8,128)(2,1)S(1)} %copy-done.7, ...), custom_call_target="tpu_custom_call" | custom-call | tf_op jit(solution)/shard_map/pallas_call | solution.py:239
  (17 shorter events, 0.1 us)
Async XLA Ops:
  2.3 14.9 %all-to-all-start = ((s32[32,1,128]{2,1,0:T(1,128)}), s32[32,1,128]{2,1,0:T(1,128)S(1)}, u32[]{:S(2)}, u32[]{:S(2)}) async-start(s32[32,1,128]{2,1,0:T(1,128)} %shard_map.103), calls=%async_computation | async-start | bytes 32768 | tf_op jit(solution)/shard_map/all_to_all | solution.py:252
  13.7 22.2 %copy-start = (bf16[768,768]{1,0:T(8,128)(2,1)S(1)}, bf16[768,768]{1,0:T(8,128)(2,1)}, u32[]{:S(2)}) copy-start(bf16[768,768]{1,0:T(8,128)(2,1)} %weight_ref.3) | copy-start | bytes 3538948
  13.7 22.2 %copy-start.3 = (bf16[1,128,768]{2,1,0:T(8,128)(2,1)S(1)}, bf16[1,128,768]{2,1,0:T(8,128)(2,1)}, u32[]{:S(2)}) copy-start(bf16[1,128,768]{2,1,0:T(8,128)(2,1)} %param.8) | copy-start | bytes 589828
  13.7 22.2 %copy-start.5 = (bf16[1,128,768]{2,1,0:T(8,128)(2,1)S(1)}, bf16[1,128,768]{2,1,0:T(8,128)(2,1)}, u32[]{:S(2)}) copy-start(bf16[1,128,768]{2,1,0:T(8,128)(2,1)} %param.15) | copy-start | bytes 589828
  15.9 20.0 %copy-start.4 = (bf16[128,512]{1,0:T(8,128)(2,1)S(1)}, bf16[128,512]{1,0:T(8,128)(2,1)}, u32[]{:S(2)}) copy-start(bf16[128,512]{1,0:T(8,128)(2,1)} %get-tuple-element.23.all_ref) | copy-start | bytes 393220
  39.7 6.7 %copy-start.1 = (bf16[256,1536]{1,0:T(8,128)(2,1)S(1)}, bf16[256,1536]{1,0:T(8,128)(2,1)}, u32[]{:S(2)}) copy-start(bf16[256,1536]{1,0:T(8,128)(2,1)} %history_in.1) | copy-start | bytes 2359300
  40.8 15.6 %all-to-all-start.2 = ((bf16[32,8,1152]{2,1,0:T(8,128)(2,1)}), bf16[32,8,1152]{2,1,0:T(8,128)(2,1)S(1)}, u32[]{:S(2)}, u32[]{:S(2)}) async-start(bf16[32,8,1152]{2,1,0:T(8,128)(2,1)} %shard_map.107), calls=%async_computation.2 | async-start | bytes 1179648 | tf_op jit(solution)/shard_map/all_to_all | solution.py:252
  46.4 0.9 copy-start.8
  49.3 1.2 %copy-start.2 = (bf16[32,16,1536]{2,1,0:T(8,128)(2,1)}, bf16[32,16,1536]{2,1,0:T(8,128)(2,1)S(1)}, u32[]{:S(2)}) copy-start(bf16[32,16,1536]{2,1,0:T(8,128)(2,1)S(1)} %get-tuple-element.30) | copy-start | bytes 4718596
  50.5 0.7 copy-start.6
  56.5 40.9 %all-to-all-start.3 = ((bf16[32,16,1536]{2,1,0:T(8,128)(2,1)}), bf16[32,16,1536]{2,1,0:T(8,128)(2,1)S(1)}, u32[]{:S(2)}, u32[]{:S(2)}) async-start(bf16[32,16,1536]{2,1,0:T(8,128)(2,1)} %copy-done.2), calls=%async_computation.3 | async-start | bytes 3145728 | tf_op jit(solution)/shard_map/all_to_all | solution.py:252
  62.9 34.5 %copy-start.7 = (bf16[128,768]{1,0:T(8,128)(2,1)S(1)}, bf16[128,768]{1,0:T(8,128)(2,1)}, u32[]{:S(2)}) copy-start(bf16[128,768]{1,0:T(8,128)(2,1)} %copy-done.6) | copy-start | bytes 589828

commit v15 on v13

--- a/solution.py
+++ b/solution.py
@@ -57,17 +57,16 @@
     for copy in copies:
         copy.wait()
     peers = ids_ref.shape[0]
-    first = tile_ref[0, 0]
+    first = tile_ref[:, :1]
     owners = in_edge_order(first, owner_ref[...])
     rows = in_edge_order(first, row_ref[...])
     named, place = slot_places(owners, peers, earlier)
     spot = lax.broadcasted_iota(jnp.int32, (LANES, rows.shape[1]), 0) == place
     spot = jnp.where(spot, 1.0, 0.0).astype(BF16)
-    low = (rows % LANES).astype(F32)
-    high = (rows // LANES).astype(F32)
-    ids = dot((named * low).astype(BF16), spot, ROWS_T) + LANES * dot(
-        (named * high).astype(BF16), spot, ROWS_T
-    )
+    low = named * (rows % LANES).astype(F32)
+    high = named * (rows // LANES).astype(F32)
+    ids = dot(jnp.concatenate([low, high], axis=0).astype(BF16), spot, ROWS_T)
+    ids = ids[:peers] + LANES * ids[peers:]
     ids_ref[...] = ids.astype(jnp.int32).reshape(ids_ref.shape)
 
 
@@ -102,7 +101,7 @@
     earlier = earlier_slots(owner_ref.shape[1])
     for copy in copies:
         copy.wait()
-    first = tile_ref[0, 0]
+    first = tile_ref[:, :1]
     owners = in_edge_order(first, owner_ref[...])
     rows = in_edge_order(first, row_ref[...])
     _, place = slot_places(owners, peers, earlier)
@@ -262,7 +261,7 @@
         hbm=(0, 1, 2),
         vmem=60,
         scratch=(
-            pltpu.SMEM(tile_map.shape, jnp.int32),
+            pltpu.VMEM(tile_map.shape, jnp.int32),
             pltpu.VMEM(owners.shape, jnp.int32),
             pltpu.VMEM(nbr_row.shape, jnp.int32),
             pltpu.SemaphoreType.DMA((3,)),
@@ -279,7 +278,7 @@
         hbm=(0, 1, 2, 3),
         vmem=60,
         scratch=(
-            pltpu.SMEM(tile_map.shape, jnp.int32),
+            pltpu.VMEM(tile_map.shape, jnp.int32),
             pltpu.VMEM(owners.shape, jnp.int32),
             pltpu.VMEM(nbr_row.shape, jnp.int32),
             pltpu.VMEM(edge_coef.shape[1:], BF16),

time: 99 us -> 99.1 us (level)
  no operation moved by 1% of the time
where the time goes in v15:
time: 99.1 us; the launch traced here: 98.5 us
  blocking collectives  60.9 us (61%)
  starting transfers between devices  19.1 us (19%)
  Pallas kernels  9.47 us (10%)
  waiting for transfers between devices  4.98 us (5%)
  local copies, waits for them, and re-layouts  2.23 us (2%)
    all_to_all x2, blocking collectives, swap(): lax.all_to_all(values, axis, split_axis=0, concat_axis=0, tiled=True, axi...  33.3 us
    all_gather x1, blocking collectives, body(): term = lax.all_gather(term, 'batch', axis=0, axis_index_groups=far)  24.4 us
    all_to_all x3, starting transfers between devices, swap(): lax.all_to_all(values, axis, split_axis=0, concat_axis=0, tiled=True, axi...  19.1 us
    pallas_call x9, Pallas kernels, call(): pl.pallas_call(kernel, out_shape=out_shape, in_specs=[pl.BlockSpec(memory...  9.47 us
    all_to_all x3, waiting for transfers between devices, swap(): lax.all_to_all(values, axis, split_axis=0, concat_axis=0, tiled=True, axi...  4.98 us
    all_gather x1, blocking collectives, body(): pairs = lax.all_gather(pair, 'hist', axis=0, axis_index_groups=chips)  3.21 us
  transfers between devices with their start and end apart: 3, of which 2 were waited for; matrix products, arithmetic and copies ran while one was open for 2% of the time, Pallas kernels for 4%

profile of v15, /device:TPU:6, one launch (start us, length us, event | category | flops | bytes accessed | tf_op | source)
XLA Modules:
  0.0 98.5 jit_solution(3052945409344215703)
XLA Ops:
  0.6 1.7 %shard_map.103 = s32[32,1,128]{2,1,0:T(1,128)} custom-call(s32[1,2]{1,0:T(1,128)} %tile_in.3, s32[1,256]{1,0:T(1,128)} %bitcast.14, s32[1,256]{1,0:T(1,128)} %row_in.3), custom_call_target="tpu_custom_call" | custom-call | tf_op jit(solution)/shard_map/pallas_call | solution.py:227
  2.4 9.4 %all-to-all-start = ((s32[32,1,128]{2,1,0:T(1,128)}), s32[32,1,128]{2,1,0:T(1,128)S(1)}, u32[]{:S(2)}, u32[]{:S(2)}) async-start(s32[32,1,128]{2,1,0:T(1,128)} %shard_map.103), calls=%async_computation | async-start | bytes 32768 | tf_op jit(solution)/shard_map/all_to_all | solution.py:240
  11.7 1.0 %slice.3 = bf16[256,768]{1,0:T(8,128)(2,1)S(1)} slice(bf16[256,1536]{1,0:T(8,128)(2,1)} %history_in.1), slice={[0:256], [0:768]} | slice | bytes 786432 | tf_op jit(solution)/shard_map/slice | solution.py:294
  12.8 1.0 pad_maximum_fusion.table_ref
  13.7 0.0 copy-start
  13.8 0.0 copy-start.3
  13.8 0.0 copy-start.5
  13.8 2.2 %shard_map.104 = (bf16[128,512]{1,0:T(8,128)(2,1)}, bf16[128,512]{1,0:T(8,128)(2,1)}) custom-call(s32[1,2]{1,0:T(1,128)} %tile_in.3, s32[1,256]{1,0:T(1,128)} %bitcast.15, s32[1,256]{1,0:T(1,128)} %row_in.3, bf16[128,256]{1,0:T(8,128)(2,1)} %bitcast.13), custom_call_target="tpu_custom_call" | custom-call | tf_op jit(solution)/shard_map/pallas_call | solution.py:227
  16.0 0.0 copy-start.4
  16.0 1.2 %all-to-all-done.ids_ref = s32[32,1,128]{2,1,0:T(1,128)S(1)} async-done(((s32[32,1,128]{2,1,0:T(1,128)}), s32[32,1,128]{2,1,0:T(1,128)S(1)}, u32[]{:S(2)}, u32[]{:S(2)}) %all-to-all-start) | async-done | bytes 16416 | tf_op jit(solution)/shard_map/all_to_all | solution.py:240
  17.3 0.7 shard_map.105
  18.0 18.0 %all_to_all.25.pulled_ref = bf16[32,16,768]{2,1,0:T(8,128)(2,1)S(1)} all-to-all(bf16[32,16,768]{2,1,0:T(8,128)(2,1)S(1)} %get-tuple-element.22), channel_id=1, replica_groups=mesh['batch'=16,'hist'=32] {'hist'}, dimensions={0} | all-to-all | bytes 1572864 | tf_op jit(solution)/shard_map/all_to_all | solution.py:240
  36.0 0.6 shard_map.106.pair_ref
  36.6 3.2 %all-gather = bf16[256,1536]{1,0:T(8,128)(2,1)S(1)} all-gather(bf16[128,1536]{1,0:T(8,128)(2,1)S(1)} %shard_map.106.pair_ref), channel_id=2, replica_groups={{0,1},{2,3},{4,5},{6,7},{8,9},{10,11},{12,13},{14,15},{16,17},{18,19},{..., dimensions={0}, use_global_device_ids=true | all-gather | bytes 1179648 | tf_op jit(solution)/shard_map/all_gather | solution.py:307
  39.8 0.4 shard_map.107
  40.2 15.2 %all_to_all.26.terms_ref = bf16[32,8,1152]{2,1,0:T(8,128)(2,1)S(1)} all-to-all(bf16[32,8,1152]{2,1,0:T(8,128)(2,1)S(1)} %shard_map.107), channel_id=1, replica_groups=mesh['batch'=16,'hist'=32] {'hist'}, dimensions={0} | all-to-all | bytes 1179648 | tf_op jit(solution)/shard_map/all_to_all | solution.py:240
  55.5 0.7 shard_map.109
  56.2 4.0 %all-to-all-start.3 = ((bf16[4,16,1152]{2,1,0:T(8,128)(2,1)}), bf16[4,16,1152]{2,1,0:T(8,128)(2,1)S(1)}, u32[]{:S(2)}, u32[]{:S(2)}) async-start(bf16[4,16,1152]{2,1,0:T(8,128)(2,1)} %shard_map.109), calls=%async_computation.3 | async-start | bytes 294912 | tf_op jit(solution)/shard_map/all_to_all | solution.py:240
  60.2 2.0 %shard_map.108 = (bf16[32,16,1536]{2,1,0:T(8,128)(2,1)S(1)}, bf16[128,768]{1,0:T(8,128)(2,1)S(1)}, bf16[128,768]{1,0:T(8,128)(2,1)}) custom-call(bf16[128,1536]{1,0:T(8,128)(2,1)S(1)} %shard_map.106.pair_ref, bf16[768,768]{1,0:T(8,128)(2,1)S(1)} %copy-done, bf16[128,512]{1,0:T(8,128)(2,1)S(1)} %copy-done.6, ...), custom_call_target="tpu_custom_call" | custom-call | tf_op jit(solution)/shard_map/pallas_call | solution.py:227
  62.3 1.2 %copy-done.2 = bf16[32,16,1536]{2,1,0:T(8,128)(2,1)} copy-done((bf16[32,16,1536]{2,1,0:T(8,128)(2,1)}, bf16[32,16,1536]{2,1,0:T(8,128)(2,1)S(1)}, u32[]{:S(2)}) %copy-start.2) | copy-done | bytes 1572888
  63.4 3.7 %all-to-all-done.3.near_ref = bf16[4,16,1152]{2,1,0:T(8,128)(2,1)S(1)} async-done(((bf16[4,16,1152]{2,1,0:T(8,128)(2,1)}), bf16[4,16,1152]{2,1,0:T(8,128)(2,1)S(1)}, u32[]{:S(2)}, u32[]{:S(2)}) %all-to-all-start.3) | async-done | bytes 147488 | tf_op jit(solution)/shard_map/all_to_all | solution.py:240
  67.2 5.8 %all-to-all-start.4 = ((bf16[32,16,1536]{2,1,0:T(8,128)(2,1)}), bf16[32,16,1536]{2,1,0:T(8,128)(2,1)S(1)}, u32[]{:S(2)}, u32[]{:S(2)}) async-start(bf16[32,16,1536]{2,1,0:T(8,128)(2,1)} %copy-done.2), calls=%async_computation.4 | async-start | bytes 3145728 | tf_op jit(solution)/shard_map/all_to_all | solution.py:240
  73.0 24.4 %all-gather.1 = bf16[64,1152]{1,0:T(8,128)(2,1)S(1)} all-gather(bf16[16,1152]{1,0:T(8,128)(2,1)S(1)} %shard_map.110), channel_id=3, replica_groups={{0,128,256,384},{32,160,288,416},{64,192,320,448},{96,224,352,480},{1,1..., dimensions={0}, use_global_device_ids=true | all-gather | bytes 184320 | tf_op jit(solution)/shard_map/all_gather | solution.py:342
  97.4 1.1 %shard_map.111 = (bf16[128,768]{1,0:T(8,128)(2,1)}, f32[24,768]{1,0:T(8,128)}) custom-call(bf16[32,16,1536]{2,1,0:T(8,128)(2,1)S(1)} %all-to-all-done.4.back_ref, bf16[512,384]{1,0:T(8,128)(2,1)S(1)} %get-tuple-element.26.pick_in.pick_ref, bf16[128,512]{1,0:T(8,128)(2,1)S(1)} %copy-done.4, bf16[128,768]{1,0:T(8,128)(2,1)S(1)} %get-tuple-element.31.mixed_ref, ...), custom_call_target="tpu_custom_call" | custom-call | tf_op jit(solution)/shard_map/pallas_call | solution.py:227
  (11 shorter events, 0.0 us)
Async XLA Ops:
  2.4 14.9 %all-to-all-start = ((s32[32,1,128]{2,1,0:T(1,128)}), s32[32,1,128]{2,1,0:T(1,128)S(1)}, u32[]{:S(2)}, u32[]{:S(2)}) async-start(s32[32,1,128]{2,1,0:T(1,128)} %shard_map.103), calls=%async_computation | async-start | bytes 32768 | tf_op jit(solution)/shard_map/all_to_all | solution.py:240
  13.7 22.3 %copy-start = (bf16[768,768]{1,0:T(8,128)(2,1)S(1)}, bf16[768,768]{1,0:T(8,128)(2,1)}, u32[]{:S(2)}) copy-start(bf16[768,768]{1,0:T(8,128)(2,1)} %weight_ref.3) | copy-start | bytes 3538948
  13.8 22.3 %copy-start.3 = (bf16[1,128,768]{2,1,0:T(8,128)(2,1)S(1)}, bf16[1,128,768]{2,1,0:T(8,128)(2,1)}, u32[]{:S(2)}) copy-start(bf16[1,128,768]{2,1,0:T(8,128)(2,1)} %param.8) | copy-start | bytes 589828
  13.8 22.2 %copy-start.5 = (bf16[1,128,768]{2,1,0:T(8,128)(2,1)S(1)}, bf16[1,128,768]{2,1,0:T(8,128)(2,1)}, u32[]{:S(2)}) copy-start(bf16[1,128,768]{2,1,0:T(8,128)(2,1)} %param.15) | copy-start | bytes 589828
  16.0 20.0 %copy-start.4 = (bf16[128,512]{1,0:T(8,128)(2,1)S(1)}, bf16[128,512]{1,0:T(8,128)(2,1)}, u32[]{:S(2)}) copy-start(bf16[128,512]{1,0:T(8,128)(2,1)} %get-tuple-element.23.all_ref) | copy-start | bytes 393220
  40.2 20.0 %copy-start.1 = (bf16[256,1536]{1,0:T(8,128)(2,1)S(1)}, bf16[256,1536]{1,0:T(8,128)(2,1)}, u32[]{:S(2)}) copy-start(bf16[256,1536]{1,0:T(8,128)(2,1)} %history_in.1) | copy-start | bytes 2359300
  40.2 20.0 %copy-start.6 = (bf16[128,512]{1,0:T(8,128)(2,1)S(1)}, bf16[128,512]{1,0:T(8,128)(2,1)}, u32[]{:S(2)}) copy-start(bf16[128,512]{1,0:T(8,128)(2,1)} %get-tuple-element.25.inside_ref) | copy-start | bytes 393220
  56.2 10.9 %all-to-all-start.3 = ((bf16[4,16,1152]{2,1,0:T(8,128)(2,1)}), bf16[4,16,1152]{2,1,0:T(8,128)(2,1)S(1)}, u32[]{:S(2)}, u32[]{:S(2)}) async-start(bf16[4,16,1152]{2,1,0:T(8,128)(2,1)} %shard_map.109), calls=%async_computation.3 | async-start | bytes 294912 | tf_op jit(solution)/shard_map/all_to_all | solution.py:240
  62.2 1.2 %copy-start.2 = (bf16[32,16,1536]{2,1,0:T(8,128)(2,1)}, bf16[32,16,1536]{2,1,0:T(8,128)(2,1)S(1)}, u32[]{:S(2)}) copy-start(bf16[32,16,1536]{2,1,0:T(8,128)(2,1)S(1)} %get-tuple-element.30) | copy-start | bytes 4718596
  67.2 30.2 %all-to-all-start.4 = ((bf16[32,16,1536]{2,1,0:T(8,128)(2,1)}), bf16[32,16,1536]{2,1,0:T(8,128)(2,1)S(1)}, u32[]{:S(2)}, u32[]{:S(2)}) async-start(bf16[32,16,1536]{2,1,0:T(8,128)(2,1)} %copy-done.2), calls=%async_computation.4 | async-start | bytes 3145728 | tf_op jit(solution)/shard_map/all_to_all | solution.py:240

commit v16 on v15

--- a/solution.py
+++ b/solution.py
@@ -21,6 +21,14 @@
 
 def sigmoid(values):
     return 1.0 / (1.0 + jnp.exp(-values))
+
+
+def lead_of(peers):
+    return 5 * peers // 8
+
+
+def to_blocks(owners, peers):
+    return (owners + peers - lead_of(peers)) % peers
 
 
 def in_edge_order(first_tile, values):
@@ -58,7 +66,7 @@
         copy.wait()
     peers = ids_ref.shape[0]
     first = tile_ref[:, :1]
-    owners = in_edge_order(first, owner_ref[...])
+    owners = in_edge_order(first, to_blocks(owner_ref[...], peers))
     rows = in_edge_order(first, row_ref[...])
     named, place = slot_places(owners, peers, earlier)
     spot = lax.broadcasted_iota(jnp.int32, (LANES, rows.shape[1]), 0) == place
@@ -102,7 +110,7 @@
     for copy in copies:
         copy.wait()
     first = tile_ref[:, :1]
-    owners = in_edge_order(first, owner_ref[...])
+    owners = in_edge_order(first, to_blocks(owner_ref[...], peers))
     rows = in_edge_order(first, row_ref[...])
     _, place = slot_places(owners, peers, earlier)
     target = owners * CAP + place
@@ -142,9 +150,8 @@
     step = 8
     term = dot(mixed, grad_pre, COLS_T)
     for peer in range(peers):
-        blocks = [
-            term[peer * share + i : peer * share + i + step, :] for i in range(0, share, step)
-        ]
+        row = (peer + lead_of(peers)) % peers * share
+        blocks = [term[row + i : row + i + step, :] for i in range(0, share, step)]
         term_ref[peer] = jnp.concatenate(blocks, axis=1).astype(BF16)
 
 
@@ -237,6 +244,9 @@
 
 
 def swap(values, axis="hist", groups=None):
+    if groups is None:
+        peers = lax.axis_size(axis)
+        groups = [[(i + lead_of(peers)) % peers for i in range(peers)]]
     return lax.all_to_all(
         values, axis, split_axis=0, concat_axis=0, tiled=True, axis_index_groups=groups
     )
@@ -332,7 +342,7 @@
         ),
     )
     side = 4
-    near = [[a * side + i for i in range(side)] for a in range(planes // side)]
+    near = [[a * side + i for i in (2, 1, 3, 0)] for a in range(planes // side)]
     term = call(weight_kernel, shape((side, 16, share * width // 16), BF16), terms)
     term = swap(term, "batch", near)
     sent, term = lax.optimization_barrier((sent, term))

time: 99.1 us -> 97.7 us (0.986)
  waiting for transfers between devices: 4.98 us -> 0.93 us
  starting transfers between devices: 19.1 us -> 20.7 us
    all_to_all x3, waiting for transfers between devices: 4.98 us -> 0.93 us  [swap(): lax.all_to_all(values, axis, split_axis=0, concat_axis=0, tiled=True, axi...]
    all_to_all x3, starting transfers between devices: 19.1 us -> 20.7 us  [swap(): lax.all_to_all(values, axis, split_axis=0, concat_axis=0, tiled=True, axi...]
    all_to_all x2, blocking collectives: 33.3 us -> 34.6 us  [swap(): lax.all_to_all(values, axis, split_axis=0, concat_axis=0, tiled=True, axi...]
  transfers between devices with their start and end apart: 3 -> 3, of which waited for: 2 -> 1; matrix products, arithmetic and copies ran while one was open for 2% -> 2% of each run, Pallas kernels for 4% -> 4%
where the time goes in v16:
time: 97.7 us; the launch traced here: 96.4 us
  blocking collectives  61.3 us (63%)
  starting transfers between devices  20.7 us (21%)
  Pallas kernels  9.46 us (10%)
  local copies, waits for them, and re-layouts  2.23 us (2%)
    all_to_all x2, blocking collectives, swap(): lax.all_to_all(values, axis, split_axis=0, concat_axis=0, tiled=True, axi...  34.6 us
    all_gather x1, blocking collectives, body(): term = lax.all_gather(term, 'batch', axis=0, axis_index_groups=far)  24.3 us
    all_to_all x3, starting transfers between devices, swap(): lax.all_to_all(values, axis, split_axis=0, concat_axis=0, tiled=True, axi...  20.7 us
    pallas_call x9, Pallas kernels, call(): pl.pallas_call(kernel, out_shape=out_shape, in_specs=[pl.BlockSpec(memory...  9.46 us
    all_gather x1, blocking collectives, body(): pairs = lax.all_gather(pair, 'hist', axis=0, axis_index_groups=chips)  2.4 us
  transfers between devices with their start and end apart: 3, of which 1 were waited for; matrix products, arithmetic and copies ran while one was open for 2% of the time, Pallas kernels for 4%

profile of v16, /device:TPU:6, one launch (start us, length us, event | category | flops | bytes accessed | tf_op | source)
XLA Modules:
  0.0 96.4 jit_solution(7202625254678413115)
XLA Ops:
  0.6 1.7 %shard_map.103 = s32[32,1,128]{2,1,0:T(1,128)} custom-call(s32[1,2]{1,0:T(1,128)} %tile_in.3, s32[1,256]{1,0:T(1,128)} %bitcast.14, s32[1,256]{1,0:T(1,128)} %row_in.3), custom_call_target="tpu_custom_call" | custom-call | tf_op jit(solution)/shard_map/pallas_call | solution.py:234
  2.4 10.6 %all-to-all-start = ((s32[32,1,128]{2,1,0:T(1,128)}), s32[32,1,128]{2,1,0:T(1,128)S(1)}, u32[]{:S(2)}, u32[]{:S(2)}) async-start(s32[32,1,128]{2,1,0:T(1,128)} %shard_map.103), calls=%async_computation | async-start | bytes 32768 | tf_op jit(solution)/shard_map/all_to_all | solution.py:250
  12.9 1.0 %slice.3 = bf16[256,768]{1,0:T(8,128)(2,1)S(1)} slice(bf16[256,1536]{1,0:T(8,128)(2,1)} %history_in.1), slice={[0:256], [0:768]} | slice | bytes 786432 | tf_op jit(solution)/shard_map/slice | solution.py:304
  14.0 1.0 %pad_maximum_fusion.table_ref = bf16[384,768]{1,0:T(8,128)(2,1)S(1)} fusion(bf16[256,768]{1,0:T(8,128)(2,1)S(1)} %slice.3, bf16[128,768]{1,0:T(8,128)(2,1)} %bitcast.9), kind=kLoop, calls=%fused_computation | loop fusion | flops 1179648 | bytes 1179648 | tf_op jit(solution)/shard_map/concatenate | solution.py:304
  14.9 0.0 copy-start
  14.9 0.0 copy-start.3
  14.9 0.0 copy-start.5
  15.0 2.2 %shard_map.104 = (bf16[128,512]{1,0:T(8,128)(2,1)}, bf16[128,512]{1,0:T(8,128)(2,1)}) custom-call(s32[1,2]{1,0:T(1,128)} %tile_in.3, s32[1,256]{1,0:T(1,128)} %bitcast.15, s32[1,256]{1,0:T(1,128)} %row_in.3, bf16[128,256]{1,0:T(8,128)(2,1)} %bitcast.13), custom_call_target="tpu_custom_call" | custom-call | tf_op jit(solution)/shard_map/pallas_call | solution.py:234
  17.2 0.0 copy-start.4
  17.2 0.7 shard_map.105
  17.9 18.3 %all_to_all.25.pulled_ref = bf16[32,16,768]{2,1,0:T(8,128)(2,1)S(1)} all-to-all(bf16[32,16,768]{2,1,0:T(8,128)(2,1)S(1)} %get-tuple-element.22), channel_id=1, replica_groups={{20,21,22,23,24,25,26,27,28,29,30,31,0,1,2,3,4,5,6,7,8,9,10,11,12,13,14..., dimensions={0} | all-to-all | bytes 1572864 | tf_op jit(solution)/shard_map/all_to_all | solution.py:250
  36.2 0.6 shard_map.106.pair_ref
  36.8 2.4 %all-gather = bf16[256,1536]{1,0:T(8,128)(2,1)S(1)} all-gather(bf16[128,1536]{1,0:T(8,128)(2,1)S(1)} %shard_map.106.pair_ref), channel_id=2, replica_groups={{0,1},{2,3},{4,5},{6,7},{8,9},{10,11},{12,13},{14,15},{16,17},{18,19},{..., dimensions={0}, use_global_device_ids=true | all-gather | bytes 1179648 | tf_op jit(solution)/shard_map/all_gather | solution.py:317
  39.2 0.4 shard_map.107
  39.6 0.0 copy-start.1
  39.6 16.3 %all_to_all.26.terms_ref = bf16[32,8,1152]{2,1,0:T(8,128)(2,1)S(1)} all-to-all(bf16[32,8,1152]{2,1,0:T(8,128)(2,1)S(1)} %shard_map.107), channel_id=1, replica_groups={{20,21,22,23,24,25,26,27,28,29,30,31,0,1,2,3,4,5,6,7,8,9,10,11,12,13,14..., dimensions={0} | all-to-all | bytes 1179648 | tf_op jit(solution)/shard_map/all_to_all | solution.py:250
  55.9 0.7 shard_map.109
  56.7 4.2 %all-to-all-start.3 = ((bf16[4,16,1152]{2,1,0:T(8,128)(2,1)}), bf16[4,16,1152]{2,1,0:T(8,128)(2,1)S(1)}, u32[]{:S(2)}, u32[]{:S(2)}) async-start(bf16[4,16,1152]{2,1,0:T(8,128)(2,1)} %shard_map.109), calls=%async_computation.3 | async-start | bytes 294912 | tf_op jit(solution)/shard_map/all_to_all | solution.py:250
  60.9 2.0 %shard_map.108 = (bf16[32,16,1536]{2,1,0:T(8,128)(2,1)S(1)}, bf16[128,768]{1,0:T(8,128)(2,1)S(1)}, bf16[128,768]{1,0:T(8,128)(2,1)}) custom-call(bf16[128,1536]{1,0:T(8,128)(2,1)S(1)} %shard_map.106.pair_ref, bf16[768,768]{1,0:T(8,128)(2,1)S(1)} %copy-done, bf16[128,512]{1,0:T(8,128)(2,1)S(1)} %copy-done.6, ...), custom_call_target="tpu_custom_call" | custom-call | tf_op jit(solution)/shard_map/pallas_call | solution.py:234
  62.9 1.2 %copy-done.2 = bf16[32,16,1536]{2,1,0:T(8,128)(2,1)} copy-done((bf16[32,16,1536]{2,1,0:T(8,128)(2,1)}, bf16[32,16,1536]{2,1,0:T(8,128)(2,1)S(1)}, u32[]{:S(2)}) %copy-start.2) | copy-done | bytes 1572888
  64.1 0.9 all-to-all-done.3.near_ref
  65.0 6.0 %all-to-all-start.4 = ((bf16[32,16,1536]{2,1,0:T(8,128)(2,1)}), bf16[32,16,1536]{2,1,0:T(8,128)(2,1)S(1)}, u32[]{:S(2)}, u32[]{:S(2)}) async-start(bf16[32,16,1536]{2,1,0:T(8,128)(2,1)} %copy-done.2), calls=%async_computation.4 | async-start | bytes 3145728 | tf_op jit(solution)/shard_map/all_to_all | solution.py:250
  71.0 24.3 %all-gather.1 = bf16[64,1152]{1,0:T(8,128)(2,1)S(1)} all-gather(bf16[16,1152]{1,0:T(8,128)(2,1)S(1)} %shard_map.110), channel_id=3, replica_groups={{0,128,256,384},{32,160,288,416},{64,192,320,448},{96,224,352,480},{1,1..., dimensions={0}, use_global_device_ids=true | all-gather | bytes 184320 | tf_op jit(solution)/shard_map/all_gather | solution.py:352
  95.4 1.1 %shard_map.111 = (bf16[128,768]{1,0:T(8,128)(2,1)}, f32[24,768]{1,0:T(8,128)}) custom-call(bf16[32,16,1536]{2,1,0:T(8,128)(2,1)S(1)} %all-to-all-done.4.back_ref, bf16[512,384]{1,0:T(8,128)(2,1)S(1)} %get-tuple-element.26.pick_in.pick_ref, bf16[128,512]{1,0:T(8,128)(2,1)S(1)} %copy-done.4, bf16[128,768]{1,0:T(8,128)(2,1)S(1)} %get-tuple-element.31.mixed_ref, ...), custom_call_target="tpu_custom_call" | custom-call | tf_op jit(solution)/shard_map/pallas_call | solution.py:234
  (11 shorter events, 0.0 us)
Async XLA Ops:
  2.4 14.9 %all-to-all-start = ((s32[32,1,128]{2,1,0:T(1,128)}), s32[32,1,128]{2,1,0:T(1,128)S(1)}, u32[]{:S(2)}, u32[]{:S(2)}) async-start(s32[32,1,128]{2,1,0:T(1,128)} %shard_map.103), calls=%async_computation | async-start | bytes 32768 | tf_op jit(solution)/shard_map/all_to_all | solution.py:250
  14.9 21.3 %copy-start = (bf16[768,768]{1,0:T(8,128)(2,1)S(1)}, bf16[768,768]{1,0:T(8,128)(2,1)}, u32[]{:S(2)}) copy-start(bf16[768,768]{1,0:T(8,128)(2,1)} %weight_ref.3) | copy-start | bytes 3538948
  14.9 21.3 %copy-start.3 = (bf16[1,128,768]{2,1,0:T(8,128)(2,1)S(1)}, bf16[1,128,768]{2,1,0:T(8,128)(2,1)}, u32[]{:S(2)}) copy-start(bf16[1,128,768]{2,1,0:T(8,128)(2,1)} %param.8) | copy-start | bytes 589828
  14.9 21.3 %copy-start.5 = (bf16[1,128,768]{2,1,0:T(8,128)(2,1)S(1)}, bf16[1,128,768]{2,1,0:T(8,128)(2,1)}, u32[]{:S(2)}) copy-start(bf16[1,128,768]{2,1,0:T(8,128)(2,1)} %param.15) | copy-start | bytes 589828
  17.2 19.0 %copy-start.4 = (bf16[128,512]{1,0:T(8,128)(2,1)S(1)}, bf16[128,512]{1,0:T(8,128)(2,1)}, u32[]{:S(2)}) copy-start(bf16[128,512]{1,0:T(8,128)(2,1)} %get-tuple-element.23.all_ref) | copy-start | bytes 393220
  39.6 21.3 %copy-start.1 = (bf16[256,1536]{1,0:T(8,128)(2,1)S(1)}, bf16[256,1536]{1,0:T(8,128)(2,1)}, u32[]{:S(2)}) copy-start(bf16[256,1536]{1,0:T(8,128)(2,1)} %history_in.1) | copy-start | bytes 2359300
  39.6 21.3 %copy-start.6 = (bf16[128,512]{1,0:T(8,128)(2,1)S(1)}, bf16[128,512]{1,0:T(8,128)(2,1)}, u32[]{:S(2)}) copy-start(bf16[128,512]{1,0:T(8,128)(2,1)} %get-tuple-element.25.inside_ref) | copy-start | bytes 393220
  56.7 8.3 %all-to-all-start.3 = ((bf16[4,16,1152]{2,1,0:T(8,128)(2,1)}), bf16[4,16,1152]{2,1,0:T(8,128)(2,1)S(1)}, u32[]{:S(2)}, u32[]{:S(2)}) async-start(bf16[4,16,1152]{2,1,0:T(8,128)(2,1)} %shard_map.109), calls=%async_computation.3 | async-start | bytes 294912 | tf_op jit(solution)/shard_map/all_to_all | solution.py:250
  62.9 1.2 %copy-start.2 = (bf16[32,16,1536]{2,1,0:T(8,128)(2,1)}, bf16[32,16,1536]{2,1,0:T(8,128)(2,1)S(1)}, u32[]{:S(2)}) copy-start(bf16[32,16,1536]{2,1,0:T(8,128)(2,1)S(1)} %get-tuple-element.30) | copy-start | bytes 4718596
  65.0 30.4 %all-to-all-start.4 = ((bf16[32,16,1536]{2,1,0:T(8,128)(2,1)}), bf16[32,16,1536]{2,1,0:T(8,128)(2,1)S(1)}, u32[]{:S(2)}, u32[]{:S(2)}) async-start(bf16[32,16,1536]{2,1,0:T(8,128)(2,1)} %copy-done.2), calls=%async_computation.4 | async-start | bytes 3145728 | tf_op jit(solution)/shard_map/all_to_all | solution.py:250

commit v17 on v16

--- a/solution.py
+++ b/solution.py
@@ -53,7 +53,9 @@
     return named, jnp.sum(named * rank, axis=0, keepdims=True).astype(jnp.int32)
 
 
-def request_kernel(tile_in, owner_in, row_in, ids_ref, tile_ref, owner_ref, row_ref, sems):
+def request_kernel(
+    tile_in, owner_in, row_in, ids_ref, slots_ref, tile_ref, owner_ref, row_ref, sems
+):
     copies = [
         pltpu.make_async_copy(tile_in, tile_ref, sems.at[0]),
         pltpu.make_async_copy(owner_in, owner_ref, sems.at[1]),
@@ -76,6 +78,8 @@
     ids = dot(jnp.concatenate([low, high], axis=0).astype(BF16), spot, ROWS_T)
     ids = ids[:peers] + LANES * ids[peers:]
     ids_ref[...] = ids.astype(jnp.int32).reshape(ids_ref.shape)
+    slots_ref[:1, :] = owners * CAP + place
+    slots_ref[1:, :] = rows
 
 
 def gather_kernel(ids_ref, table_ref, taken_ref, pick):
@@ -94,31 +98,26 @@
         taken_ref[start : start + part] = emb.astype(BF16).reshape(part, CAP, width)
 
 
-def coef_kernel(
-    peers, node_rows, tile_in, owner_in, row_in, edge_in, all_ref, inside_ref, tile_ref, owner_ref,
-    row_ref, edge_ref, sems
-):
+def coef_kernel(node_rows, slots_in, edge_in, all_ref, inside_ref, slots_ref, edge_ref, sems):
     copies = [
-        pltpu.make_async_copy(tile_in, tile_ref, sems.at[0]),
-        pltpu.make_async_copy(owner_in, owner_ref, sems.at[1]),
-        pltpu.make_async_copy(row_in, row_ref, sems.at[2]),
-        pltpu.make_async_copy(edge_in, edge_ref, sems.at[3]),
+        pltpu.make_async_copy(slots_in, slots_ref, sems.at[0]),
+        pltpu.make_async_copy(edge_in, edge_ref, sems.at[1]),
     ]
     for copy in copies:
         copy.start()
-    earlier = earlier_slots(owner_ref.shape[1])
+    places, slots = all_ref.shape[1], slots_ref.shape[1]
+    columns = lax.broadcasted_iota(jnp.int32, (places, slots), 0)
     for copy in copies:
         copy.wait()
-    first = tile_ref[:, :1]
-    owners = in_edge_order(first, to_blocks(owner_ref[...], peers))
-    rows = in_edge_order(first, row_ref[...])
-    _, place = slot_places(owners, peers, earlier)
-    target = owners * CAP + place
-    at = lax.broadcasted_iota(jnp.int32, (peers * CAP, target.shape[1]), 0) == target
-    moved = jnp.where(at, 1.0, 0.0)
-    all_ref[...] = dot(edge_ref[...], moved.astype(BF16), ROWS_T).astype(BF16)
-    kept = jnp.where(rows < node_rows, moved, 0.0).astype(BF16)
-    inside_ref[...] = dot(edge_ref[...], kept, ROWS_T).astype(BF16)
+    moved = jnp.where(columns == slots_ref[:1, :], 1.0, 0.0).astype(BF16)
+    kept = jnp.where(slots_ref[1:, :] < node_rows, 1.0, 0.0)
+    kept = jnp.broadcast_to(kept, (16, slots)).astype(BF16)
+    edge = edge_ref[...]
+    rows = edge.shape[0]
+    both = dot(jnp.concatenate([edge, kept], axis=0), moved, ROWS_T)
+    coef = both[:rows]
+    all_ref[...] = coef.astype(BF16)
+    inside_ref[...] = (coef * both[rows : rows + 1]).astype(BF16)
 
 
 def forward_kernel(
@@ -262,9 +261,9 @@
     share = width // peers
     shape = jax.ShapeDtypeStruct
     owners = nbr_owner.reshape(1, slots)
-    ids = call(
+    ids, placed = call(
         request_kernel,
-        shape((peers, 1, LANES), jnp.int32),
+        [shape((peers, 1, LANES), jnp.int32), shape((2, slots), jnp.int32)],
         tile_map,
         owners,
         nbr_row,
@@ -279,20 +278,16 @@
     )
     received = swap(ids)
     coef, coef_inside = call(
-        functools.partial(coef_kernel, peers, node_rows),
+        functools.partial(coef_kernel, node_rows),
         [shape((node_rows, peers * CAP), BF16)] * 2,
-        tile_map,
-        owners,
-        nbr_row,
+        placed,
         edge_coef[0],
-        hbm=(0, 1, 2, 3),
+        hbm=(0, 1),
         vmem=60,
         scratch=(
-            pltpu.VMEM(tile_map.shape, jnp.int32),
-            pltpu.VMEM(owners.shape, jnp.int32),
-            pltpu.VMEM(nbr_row.shape, jnp.int32),
+            pltpu.VMEM((2, slots), jnp.int32),
             pltpu.VMEM(edge_coef.shape[1:], BF16),
-            pltpu.SemaphoreType.DMA((4,)),
+            pltpu.SemaphoreType.DMA((2,)),
         ),
     )
     table = node_rows + table_rows

time: 97.7 us -> 97.3 us (level)
  transfers between devices with their start and end apart: 3 -> 3, of which waited for: 1 -> 2; matrix products, arithmetic and copies ran while one was open for 2% -> 2% of each run, Pallas kernels for 4% -> 4%
where the time goes in v17:
time: 97.3 us; the launch traced here: 96.1 us
  blocking collectives  61 us (63%)
  starting transfers between devices  20.7 us (21%)
  Pallas kernels  9.12 us (9%)
  local copies, waits for them, and re-layouts  2.23 us (2%)
  waiting for transfers between devices  1.27 us (1%)
    all_to_all x2, blocking collectives, swap(): lax.all_to_all(values, axis, split_axis=0, concat_axis=0, tiled=True, axi...  34.3 us
    all_gather x1, blocking collectives, body(): term = lax.all_gather(term, 'batch', axis=0, axis_index_groups=far)  24.4 us
    all_to_all x3, starting transfers between devices, swap(): lax.all_to_all(values, axis, split_axis=0, concat_axis=0, tiled=True, axi...  20.7 us
    pallas_call x9, Pallas kernels, call(): pl.pallas_call(kernel, out_shape=out_shape, in_specs=[pl.BlockSpec(memory...  9.12 us
    all_gather x1, blocking collectives, body(): pairs = lax.all_gather(pair, 'hist', axis=0, axis_index_groups=chips)  2.38 us
  transfers between devices with their start and end apart: 3, of which 2 were waited for; matrix products, arithmetic and copies ran while one was open for 2% of the time, Pallas kernels for 4%

profile of v17, /device:TPU:6, one launch (start us, length us, event | category | flops | bytes accessed | tf_op | source)
XLA Modules:
  0.0 96.1 jit_solution(4261581992343232095)
XLA Ops:
  0.6 1.7 %shard_map.103 = (s32[32,1,128]{2,1,0:T(1,128)}, s32[2,256]{1,0:T(2,128)}) custom-call(s32[1,2]{1,0:T(1,128)} %tile_in.1, s32[1,256]{1,0:T(1,128)} %bitcast.14, s32[1,256]{1,0:T(1,128)} %row_in.1), custom_call_target="tpu_custom_call" | custom-call | tf_op jit(solution)/shard_map/pallas_call | solution.py:233
  2.4 10.6 %all-to-all-start = ((s32[32,1,128]{2,1,0:T(1,128)}), s32[32,1,128]{2,1,0:T(1,128)S(1)}, u32[]{:S(2)}, u32[]{:S(2)}) async-start(s32[32,1,128]{2,1,0:T(1,128)} %get-tuple-element.21), calls=%async_computation | async-start | bytes 32768 | tf_op jit(solution)/shard_map/all_to_all | solution.py:249
  12.9 1.0 %slice.3 = bf16[256,768]{1,0:T(8,128)(2,1)S(1)} slice(bf16[256,1536]{1,0:T(8,128)(2,1)} %history_in.1), slice={[0:256], [0:768]} | slice | bytes 786432 | tf_op jit(solution)/shard_map/slice | solution.py:299
  14.0 1.0 %pad_maximum_fusion.table_ref = bf16[384,768]{1,0:T(8,128)(2,1)S(1)} fusion(bf16[256,768]{1,0:T(8,128)(2,1)S(1)} %slice.3, bf16[128,768]{1,0:T(8,128)(2,1)} %bitcast.9), kind=kLoop, calls=%fused_computation | loop fusion | flops 1179648 | bytes 1179648 | tf_op jit(solution)/shard_map/concatenate | solution.py:299
  14.9 0.0 copy-start
  14.9 0.0 copy-start.3
  15.0 0.0 copy-start.5
  15.0 1.9 %shard_map.104 = (bf16[128,512]{1,0:T(8,128)(2,1)}, bf16[128,512]{1,0:T(8,128)(2,1)}) custom-call(s32[2,256]{1,0:T(2,128)} %get-tuple-element.22.slots_in, bf16[128,256]{1,0:T(8,128)(2,1)} %bitcast.13), custom_call_target="tpu_custom_call" | custom-call | tf_op jit(solution)/shard_map/pallas_call | solution.py:233
  16.9 0.3 all-to-all-done.ids_ref
  17.2 0.7 shard_map.105
  17.9 18.0 %all_to_all.25.pulled_ref = bf16[32,16,768]{2,1,0:T(8,128)(2,1)S(1)} all-to-all(bf16[32,16,768]{2,1,0:T(8,128)(2,1)S(1)} %get-tuple-element.26), channel_id=1, replica_groups={{20,21,22,23,24,25,26,27,28,29,30,31,0,1,2,3,4,5,6,7,8,9,10,11,12,13,14..., dimensions={0} | all-to-all | bytes 1572864 | tf_op jit(solution)/shard_map/all_to_all | solution.py:249
  35.9 0.6 shard_map.106.pair_ref
  36.5 2.4 %all-gather = bf16[256,1536]{1,0:T(8,128)(2,1)S(1)} all-gather(bf16[128,1536]{1,0:T(8,128)(2,1)S(1)} %shard_map.106.pair_ref), channel_id=2, replica_groups={{0,1},{2,3},{4,5},{6,7},{8,9},{10,11},{12,13},{14,15},{16,17},{18,19},{..., dimensions={0}, use_global_device_ids=true | all-gather | bytes 1179648 | tf_op jit(solution)/shard_map/all_gather | solution.py:312
  38.9 0.4 shard_map.107
  39.3 0.0 copy-start.6
  39.3 16.3 %all_to_all.26.terms_ref = bf16[32,8,1152]{2,1,0:T(8,128)(2,1)S(1)} all-to-all(bf16[32,8,1152]{2,1,0:T(8,128)(2,1)S(1)} %shard_map.107), channel_id=1, replica_groups={{20,21,22,23,24,25,26,27,28,29,30,31,0,1,2,3,4,5,6,7,8,9,10,11,12,13,14..., dimensions={0} | all-to-all | bytes 1179648 | tf_op jit(solution)/shard_map/all_to_all | solution.py:249
  55.6 0.7 shard_map.109
  56.3 4.2 %all-to-all-start.3 = ((bf16[4,16,1152]{2,1,0:T(8,128)(2,1)}), bf16[4,16,1152]{2,1,0:T(8,128)(2,1)S(1)}, u32[]{:S(2)}, u32[]{:S(2)}) async-start(bf16[4,16,1152]{2,1,0:T(8,128)(2,1)} %shard_map.109), calls=%async_computation.3 | async-start | bytes 294912 | tf_op jit(solution)/shard_map/all_to_all | solution.py:249
  60.5 2.0 %shard_map.108 = (bf16[32,16,1536]{2,1,0:T(8,128)(2,1)S(1)}, bf16[128,768]{1,0:T(8,128)(2,1)S(1)}, bf16[128,768]{1,0:T(8,128)(2,1)}) custom-call(bf16[128,1536]{1,0:T(8,128)(2,1)S(1)} %shard_map.106.pair_ref, bf16[768,768]{1,0:T(8,128)(2,1)S(1)} %copy-done, bf16[128,512]{1,0:T(8,128)(2,1)S(1)} %copy-done.6, ...), custom_call_target="tpu_custom_call" | custom-call | tf_op jit(solution)/shard_map/pallas_call | solution.py:233
  62.6 1.2 %copy-done.2 = bf16[32,16,1536]{2,1,0:T(8,128)(2,1)} copy-done((bf16[32,16,1536]{2,1,0:T(8,128)(2,1)}, bf16[32,16,1536]{2,1,0:T(8,128)(2,1)S(1)}, u32[]{:S(2)}) %copy-start.2) | copy-done | bytes 1572888
  63.7 0.9 all-to-all-done.3.near_ref
  64.7 6.0 %all-to-all-start.4 = ((bf16[32,16,1536]{2,1,0:T(8,128)(2,1)}), bf16[32,16,1536]{2,1,0:T(8,128)(2,1)S(1)}, u32[]{:S(2)}, u32[]{:S(2)}) async-start(bf16[32,16,1536]{2,1,0:T(8,128)(2,1)} %copy-done.2), calls=%async_computation.4 | async-start | bytes 3145728 | tf_op jit(solution)/shard_map/all_to_all | solution.py:249
  70.7 24.4 %all-gather.1 = bf16[64,1152]{1,0:T(8,128)(2,1)S(1)} all-gather(bf16[16,1152]{1,0:T(8,128)(2,1)S(1)} %shard_map.110), channel_id=3, replica_groups={{0,128,256,384},{32,160,288,416},{64,192,320,448},{96,224,352,480},{1,1..., dimensions={0}, use_global_device_ids=true | all-gather | bytes 184320 | tf_op jit(solution)/shard_map/all_gather | solution.py:347
  95.0 1.1 %shard_map.111 = (bf16[128,768]{1,0:T(8,128)(2,1)}, f32[24,768]{1,0:T(8,128)}) custom-call(bf16[32,16,1536]{2,1,0:T(8,128)(2,1)S(1)} %all-to-all-done.4.back_ref, bf16[512,384]{1,0:T(8,128)(2,1)S(1)} %get-tuple-element.30.pick_in.pick_ref, bf16[128,512]{1,0:T(8,128)(2,1)S(1)} %copy-done.4, bf16[128,768]{1,0:T(8,128)(2,1)S(1)} %get-tuple-element.35.mixed_ref, ...), custom_call_target="tpu_custom_call" | custom-call | tf_op jit(solution)/shard_map/pallas_call | solution.py:233
  (11 shorter events, 0.0 us)
Async XLA Ops:
  2.4 14.9 %all-to-all-start = ((s32[32,1,128]{2,1,0:T(1,128)}), s32[32,1,128]{2,1,0:T(1,128)S(1)}, u32[]{:S(2)}, u32[]{:S(2)}) async-start(s32[32,1,128]{2,1,0:T(1,128)} %get-tuple-element.21), calls=%async_computation | async-start | bytes 32768 | tf_op jit(solution)/shard_map/all_to_all | solution.py:249
  14.9 20.9 %copy-start = (bf16[768,768]{1,0:T(8,128)(2,1)S(1)}, bf16[768,768]{1,0:T(8,128)(2,1)}, u32[]{:S(2)}) copy-start(bf16[768,768]{1,0:T(8,128)(2,1)} %weight_ref.3) | copy-start | bytes 3538948
  14.9 20.9 %copy-start.3 = (bf16[1,128,768]{2,1,0:T(8,128)(2,1)S(1)}, bf16[1,128,768]{2,1,0:T(8,128)(2,1)}, u32[]{:S(2)}) copy-start(bf16[1,128,768]{2,1,0:T(8,128)(2,1)} %param.8) | copy-start | bytes 589828
  15.0 20.9 %copy-start.5 = (bf16[1,128,768]{2,1,0:T(8,128)(2,1)S(1)}, bf16[1,128,768]{2,1,0:T(8,128)(2,1)}, u32[]{:S(2)}) copy-start(bf16[1,128,768]{2,1,0:T(8,128)(2,1)} %param.15) | copy-start | bytes 589828
  16.9 19.0 %copy-start.4 = (bf16[128,512]{1,0:T(8,128)(2,1)S(1)}, bf16[128,512]{1,0:T(8,128)(2,1)}, u32[]{:S(2)}) copy-start(bf16[128,512]{1,0:T(8,128)(2,1)} %get-tuple-element.27.all_ref) | copy-start | bytes 393220
  39.3 21.3 %copy-start.1 = (bf16[256,1536]{1,0:T(8,128)(2,1)S(1)}, bf16[256,1536]{1,0:T(8,128)(2,1)}, u32[]{:S(2)}) copy-start(bf16[256,1536]{1,0:T(8,128)(2,1)} %history_in.1) | copy-start | bytes 2359300
  39.3 21.3 %copy-start.6 = (bf16[128,512]{1,0:T(8,128)(2,1)S(1)}, bf16[128,512]{1,0:T(8,128)(2,1)}, u32[]{:S(2)}) copy-start(bf16[128,512]{1,0:T(8,128)(2,1)} %get-tuple-element.29.inside_ref) | copy-start | bytes 393220
  56.3 8.3 %all-to-all-start.3 = ((bf16[4,16,1152]{2,1,0:T(8,128)(2,1)}), bf16[4,16,1152]{2,1,0:T(8,128)(2,1)S(1)}, u32[]{:S(2)}, u32[]{:S(2)}) async-start(bf16[4,16,1152]{2,1,0:T(8,128)(2,1)} %shard_map.109), calls=%async_computation.3 | async-start | bytes 294912 | tf_op jit(solution)/shard_map/all_to_all | solution.py:249
  62.5 1.2 %copy-start.2 = (bf16[32,16,1536]{2,1,0:T(8,128)(2,1)}, bf16[32,16,1536]{2,1,0:T(8,128)(2,1)S(1)}, u32[]{:S(2)}) copy-start(bf16[32,16,1536]{2,1,0:T(8,128)(2,1)S(1)} %get-tuple-element.34) | copy-start | bytes 4718596
  64.7 30.4 %all-to-all-start.4 = ((bf16[32,16,1536]{2,1,0:T(8,128)(2,1)}), bf16[32,16,1536]{2,1,0:T(8,128)(2,1)S(1)}, u32[]{:S(2)}, u32[]{:S(2)}) async-start(bf16[32,16,1536]{2,1,0:T(8,128)(2,1)} %copy-done.2), calls=%async_computation.4 | async-start | bytes 3145728 | tf_op jit(solution)/shard_map/all_to_all | solution.py:249

commit v18 on v17

--- a/solution.py
+++ b/solution.py
@@ -24,7 +24,7 @@
 
 
 def lead_of(peers):
-    return 5 * peers // 8
+    return 5 * peers // 8 + 1
 
 
 def to_blocks(owners, peers):
@@ -188,8 +188,9 @@
 def weight_kernel(terms_ref, sum_ref):
     peers, step = terms_ref.shape[:2]
     for core in range(2):
-        total = terms_ref[core].astype(F32)
-        for peer in range(core + 2, peers, 2):
+        first = (core + lead_of(peers)) % 2
+        total = terms_ref[first].astype(F32)
+        for peer in range(first + 2, peers, 2):
             total = total + terms_ref[peer].astype(F32)
         total = total.astype(BF16)
         for plane in range(sum_ref.shape[0]):

time: 97.3 us -> 96.1 us (0.988)
  no operation moved by 1% of the time
where the time goes in v18:
time: 96.1 us; the launch traced here: 94.7 us
  blocking collectives  60.2 us (63%)
  starting transfers between devices  20.1 us (21%)
  Pallas kernels  9.13 us (10%)
  local copies, waits for them, and re-layouts  2.23 us (2%)
  waiting for transfers between devices  1.27 us (1%)
  other arithmetic  0.97 us (1%)
    all_to_all x2, blocking collectives, swap(): lax.all_to_all(values, axis, split_axis=0, concat_axis=0, tiled=True, axi...  33.8 us
    all_gather x1, blocking collectives, body(): term = lax.all_gather(term, 'batch', axis=0, axis_index_groups=far)  24.1 us
    all_to_all x3, starting transfers between devices, swap(): lax.all_to_all(values, axis, split_axis=0, concat_axis=0, tiled=True, axi...  20.1 us
    pallas_call x9, Pallas kernels, call(): pl.pallas_call(kernel, out_shape=out_shape, in_specs=[pl.BlockSpec(memory...  9.13 us
    all_gather x1, blocking collectives, body(): pairs = lax.all_gather(pair, 'hist', axis=0, axis_index_groups=chips)  2.38 us
  transfers between devices with their start and end apart: 3, of which 2 were waited for; matrix products, arithmetic and copies ran while one was open for 2% of the time, Pallas kernels for 4%

profile of v18, /device:TPU:6, one launch (start us, length us, event | category | flops | bytes accessed | tf_op | source)
XLA Modules:
  0.0 94.7 jit_solution(13207597912543502255)
XLA Ops:
  0.6 1.7 %shard_map.103 = (s32[32,1,128]{2,1,0:T(1,128)}, s32[2,256]{1,0:T(2,128)}) custom-call(s32[1,2]{1,0:T(1,128)} %tile_in.1, s32[1,256]{1,0:T(1,128)} %bitcast.14, s32[1,256]{1,0:T(1,128)} %row_in.1), custom_call_target="tpu_custom_call" | custom-call | tf_op jit(solution)/shard_map/pallas_call | solution.py:234
  2.4 10.3 %all-to-all-start = ((s32[32,1,128]{2,1,0:T(1,128)}), s32[32,1,128]{2,1,0:T(1,128)S(1)}, u32[]{:S(2)}, u32[]{:S(2)}) async-start(s32[32,1,128]{2,1,0:T(1,128)} %get-tuple-element.21), calls=%async_computation | async-start | bytes 32768 | tf_op jit(solution)/shard_map/all_to_all | solution.py:250
  12.6 1.0 %slice.3 = bf16[256,768]{1,0:T(8,128)(2,1)S(1)} slice(bf16[256,1536]{1,0:T(8,128)(2,1)} %history_in.1), slice={[0:256], [0:768]} | slice | bytes 786432 | tf_op jit(solution)/shard_map/slice | solution.py:300
  13.7 1.0 %pad_maximum_fusion.table_ref = bf16[384,768]{1,0:T(8,128)(2,1)S(1)} fusion(bf16[256,768]{1,0:T(8,128)(2,1)S(1)} %slice.3, bf16[128,768]{1,0:T(8,128)(2,1)} %bitcast.9), kind=kLoop, calls=%fused_computation | loop fusion | flops 1179648 | bytes 1179648 | tf_op jit(solution)/shard_map/concatenate | solution.py:300
  14.6 0.0 copy-start
  14.7 0.0 copy-start.3
  14.7 0.0 copy-start.5
  14.7 1.9 %shard_map.104 = (bf16[128,512]{1,0:T(8,128)(2,1)}, bf16[128,512]{1,0:T(8,128)(2,1)}) custom-call(s32[2,256]{1,0:T(2,128)} %get-tuple-element.22.slots_in, bf16[128,256]{1,0:T(8,128)(2,1)} %bitcast.13), custom_call_target="tpu_custom_call" | custom-call | tf_op jit(solution)/shard_map/pallas_call | solution.py:234
  16.6 0.3 all-to-all-done.ids_ref
  16.9 0.7 shard_map.105
  17.6 17.7 %all_to_all.25.pulled_ref = bf16[32,16,768]{2,1,0:T(8,128)(2,1)S(1)} all-to-all(bf16[32,16,768]{2,1,0:T(8,128)(2,1)S(1)} %get-tuple-element.26), channel_id=1, replica_groups={{21,22,23,24,25,26,27,28,29,30,31,0,1,2,3,4,5,6,7,8,9,10,11,12,13,14,15..., dimensions={0} | all-to-all | bytes 1572864 | tf_op jit(solution)/shard_map/all_to_all | solution.py:250
  35.3 0.6 shard_map.106.pair_ref
  35.9 2.4 %all-gather = bf16[256,1536]{1,0:T(8,128)(2,1)S(1)} all-gather(bf16[128,1536]{1,0:T(8,128)(2,1)S(1)} %shard_map.106.pair_ref), channel_id=2, replica_groups={{0,1},{2,3},{4,5},{6,7},{8,9},{10,11},{12,13},{14,15},{16,17},{18,19},{..., dimensions={0}, use_global_device_ids=true | all-gather | bytes 1179648 | tf_op jit(solution)/shard_map/all_gather | solution.py:313
  38.3 0.4 shard_map.107
  38.7 0.0 copy-start.1
  38.7 16.1 %all_to_all.26.terms_ref = bf16[32,8,1152]{2,1,0:T(8,128)(2,1)S(1)} all-to-all(bf16[32,8,1152]{2,1,0:T(8,128)(2,1)S(1)} %shard_map.107), channel_id=1, replica_groups={{21,22,23,24,25,26,27,28,29,30,31,0,1,2,3,4,5,6,7,8,9,10,11,12,13,14,15..., dimensions={0} | all-to-all | bytes 1179648 | tf_op jit(solution)/shard_map/all_to_all | solution.py:250
  54.8 0.7 shard_map.109
  55.6 4.2 %all-to-all-start.3 = ((bf16[4,16,1152]{2,1,0:T(8,128)(2,1)}), bf16[4,16,1152]{2,1,0:T(8,128)(2,1)S(1)}, u32[]{:S(2)}, u32[]{:S(2)}) async-start(bf16[4,16,1152]{2,1,0:T(8,128)(2,1)} %shard_map.109), calls=%async_computation.3 | async-start | bytes 294912 | tf_op jit(solution)/shard_map/all_to_all | solution.py:250
  59.8 2.0 %shard_map.108 = (bf16[32,16,1536]{2,1,0:T(8,128)(2,1)S(1)}, bf16[128,768]{1,0:T(8,128)(2,1)S(1)}, bf16[128,768]{1,0:T(8,128)(2,1)}) custom-call(bf16[128,1536]{1,0:T(8,128)(2,1)S(1)} %shard_map.106.pair_ref, bf16[768,768]{1,0:T(8,128)(2,1)S(1)} %copy-done, bf16[128,512]{1,0:T(8,128)(2,1)S(1)} %copy-done.6, ...), custom_call_target="tpu_custom_call" | custom-call | tf_op jit(solution)/shard_map/pallas_call | solution.py:234
  61.8 1.2 %copy-done.2 = bf16[32,16,1536]{2,1,0:T(8,128)(2,1)} copy-done((bf16[32,16,1536]{2,1,0:T(8,128)(2,1)}, bf16[32,16,1536]{2,1,0:T(8,128)(2,1)S(1)}, u32[]{:S(2)}) %copy-start.2) | copy-done | bytes 1572888
  62.9 0.9 all-to-all-done.3.near_ref
  63.9 5.7 %all-to-all-start.4 = ((bf16[32,16,1536]{2,1,0:T(8,128)(2,1)}), bf16[32,16,1536]{2,1,0:T(8,128)(2,1)S(1)}, u32[]{:S(2)}, u32[]{:S(2)}) async-start(bf16[32,16,1536]{2,1,0:T(8,128)(2,1)} %copy-done.2), calls=%async_computation.4 | async-start | bytes 3145728 | tf_op jit(solution)/shard_map/all_to_all | solution.py:250
  69.6 24.1 %all-gather.1 = bf16[64,1152]{1,0:T(8,128)(2,1)S(1)} all-gather(bf16[16,1152]{1,0:T(8,128)(2,1)S(1)} %shard_map.110), channel_id=3, replica_groups={{0,128,256,384},{32,160,288,416},{64,192,320,448},{96,224,352,480},{1,1..., dimensions={0}, use_global_device_ids=true | all-gather | bytes 184320 | tf_op jit(solution)/shard_map/all_gather | solution.py:348
  93.6 1.1 %shard_map.111 = (bf16[128,768]{1,0:T(8,128)(2,1)}, f32[24,768]{1,0:T(8,128)}) custom-call(bf16[32,16,1536]{2,1,0:T(8,128)(2,1)S(1)} %all-to-all-done.4.back_ref, bf16[512,384]{1,0:T(8,128)(2,1)S(1)} %get-tuple-element.30.pick_in.pick_ref, bf16[128,512]{1,0:T(8,128)(2,1)S(1)} %copy-done.4, bf16[128,768]{1,0:T(8,128)(2,1)S(1)} %get-tuple-element.35.mixed_ref, ...), custom_call_target="tpu_custom_call" | custom-call | tf_op jit(solution)/shard_map/pallas_call | solution.py:234
  (11 shorter events, 0.0 us)
Async XLA Ops:
  2.4 14.6 %all-to-all-start = ((s32[32,1,128]{2,1,0:T(1,128)}), s32[32,1,128]{2,1,0:T(1,128)S(1)}, u32[]{:S(2)}, u32[]{:S(2)}) async-start(s32[32,1,128]{2,1,0:T(1,128)} %get-tuple-element.21), calls=%async_computation | async-start | bytes 32768 | tf_op jit(solution)/shard_map/all_to_all | solution.py:250
  14.6 20.7 %copy-start = (bf16[768,768]{1,0:T(8,128)(2,1)S(1)}, bf16[768,768]{1,0:T(8,128)(2,1)}, u32[]{:S(2)}) copy-start(bf16[768,768]{1,0:T(8,128)(2,1)} %weight_ref.3) | copy-start | bytes 3538948
  14.7 20.7 %copy-start.3 = (bf16[1,128,768]{2,1,0:T(8,128)(2,1)S(1)}, bf16[1,128,768]{2,1,0:T(8,128)(2,1)}, u32[]{:S(2)}) copy-start(bf16[1,128,768]{2,1,0:T(8,128)(2,1)} %param.8) | copy-start | bytes 589828
  14.7 20.7 %copy-start.5 = (bf16[1,128,768]{2,1,0:T(8,128)(2,1)S(1)}, bf16[1,128,768]{2,1,0:T(8,128)(2,1)}, u32[]{:S(2)}) copy-start(bf16[1,128,768]{2,1,0:T(8,128)(2,1)} %param.15) | copy-start | bytes 589828
  16.6 18.7 %copy-start.4 = (bf16[128,512]{1,0:T(8,128)(2,1)S(1)}, bf16[128,512]{1,0:T(8,128)(2,1)}, u32[]{:S(2)}) copy-start(bf16[128,512]{1,0:T(8,128)(2,1)} %get-tuple-element.27.all_ref) | copy-start | bytes 393220
  38.7 21.0 %copy-start.1 = (bf16[256,1536]{1,0:T(8,128)(2,1)S(1)}, bf16[256,1536]{1,0:T(8,128)(2,1)}, u32[]{:S(2)}) copy-start(bf16[256,1536]{1,0:T(8,128)(2,1)} %history_in.1) | copy-start | bytes 2359300
  38.7 21.0 %copy-start.6 = (bf16[128,512]{1,0:T(8,128)(2,1)S(1)}, bf16[128,512]{1,0:T(8,128)(2,1)}, u32[]{:S(2)}) copy-start(bf16[128,512]{1,0:T(8,128)(2,1)} %get-tuple-element.29.inside_ref) | copy-start | bytes 393220
  55.6 8.3 %all-to-all-start.3 = ((bf16[4,16,1152]{2,1,0:T(8,128)(2,1)}), bf16[4,16,1152]{2,1,0:T(8,128)(2,1)S(1)}, u32[]{:S(2)}, u32[]{:S(2)}) async-start(bf16[4,16,1152]{2,1,0:T(8,128)(2,1)} %shard_map.109), calls=%async_computation.3 | async-start | bytes 294912 | tf_op jit(solution)/shard_map/all_to_all | solution.py:250
  61.8 1.2 %copy-start.2 = (bf16[32,16,1536]{2,1,0:T(8,128)(2,1)}, bf16[32,16,1536]{2,1,0:T(8,128)(2,1)S(1)}, u32[]{:S(2)}) copy-start(bf16[32,16,1536]{2,1,0:T(8,128)(2,1)S(1)} %get-tuple-element.34) | copy-start | bytes 4718596
  63.9 29.8 %all-to-all-start.4 = ((bf16[32,16,1536]{2,1,0:T(8,128)(2,1)}), bf16[32,16,1536]{2,1,0:T(8,128)(2,1)S(1)}, u32[]{:S(2)}, u32[]{:S(2)}) async-start(bf16[32,16,1536]{2,1,0:T(8,128)(2,1)} %copy-done.2), calls=%async_computation.4 | async-start | bytes 3145728 | tf_op jit(solution)/shard_map/all_to_all | solution.py:250

commit v19 on v18

--- a/solution.py
+++ b/solution.py
@@ -309,7 +309,7 @@
         weight,
         grad_out[0],
     )
-    chips = [[i, i + 1] for i in range(0, peers, 2)]
+    chips = [[i + 1, i] for i in range(0, peers, 2)]
     pairs = lax.all_gather(pair, "hist", axis=0, axis_index_groups=chips)
     terms = call(
         functools.partial(term_kernel, peers, width),

time: 96.1 us -> 96.1 us (level)
  no operation moved by 1% of the time
where the time goes in v19:
time: 96.1 us; the launch traced here: 94.7 us
  blocking collectives  60.2 us (63%)
  starting transfers between devices  20.1 us (21%)
  Pallas kernels  9.13 us (10%)
  local copies, waits for them, and re-layouts  2.23 us (2%)
  waiting for transfers between devices  1.27 us (1%)
  other arithmetic  0.97 us (1%)
    all_to_all x2, blocking collectives, swap(): lax.all_to_all(values, axis, split_axis=0, concat_axis=0, tiled=True, axi...  33.8 us
    all_gather x1, blocking collectives, body(): term = lax.all_gather(term, 'batch', axis=0, axis_index_groups=far)  24.1 us
    all_to_all x3, starting transfers between devices, swap(): lax.all_to_all(values, axis, split_axis=0, concat_axis=0, tiled=True, axi...  20.1 us
    pallas_call x9, Pallas kernels, call(): pl.pallas_call(kernel, out_shape=out_shape, in_specs=[pl.BlockSpec(memory...  9.13 us
    all_gather x1, blocking collectives, body(): pairs = lax.all_gather(pair, 'hist', axis=0, axis_index_groups=chips)  2.38 us
  transfers between devices with their start and end apart: 3, of which 2 were waited for; matrix products, arithmetic and copies ran while one was open for 2% of the time, Pallas kernels for 4%

profile of v19, /device:TPU:6, one launch (start us, length us, event | category | flops | bytes accessed | tf_op | source)
XLA Modules:
  0.0 94.7 jit_solution(4742974780541044260)
XLA Ops:
  0.6 1.7 %shard_map.103 = (s32[32,1,128]{2,1,0:T(1,128)}, s32[2,256]{1,0:T(2,128)}) custom-call(s32[1,2]{1,0:T(1,128)} %tile_in.1, s32[1,256]{1,0:T(1,128)} %bitcast.14, s32[1,256]{1,0:T(1,128)} %row_in.1), custom_call_target="tpu_custom_call" | custom-call | tf_op jit(solution)/shard_map/pallas_call | solution.py:234
  2.4 10.3 %all-to-all-start = ((s32[32,1,128]{2,1,0:T(1,128)}), s32[32,1,128]{2,1,0:T(1,128)S(1)}, u32[]{:S(2)}, u32[]{:S(2)}) async-start(s32[32,1,128]{2,1,0:T(1,128)} %get-tuple-element.21), calls=%async_computation | async-start | bytes 32768 | tf_op jit(solution)/shard_map/all_to_all | solution.py:250
  12.6 1.0 %slice.3 = bf16[256,768]{1,0:T(8,128)(2,1)S(1)} slice(bf16[256,1536]{1,0:T(8,128)(2,1)} %history_in.1), slice={[0:256], [0:768]} | slice | bytes 786432 | tf_op jit(solution)/shard_map/slice | solution.py:300
  13.7 1.0 %pad_maximum_fusion.table_ref = bf16[384,768]{1,0:T(8,128)(2,1)S(1)} fusion(bf16[256,768]{1,0:T(8,128)(2,1)S(1)} %slice.3, bf16[128,768]{1,0:T(8,128)(2,1)} %bitcast.9), kind=kLoop, calls=%fused_computation | loop fusion | flops 1179648 | bytes 1179648 | tf_op jit(solution)/shard_map/concatenate | solution.py:300
  14.6 0.0 copy-start
  14.7 0.0 copy-start.3
  14.7 0.0 copy-start.5
  14.7 1.9 %shard_map.104 = (bf16[128,512]{1,0:T(8,128)(2,1)}, bf16[128,512]{1,0:T(8,128)(2,1)}) custom-call(s32[2,256]{1,0:T(2,128)} %get-tuple-element.22.slots_in, bf16[128,256]{1,0:T(8,128)(2,1)} %bitcast.13), custom_call_target="tpu_custom_call" | custom-call | tf_op jit(solution)/shard_map/pallas_call | solution.py:234
  16.6 0.3 all-to-all-done.ids_ref
  16.9 0.7 shard_map.105
  17.6 17.7 %all_to_all.25.pulled_ref = bf16[32,16,768]{2,1,0:T(8,128)(2,1)S(1)} all-to-all(bf16[32,16,768]{2,1,0:T(8,128)(2,1)S(1)} %get-tuple-element.26), channel_id=1, replica_groups={{21,22,23,24,25,26,27,28,29,30,31,0,1,2,3,4,5,6,7,8,9,10,11,12,13,14,15..., dimensions={0} | all-to-all | bytes 1572864 | tf_op jit(solution)/shard_map/all_to_all | solution.py:250
  35.3 0.6 shard_map.106.pair_ref
  35.9 2.4 %all-gather = bf16[256,1536]{1,0:T(8,128)(2,1)S(1)} all-gather(bf16[128,1536]{1,0:T(8,128)(2,1)S(1)} %shard_map.106.pair_ref), channel_id=2, replica_groups={{1,0},{3,2},{5,4},{7,6},{9,8},{11,10},{13,12},{15,14},{17,16},{19,18},{..., dimensions={0}, use_global_device_ids=true | all-gather | bytes 1179648 | tf_op jit(solution)/shard_map/all_gather | solution.py:313
  38.3 0.4 shard_map.107
  38.7 0.0 copy-start.1
  38.7 16.1 %all_to_all.26.terms_ref = bf16[32,8,1152]{2,1,0:T(8,128)(2,1)S(1)} all-to-all(bf16[32,8,1152]{2,1,0:T(8,128)(2,1)S(1)} %shard_map.107), channel_id=1, replica_groups={{21,22,23,24,25,26,27,28,29,30,31,0,1,2,3,4,5,6,7,8,9,10,11,12,13,14,15..., dimensions={0} | all-to-all | bytes 1179648 | tf_op jit(solution)/shard_map/all_to_all | solution.py:250
  54.8 0.7 shard_map.109
  55.6 4.2 %all-to-all-start.3 = ((bf16[4,16,1152]{2,1,0:T(8,128)(2,1)}), bf16[4,16,1152]{2,1,0:T(8,128)(2,1)S(1)}, u32[]{:S(2)}, u32[]{:S(2)}) async-start(bf16[4,16,1152]{2,1,0:T(8,128)(2,1)} %shard_map.109), calls=%async_computation.3 | async-start | bytes 294912 | tf_op jit(solution)/shard_map/all_to_all | solution.py:250
  59.8 2.0 %shard_map.108 = (bf16[32,16,1536]{2,1,0:T(8,128)(2,1)S(1)}, bf16[128,768]{1,0:T(8,128)(2,1)S(1)}, bf16[128,768]{1,0:T(8,128)(2,1)}) custom-call(bf16[128,1536]{1,0:T(8,128)(2,1)S(1)} %shard_map.106.pair_ref, bf16[768,768]{1,0:T(8,128)(2,1)S(1)} %copy-done, bf16[128,512]{1,0:T(8,128)(2,1)S(1)} %copy-done.6, ...), custom_call_target="tpu_custom_call" | custom-call | tf_op jit(solution)/shard_map/pallas_call | solution.py:234
  61.8 1.2 %copy-done.2 = bf16[32,16,1536]{2,1,0:T(8,128)(2,1)} copy-done((bf16[32,16,1536]{2,1,0:T(8,128)(2,1)}, bf16[32,16,1536]{2,1,0:T(8,128)(2,1)S(1)}, u32[]{:S(2)}) %copy-start.2) | copy-done | bytes 1572888
  62.9 0.9 all-to-all-done.3.near_ref
  63.9 5.7 %all-to-all-start.4 = ((bf16[32,16,1536]{2,1,0:T(8,128)(2,1)}), bf16[32,16,1536]{2,1,0:T(8,128)(2,1)S(1)}, u32[]{:S(2)}, u32[]{:S(2)}) async-start(bf16[32,16,1536]{2,1,0:T(8,128)(2,1)} %copy-done.2), calls=%async_computation.4 | async-start | bytes 3145728 | tf_op jit(solution)/shard_map/all_to_all | solution.py:250
  69.6 24.1 %all-gather.1 = bf16[64,1152]{1,0:T(8,128)(2,1)S(1)} all-gather(bf16[16,1152]{1,0:T(8,128)(2,1)S(1)} %shard_map.110), channel_id=3, replica_groups={{0,128,256,384},{32,160,288,416},{64,192,320,448},{96,224,352,480},{1,1..., dimensions={0}, use_global_device_ids=true | all-gather | bytes 184320 | tf_op jit(solution)/shard_map/all_gather | solution.py:348
  93.6 1.1 %shard_map.111 = (bf16[128,768]{1,0:T(8,128)(2,1)}, f32[24,768]{1,0:T(8,128)}) custom-call(bf16[32,16,1536]{2,1,0:T(8,128)(2,1)S(1)} %all-to-all-done.4.back_ref, bf16[512,384]{1,0:T(8,128)(2,1)S(1)} %get-tuple-element.30.pick_in.pick_ref, bf16[128,512]{1,0:T(8,128)(2,1)S(1)} %copy-done.4, bf16[128,768]{1,0:T(8,128)(2,1)S(1)} %get-tuple-element.35.mixed_ref, ...), custom_call_target="tpu_custom_call" | custom-call | tf_op jit(solution)/shard_map/pallas_call | solution.py:234
  (11 shorter events, 0.0 us)
Async XLA Ops:
  2.4 14.6 %all-to-all-start = ((s32[32,1,128]{2,1,0:T(1,128)}), s32[32,1,128]{2,1,0:T(1,128)S(1)}, u32[]{:S(2)}, u32[]{:S(2)}) async-start(s32[32,1,128]{2,1,0:T(1,128)} %get-tuple-element.21), calls=%async_computation | async-start | bytes 32768 | tf_op jit(solution)/shard_map/all_to_all | solution.py:250
  14.6 20.7 %copy-start = (bf16[768,768]{1,0:T(8,128)(2,1)S(1)}, bf16[768,768]{1,0:T(8,128)(2,1)}, u32[]{:S(2)}) copy-start(bf16[768,768]{1,0:T(8,128)(2,1)} %weight_ref.3) | copy-start | bytes 3538948
  14.7 20.7 %copy-start.3 = (bf16[1,128,768]{2,1,0:T(8,128)(2,1)S(1)}, bf16[1,128,768]{2,1,0:T(8,128)(2,1)}, u32[]{:S(2)}) copy-start(bf16[1,128,768]{2,1,0:T(8,128)(2,1)} %param.8) | copy-start | bytes 589828
  14.7 20.7 %copy-start.5 = (bf16[1,128,768]{2,1,0:T(8,128)(2,1)S(1)}, bf16[1,128,768]{2,1,0:T(8,128)(2,1)}, u32[]{:S(2)}) copy-start(bf16[1,128,768]{2,1,0:T(8,128)(2,1)} %param.15) | copy-start | bytes 589828
  16.6 18.7 %copy-start.4 = (bf16[128,512]{1,0:T(8,128)(2,1)S(1)}, bf16[128,512]{1,0:T(8,128)(2,1)}, u32[]{:S(2)}) copy-start(bf16[128,512]{1,0:T(8,128)(2,1)} %get-tuple-element.27.all_ref) | copy-start | bytes 393220
  38.7 21.0 %copy-start.1 = (bf16[256,1536]{1,0:T(8,128)(2,1)S(1)}, bf16[256,1536]{1,0:T(8,128)(2,1)}, u32[]{:S(2)}) copy-start(bf16[256,1536]{1,0:T(8,128)(2,1)} %history_in.1) | copy-start | bytes 2359300
  38.7 21.0 %copy-start.6 = (bf16[128,512]{1,0:T(8,128)(2,1)S(1)}, bf16[128,512]{1,0:T(8,128)(2,1)}, u32[]{:S(2)}) copy-start(bf16[128,512]{1,0:T(8,128)(2,1)} %get-tuple-element.29.inside_ref) | copy-start | bytes 393220
  55.6 8.3 %all-to-all-start.3 = ((bf16[4,16,1152]{2,1,0:T(8,128)(2,1)}), bf16[4,16,1152]{2,1,0:T(8,128)(2,1)S(1)}, u32[]{:S(2)}, u32[]{:S(2)}) async-start(bf16[4,16,1152]{2,1,0:T(8,128)(2,1)} %shard_map.109), calls=%async_computation.3 | async-start | bytes 294912 | tf_op jit(solution)/shard_map/all_to_all | solution.py:250
  61.8 1.2 %copy-start.2 = (bf16[32,16,1536]{2,1,0:T(8,128)(2,1)}, bf16[32,16,1536]{2,1,0:T(8,128)(2,1)S(1)}, u32[]{:S(2)}) copy-start(bf16[32,16,1536]{2,1,0:T(8,128)(2,1)S(1)} %get-tuple-element.34) | copy-start | bytes 4718596
  63.9 29.8 %all-to-all-start.4 = ((bf16[32,16,1536]{2,1,0:T(8,128)(2,1)}), bf16[32,16,1536]{2,1,0:T(8,128)(2,1)S(1)}, u32[]{:S(2)}, u32[]{:S(2)}) async-start(bf16[32,16,1536]{2,1,0:T(8,128)(2,1)} %copy-done.2), calls=%async_computation.4 | async-start | bytes 3145728 | tf_op jit(solution)/shard_map/all_to_all | solution.py:250
